TPU v7x, 256 devices: a whole 4x4x8 slice. The times are simulated.
256 devices in a mesh: cin: 32 (over y, x, core), cout: 8 (over z).
Axes of the slice: x: 4, y: 4, z: 8, core: 2. Of those that a mesh axis runs over, the one named last changes fastest.
Arguments:
- inputs: bfloat16 [8, 1024, 2048], P('cout', 'cin'), may hold values from -6 to 6
- weight: bfloat16 [27, 1024, 1024], P(None, 'cin', 'cout'), may hold values from -0.0390625 to 0.0390625
- grad_out: bfloat16 [8, 1024, 2048], P(None, 'cout', 'cin'), may hold values from -6 to 6
Outputs:
- output: bfloat16 [8, 1024, 2048], P(None, 'cout', 'cin')
- grad_input: bfloat16 [8, 1024, 2048], P('cout', 'cin')
- grad_weight: float32 [27, 1024, 1024], P(None, 'cin', 'cout')
All inputs are finite; a program needn't handle non-finite values.
Results may differ from a plain program's by a relative error of at most 0.0016.
Values may be sent and summed in bfloat16 or wider, within the bound.
No kernel may reach another device: no remote copies, remote signals or barrier semaphores. Data moves between devices by JAX's collectives and lax.ppermute only.
A program may use at most 64 MiB of HBM per device.

v0:
```python
import math

import jax
import jax.numpy as jnp
from jax import lax
from jax.sharding import PartitionSpec as P

SX = 16
SY = 16
SZ = 8


tap_offsets = [(a, b, c) for a in (-1, 0, 1) for b in (-1, 0, 1) for c in (-1, 0, 1)]


def tap_shift(values, a, b, c):
    cell_count = values.shape[-1]
    margin = SY * SZ + SZ + 1
    widths = [(0, 0)] * (values.ndim - 1) + [(margin, margin)]
    padded = jnp.pad(values, widths)
    offset = a * SY * SZ + b * SZ + c
    shifted = lax.slice_in_dim(
        padded, margin + offset, margin + offset + cell_count, axis=values.ndim - 1
    )
    position = jnp.arange(cell_count, dtype=jnp.int32)
    coord_x = position // (SY * SZ) + a
    coord_y = position // SZ % SY + b
    coord_z = position % SZ + c
    inside = (
        (coord_x >= 0)
        & (coord_x < SX)
        & (coord_y >= 0)
        & (coord_y < SY)
        & (coord_z >= 0)
        & (coord_z < SZ)
    )
    return jnp.where(inside, shifted, jnp.zeros_like(shifted))


def stacked_columns(values, sign):
    return jnp.concatenate(
        [tap_shift(values, sign * a, sign * b, sign * c) for a, b, c in tap_offsets], axis=0
    )


def body(inputs, weight, grad_out):
    cin_local = weight.shape[1]
    cout_local = weight.shape[2]
    flat_weight = weight.reshape(27 * cin_local, cout_local)
    gathered = lax.all_gather(inputs, "cout", axis=0, tiled=True)
    grad_full = lax.all_gather(grad_out, "cin", axis=2, tiled=True)
    batch_total = gathered.shape[0]
    cell_count = gathered.shape[2]

    def one_sample(grad_sum, sample_pair):
        sample, grad_rows = sample_pair
        columns = stacked_columns(sample, 1)
        partial_value = lax.dot_general(
            flat_weight, columns, (((0,), (0,)), ((), ())), preferred_element_type=jnp.float32
        )
        products = jnp.dot(flat_weight, grad_rows, preferred_element_type=jnp.float32)
        products = products.reshape(27, cin_local, cell_count)
        input_term = jnp.zeros((cin_local, cell_count), jnp.float32)
        for index, (a, b, c) in enumerate(tap_offsets):
            input_term = input_term + tap_shift(products[index], -a, -b, -c)
        grad_sum = grad_sum + lax.dot_general(
            columns, grad_rows, (((1,), (1,)), ((), ())), preferred_element_type=jnp.float32
        )
        return (grad_sum, (partial_value, input_term))

    start_sum = jnp.zeros((27 * cin_local, cout_local), jnp.float32)
    grad_sum, (partials, input_terms) = lax.scan(one_sample, start_sum, (gathered, grad_full))
    output = lax.psum_scatter(partials, "cin", scatter_dimension=2, tiled=True).astype(jnp.bfloat16)
    grad_input = lax.psum_scatter(input_terms, "cout", scatter_dimension=0, tiled=True).astype(
        jnp.bfloat16
    )
    grad_weight = grad_sum.reshape(27, cin_local, cout_local) / math.sqrt(batch_total * cell_count)
    return (output, grad_input, grad_weight)


def solution(mesh):
    placed = (P("cout", "cin", None), P(None, "cin", "cout"), P(None, "cout", "cin"))
    return jax.shard_map(
        body,
        mesh=mesh,
        in_specs=placed,
        out_specs=(P(None, "cout", "cin"), P("cout", "cin", None), P(None, "cin", "cout")),
        check_vma=False,
    )
```

profile of v0, /device:TPU:1, one launch (start us, length us, event | category | flops | bytes accessed | tf_op | source)
XLA Modules:
  0.0 388.8 jit_solution(782218324662529904)
XLA Ops:
  7.2 1.6 copy.7
  9.7 56.8 %all-gather.5.cloned.1.call-done = bf16[8,128,2048]{1,0,2:T(8,128)(2,1)} async-done(((bf16[8,128,64]{1,0,2:T(8,128)(2,1)}), bf16[8,128,2048]{1,0,2:T(8,128)(2,1)}) %all-gather.5.cloned.1.call-update) | async-done | bytes 4194320 | tf_op jit(solution)/shard_map/all_gather | solution.py:51
  66.5 6.7 %copy.8 = bf16[8,128,2048]{2,1,0:T(8,128)(2,1)} copy(bf16[8,128,2048]{1,0,2:T(8,128)(2,1)} %all-gather.5.cloned.1.call-done) | data formatting | bytes 8388608
  73.2 27.8 %all-gather.3.cloned.1.call-done = bf16[8,32,2048]{2,1,0:T(8,128)(2,1)} async-done(((bf16[1,32,2048]{2,1,0:T(8,128)(2,1)}), bf16[8,32,2048]{2,1,0:T(8,128)(2,1)}) %all-gather.3.cloned.1.call-update) | async-done | bytes 1048592 | tf_op jit(solution)/shard_map/all_gather | solution.py:50
  100.9 132.5 %while.18 = (s32[]{:T(128)}, f32[864,128]{1,0:T(8,128)}, f32[8,128,2048]{1,2,0:T(8,128)}, f32[8,32,2048]{2,1,0:T(8,128)}, bf16[8,32,2048]{2,1,0:T(8,128)(2,1)}, ...) while((s32[]{:T(128)}, f32[864,128]{1,0:T(8,128)}, ...), condition=%wide.region_1.2_spmd.clone, body=%wide.region_0.1_spmd.clone.sunk | while | flops 1365792768 | bytes 46059632 | solution.py:72
  100.9 2.2 convolution_bitcast_fusion.3
  104.2 2.6 fusion.115
  109.1 0.9 select_dynamic-update-slice_fusion.67
  111.4 3.1 fusion.112
  114.5 2.9 convolution_add_fusion.2
  117.4 2.2 convolution_bitcast_fusion.3
  120.7 2.6 fusion.115
  125.6 0.9 select_dynamic-update-slice_fusion.67
  127.9 3.1 fusion.112
  130.9 3.0 convolution_add_fusion.2
  134.0 2.2 convolution_bitcast_fusion.3
  137.3 2.6 fusion.115
  142.1 0.9 select_dynamic-update-slice_fusion.67
  144.4 3.1 fusion.112
  147.5 3.0 convolution_add_fusion.2
  150.5 2.2 convolution_bitcast_fusion.3
  153.8 2.6 fusion.115
  158.7 0.9 select_dynamic-update-slice_fusion.67
  161.0 3.1 fusion.112
  164.1 3.0 convolution_add_fusion.2
  167.1 2.2 convolution_bitcast_fusion.3
  170.4 2.6 fusion.115
  175.2 0.9 select_dynamic-update-slice_fusion.67
  177.6 3.1 fusion.112
  180.6 3.0 convolution_add_fusion.2
  183.7 2.2 convolution_bitcast_fusion.3
  187.0 2.6 fusion.115
  191.8 0.9 select_dynamic-update-slice_fusion.67
  194.1 3.1 fusion.112
  197.2 3.0 convolution_add_fusion.2
  200.2 2.2 convolution_bitcast_fusion.3
  203.5 2.6 fusion.115
  208.4 0.9 select_dynamic-update-slice_fusion.67
  210.7 3.1 fusion.112
  213.8 3.0 convolution_add_fusion.2
  216.8 2.2 convolution_bitcast_fusion.3
  220.1 2.6 fusion.115
  227.3 3.2 fusion.112
  230.4 3.0 convolution_add_fusion.2
  235.3 39.9 %reduce-scatter.5.cloned.1.call-done = f32[1,32,2048]{2,1,0:T(8,128)} async-done(((f32[8,32,2048]{2,1,0:T(8,128)}), f32[1,32,2048]{2,1,0:T(8,128)}) %reduce-scatter.5.cloned.1.call-update) | async-done | bytes 262160 | tf_op jit(solution)/shard_map/reduce_scatter | solution.py:74
  275.2 1.6 convert_element_type.67
  276.9 103.7 %reduce-scatter.3.cloned.1.call-done = f32[8,128,64]{1,2,0:T(8,128)} async-done(((f32[8,128,2048]{1,2,0:T(8,128)}), f32[8,128,64]{1,2,0:T(8,128)}) %reduce-scatter.3.cloned.1.call-update) | async-done | bytes 262160 | tf_op jit(solution)/shard_map/reduce_scatter | solution.py:73
  380.6 1.6 convert_element_type.66
  (359 shorter events, 39.1 us)
Async XLA Ops:
  7.2 59.3 %all-gather.5.cloned.1.call-start = ((), (), s32[]{:S(2)}) async-start(), calls=%async_computation.3 | async-start | bytes 4325376 | tf_op jit(solution)/shard_map/all_gather | solution.py:51
  8.9 92.0 %all-gather.3.cloned.1.call-start = ((), (), s32[]{:S(2)}) async-start(), calls=%async_computation.2 | async-start | bytes 1179648 | tf_op jit(solution)/shard_map/all_gather | solution.py:50
  9.6 265.6 %reduce-scatter.5.cloned.1.call-start = ((), (), s32[]{:S(2)}) async-start(), calls=%async_computation.5 | async-start | bytes 2359296 | tf_op jit(solution)/shard_map/reduce_scatter | solution.py:74
  233.5 147.1 %reduce-scatter.3.cloned.1.call-start = ((), (), s32[]{:S(2)}) async-start(), calls=%async_computation.4 | async-start | bytes 8650752 | tf_op jit(solution)/shard_map/reduce_scatter | solution.py:73
  233.5 1.0 copy-start
Sparse Core Ops, SparseCore 0:
  11.1 55.2 all-gather.4
  68.3 32.6 all-gather.2
  233.6 41.6 reduce-scatter.4
  279.1 101.4 reduce-scatter.2
where the time goes:
time: 391 us; the launch traced here: 389 us
  waiting for transfers between devices  229 us (59%)
  matrix products  66.6 us (17%)
  other arithmetic  54.1 us (14%)
  local copies, waits for them, and re-layouts  22.5 us (6%)
  between operations  13.8 us (4%)
    reduce_scatter x1, waiting for transfers between devices, body(): lax.psum_scatter(partials, 'cin', scatter_dimension=2, tiled=True)  104 us
    all_gather x1, waiting for transfers between devices, body(): grad_full = lax.all_gather(grad_out, 'cin', axis=2, tiled=True)  56.8 us
    reduce_scatter x1, waiting for transfers between devices, body(): lax.psum_scatter(input_terms, 'cout', scatter_dimension=0, tiled=True)  39.9 us
    all_gather x1, waiting for transfers between devices, body(): gathered = lax.all_gather(inputs, 'cout', axis=0, tiled=True)  27.8 us
    while x208, other arithmetic  27.2 us
    dot_general x8, matrix products, one_sample(): lax.dot_general(flat_weight, columns, (((0,), (0,)), ((), ())), preferred...  24.7 us
    dot_general x8, matrix products, one_sample(): lax.dot_general(columns, grad_rows, (((1,), (1,)), ((), ())), preferred_e...  24.1 us
    dynamic_update_slice x8, other arithmetic, body(): lax.scan(one_sample, start_sum, (gathered, grad_full))  20.6 us
  transfers between devices with their start and end apart: 4, of which 4 were waited for; matrix products, arithmetic and copies ran while one was open for 2% of the time, Pallas kernels for 0%

commit v1 on v0

v1 whole, which is shorter than its diff:
```python
import functools
import math

import jax
import jax.numpy as jnp
from jax import lax
from jax.experimental import pallas as pl
from jax.experimental.pallas import tpu as pltpu
from jax.sharding import PartitionSpec as P

SX = 16
SY = 16
SZ = 8
PLANE = SY * SZ
SIDE = 4
BF16 = jnp.bfloat16
F16 = jnp.float16
F32 = jnp.float32

in_plane = [(b, c) for b in (-1, 0, 1) for c in (-1, 0, 1)]
VMEM_LIMIT = 40 * 1024 * 1024


def move_xy(value, dy, dx, flip=0):
    pairs = []
    for y in range(SIDE):
        for x in range(SIDE):
            for core in range(2):
                target = ((y + dy) % SIDE * SIDE + (x + dx) % SIDE) * 2 + (core ^ flip)
                pairs.append(((y * SIDE + x) * 2 + core, target))
    return lax.ppermute(value, "cin", pairs)


def swap_cores(value):
    return move_xy(value, 0, 0, 1)


def plane_mask(rows, b, c):
    lane = lax.broadcasted_iota(jnp.int32, (rows, PLANE), 1)
    y = (lane >> 3) + b
    z = (lane & 7) + c
    return (y >= 0) & (y < SY) & (z >= 0) & (z < SZ)


def dgrad_kernel(place, *refs):
    half_a, half_b = refs[0:4], refs[4:8]
    wd_ref, taps_ref, out_ref = refs[8:11]
    ci = out_ref.shape[1]
    co = taps_ref.shape[2] // 3
    n = pl.program_id(0)
    my_y, my_x = place[0], place[1]

    def fill(parts, first, second, flip):
        for p in range(SX):
            y, x = p // SIDE, p % SIDE
            rel_y = lax.rem(my_y - y + SIDE, SIDE)
            rel_x = lax.rem(my_x - x + SIDE, SIDE)
            outer, inner = (rel_y, rel_x) if not flip else (rel_x, rel_y)
            for index in range(4):

                @pl.when(outer == index)
                def _():
                    cells = parts[index][inner, lax.rem(n, 2)]
                    for a in (-1, 0, 1):
                        q = p + a
                        if 0 <= q < SX:
                            taps_ref[0, q * PLANE : (q + 1) * PLANE, (a + 1) * co : (a + 2) * co] = cells

    taps_ref[0, (SX - 1) * PLANE :, 0:co] = jnp.zeros((PLANE, co), BF16)
    taps_ref[0, 0:PLANE, 2 * co :] = jnp.zeros((PLANE, co), BF16)

    @pl.when(n < 2)
    def _():
        fill(half_a, 0, 1, False)

    @pl.when(n >= 2)
    def _():
        fill(half_b, 0, 1, True)

    wd = wd_ref[...]
    step = 4
    for first in range(0, SX, step):
        rows = taps_ref[0, first * PLANE : (first + step) * PLANE, :]
        product = lax.dot_general(wd, rows, (((1,), (1,)), ((), ())), preferred_element_type=F32)
        for j in range(step):
            total = None
            for index, (b, c) in enumerate(in_plane):
                term = product[index * ci : (index + 1) * ci, j * PLANE : (j + 1) * PLANE]
                shift = (b * SZ + c) % PLANE
                if shift:
                    term = jnp.where(plane_mask(ci, -b, -c), pltpu.roll(term, shift, 1), 0.0)
                total = term if total is None else total + term
            out_ref[0, :, (first + j) * PLANE : (first + j + 1) * PLANE] = total


def fwd_kernel(place, in_ref, wa_ref, cols_ref, out_a, out_b, peak_ref, stage):
    ci = in_ref.shape[1]
    co = wa_ref.shape[0] // 3
    n = pl.program_id(0)
    my_y, my_x = place[0], place[1]

    @pl.when(n == 0)
    def _():
        peak_ref[...] = jnp.zeros_like(peak_ref)

    for p in range(SX):
        cells = in_ref[0, :, p * PLANE : (p + 1) * PLANE].astype(F32)
        for index, (b, c) in enumerate(in_plane):
            shift = -(b * SZ + c) % PLANE
            term = cells
            if shift:
                term = jnp.where(plane_mask(ci, b, c), pltpu.roll(term, shift, 1), 0.0)
            cols_ref[0, index * ci : (index + 1) * ci, p * PLANE : (p + 1) * PLANE] = term.astype(BF16)

    step = 4
    for first in range(0, SX, step):
        lanes = slice(first * PLANE, (first + step) * PLANE)
        stage[:, lanes] = jnp.dot(wa_ref[...], cols_ref[0, :, lanes], preferred_element_type=F32)

    peak = None
    for p in range(SX):
        total = stage[co : 2 * co, p * PLANE : (p + 1) * PLANE]
        if p > 0:
            total = total + stage[0:co, (p - 1) * PLANE : p * PLANE]
        if p < SX - 1:
            total = total + stage[2 * co :, (p + 1) * PLANE : (p + 2) * PLANE]
        y, x = p // SIDE, p % SIDE
        rel_y = lax.rem(y - my_y + SIDE, SIDE)
        rel_x = lax.rem(x - my_x + SIDE, SIDE)

        @pl.when(n < 2)
        def _():
            out_a[rel_x, rel_y, lax.rem(n, 2)] = total

        @pl.when(n >= 2)
        def _():
            out_b[rel_y, rel_x, lax.rem(n, 2)] = total

        size = jnp.abs(total)
        peak = size if peak is None else jnp.maximum(peak, size)
    peak_ref[...] = jnp.maximum(peak_ref[...], peak)


def wgrad_kernel(cols_ref, taps_ref, out_ref):
    @pl.when(pl.program_id(0) == 0)
    def _():
        out_ref[...] = jnp.zeros_like(out_ref)

    out_ref[...] += jnp.dot(cols_ref[0], taps_ref[0], preferred_element_type=F32)


def whole(shape):
    return pl.BlockSpec(shape, lambda *_: (0,) * len(shape))


def per_sample(shape):
    return pl.BlockSpec((1,) + shape, lambda n, *_: (n,) + (0,) * len(shape))


def coded(block, power):
    rows = (block * jnp.exp2(power)).reshape(-1, block.shape[-1]).astype(F16)
    note = jnp.broadcast_to(power, (16, block.shape[-1])).astype(F16)
    return jnp.concatenate([rows, note], axis=0)


def decoded(message, shape):
    power = message[-1, 0].astype(F32)
    return message[:-16].astype(F32).reshape(shape) * jnp.exp2(-power), power


def reduce_stage(blocks, power, moves):
    arrived = [moves[s](coded(blocks[s], power)) for s in (1, 2, 3)]
    total, least = blocks[0], power
    for message in arrived:
        value, other = decoded(message, total.shape)
        total, least = total + value, jnp.minimum(least, other)
    return total, least


def body(inputs, weight, grad_out):
    ci, co = weight.shape[1], weight.shape[2]
    where_cin = lax.axis_index("cin")
    core = where_cin % 2
    place = jnp.stack([where_cin // 2 // SIDE, where_cin // 2 % SIDE]).astype(jnp.int32)
    batch = grad_out.shape[0]
    mine = batch // 2
    first_core = core == 0

    def split(value, size, axis):
        own = lax.dynamic_slice_in_dim(value, core * size, size, axis)
        other = lax.dynamic_slice_in_dim(value, (1 - core) * size, size, axis)
        return own, other

    def in_order(own, other, axis):
        return jnp.where(
            first_core,
            jnp.concatenate([own, other], axis),
            jnp.concatenate([other, own], axis),
        )

    gathered = lax.all_gather(inputs, "cout", axis=0, tiled=True)

    own, other = split(jnp.transpose(grad_out, (0, 2, 1)), mine, 0)
    plane = in_order(own, swap_cores(other), 1)
    along_x = [None] + [functools.partial(move_xy, dy=0, dx=s) for s in (1, 2, 3)]
    along_y = [None] + [functools.partial(move_xy, dy=s, dx=0) for s in (1, 2, 3)]

    def gather_stage(value, moves):
        return [value] + [moves[s](value) for s in (1, 2, 3)]

    row_a = jnp.stack(gather_stage(plane[: mine // 2], along_x))
    row_b = jnp.stack(gather_stage(plane[mine // 2 :], along_y))
    parts = gather_stage(row_a, along_y) + gather_stage(row_b, along_x)

    pair = in_order(weight, swap_cores(weight), 1)
    wd = jnp.transpose(pair.reshape(3, 9, 2 * ci, co), (1, 2, 0, 3)).reshape(9 * 2 * ci, 3 * co)
    wa = wd.T

    cells = inputs.shape[2]
    params = pltpu.CompilerParams(vmem_limit_bytes=VMEM_LIMIT)
    taps, input_term = pl.pallas_call(
        dgrad_kernel,
        grid_spec=pltpu.PrefetchScalarGridSpec(
            num_scalar_prefetch=1,
            grid=(mine,),
            in_specs=[whole(p.shape) for p in parts] + [whole(wd.shape)],
            out_specs=[per_sample((cells, 3 * co)), per_sample((2 * ci, cells))],
        ),
        out_shape=[
            jax.ShapeDtypeStruct((mine, cells, 3 * co), BF16),
            jax.ShapeDtypeStruct((mine, 2 * ci, cells), F32),
        ],
        compiler_params=params,
        name="dgrad",
    )(place, *parts, wd)

    own, other = split(input_term, ci, 1)
    input_term = in_order(own, swap_cores(other), 0)
    grad_input = lax.psum_scatter(input_term, "cout", scatter_dimension=0, tiled=True).astype(BF16)

    own, other = split(gathered, mine, 0)
    sample = in_order(own, swap_cores(other), 1)
    half = (SIDE, SIDE, mine // 2, co, PLANE)
    columns, out_a, out_b, peak = pl.pallas_call(
        fwd_kernel,
        grid_spec=pltpu.PrefetchScalarGridSpec(
            num_scalar_prefetch=1,
            grid=(mine,),
            in_specs=[per_sample((2 * ci, cells)), whole(wa.shape)],
            out_specs=[per_sample((9 * 2 * ci, cells)), whole(half), whole(half), whole((co, PLANE))],
            scratch_shapes=[pltpu.VMEM((3 * co, cells), F32)],
        ),
        out_shape=[
            jax.ShapeDtypeStruct((mine, 9 * 2 * ci, cells), BF16),
            jax.ShapeDtypeStruct(half, F32),
            jax.ShapeDtypeStruct(half, F32),
            jax.ShapeDtypeStruct((co, PLANE), F32),
        ],
        compiler_params=params,
        name="forward",
    )(place, sample, wa)

    power = 14.0 - jnp.ceil(jnp.log2(jnp.maximum(jnp.max(peak), 1e-30)))
    sum_a, power_a = reduce_stage(out_a, power, along_x)
    sum_b, power_b = reduce_stage(out_b, power, along_y)
    sum_a, _ = reduce_stage(sum_a, power_a - 2.0, along_y)
    sum_b, _ = reduce_stage(sum_b, power_b - 2.0, along_x)
    output = jnp.transpose(jnp.concatenate([sum_a, sum_b], 0).astype(BF16), (0, 2, 1))
    own, other = split(output, PLANE // 2, 1)
    output = jnp.transpose(in_order(own, swap_cores(other), 0), (0, 2, 1))

    grad_sum = pl.pallas_call(
        wgrad_kernel,
        grid=(mine,),
        in_specs=[per_sample((9 * 2 * ci, cells)), per_sample((cells, 3 * co))],
        out_specs=whole((9 * 2 * ci, 3 * co)),
        out_shape=jax.ShapeDtypeStruct((9 * 2 * ci, 3 * co), F32),
        compiler_params=params,
        name="wgrad",
    )(columns, taps)
    grad_sum = jnp.transpose(grad_sum.reshape(9, 2 * ci, 3, co), (2, 0, 1, 3)).reshape(27, 2 * ci, co)
    own, other = split(grad_sum, ci, 1)
    grad_weight = (own + swap_cores(other)) / math.sqrt(batch * cells)
    return output, grad_input, grad_weight


def solution(mesh):
    placed = (P("cout", "cin", None), P(None, "cin", "cout"), P(None, "cout", "cin"))
    return jax.shard_map(
        body,
        mesh=mesh,
        in_specs=placed,
        out_specs=(P(None, "cout", "cin"), P("cout", "cin", None), P(None, "cin", "cout")),
        check_vma=False,
    )
```

time: 391 us -> 174 us (0.45)
  waiting for transfers between devices: 229 us -> 22 us
  matrix products: 66.6 us -> 0 us
  starting transfers between devices: 0.16 us -> 40 us
  other arithmetic: 54.1 us -> 21.3 us
  Pallas kernels: 0 us -> 27 us
  local copies, waits for them, and re-layouts: 22.5 us -> 38.6 us
  between operations: 13.8 us -> 23.7 us
    reduce_scatter x2 -> x1, waiting for transfers between devices: 144 us -> 0.01 us  [body(): lax.psum_scatter(input_term, 'cout', scatter_dimension=0, tiled=True)]
    dot_general x24 -> x0, matrix products: 66.6 us -> none  [the longest x8 24.7 us: one_sample(): lax.dot_general(flat_weight, columns, (((0,), (0,)), ((), ())), preferred...]
    all_gather x1 -> x0, waiting for transfers between devices: 56.8 us -> none  [body(): grad_full = lax.all_gather(grad_out, 'cin', axis=2, tiled=True)]
    ppermute x0 -> x30, starting transfers between devices: none -> 40 us  [move_xy(): return lax.ppermute(value, 'cin', pairs)]
    while x208 -> x0, other arithmetic: 27.2 us -> none
    pallas_call x0 -> x3, Pallas kernels: none -> 27 us  [the longest x1 10.1 us: body(): pl.pallas_call(fwd_kernel, grid_spec=pltpu.PrefetchScalarGridSpec(num_sca...]
    dynamic_update_slice x8 -> x0, other arithmetic: 20.6 us -> none  [body(): lax.scan(one_sample, start_sum, (gathered, grad_full))]
    all_gather x1, waiting for transfers between devices: 27.8 us -> 12.5 us  [body(): gathered = lax.all_gather(inputs, 'cout', axis=0, tiled=True)]
  transfers between devices with their start and end apart: 4 -> 32, of which waited for: 4 -> 9; matrix products, arithmetic and copies ran while one was open for 2% -> 30% of each run, Pallas kernels for 0% -> 16%
where the time goes in v1:
time: 174 us; the launch traced here: 173 us
  starting transfers between devices  40 us (23%)
  local copies, waits for them, and re-layouts  38.6 us (22%)
  Pallas kernels  27 us (16%)
  between operations  23.7 us (14%)
  waiting for transfers between devices  22 us (13%)
  other arithmetic  21.3 us (12%)
    ppermute x30, starting transfers between devices, move_xy(): return lax.ppermute(value, 'cin', pairs)  40 us
    all_gather x1, waiting for transfers between devices, body(): gathered = lax.all_gather(inputs, 'cout', axis=0, tiled=True)  12.5 us
    slice x12, local copies, waits for them, and re-layouts, decoded(): power = message[-1, 0].astype(F32)  11.7 us
    concatenate x12, local copies, waits for them, and re-layouts, coded(): return jnp.concatenate([rows, note], axis=0)  10.4 us
    pallas_call x1, Pallas kernels, body(): pl.pallas_call(fwd_kernel, grid_spec=pltpu.PrefetchScalarGridSpec(num_sca...  10.1 us
    pallas_call x1, Pallas kernels, body(): pl.pallas_call(dgrad_kernel, grid_spec=pltpu.PrefetchScalarGridSpec(num_s...  9.26 us
    ppermute x30, waiting for transfers between devices, move_xy(): return lax.ppermute(value, 'cin', pairs)  8.83 us
    mul x12, other arithmetic, decoded(): return (message[:-16].astype(F32).reshape(shape) * jnp.exp2(-power), power)  8.55 us
  transfers between devices with their start and end apart: 32, of which 9 were waited for; matrix products, arithmetic and copies ran while one was open for 30% of the time, Pallas kernels for 16%

profile of v1, /device:TPU:1, one launch (start us, length us, event | category | flops | bytes accessed | tf_op | source)
XLA Modules:
  0.0 172.6 jit_solution(7587731221317359375)
XLA Ops:
  8.9 3.3 %collective-permute-start.15 = (bf16[4,64,128]{2,1,0:T(8,128)(2,1)S(1)}, bf16[4,64,128]{2,1,0:T(8,128)(2,1)S(1)}, u32[]{:S(2)}, u32[]{:S(2)}) collective-permute-start(bf16[4,64,128]{2,1,0:T(8,128)(2,1)S(1)} %get-tuple-element.48), channel_id=1, source_target_pairs={{0,8},{8,0},{16,24},{24,16},{32,40},{40,32},{48,56},{56,48},{64,72... | collective-permute-start | bytes 196616 | tf_op jit(solution)/shard_map/ppermute | solution.py:31
  15.1 1.2 collective-permute-done.18
  16.4 2.3 %collective-permute-done.17 = bf16[2,128,128]{2,1,0:T(8,128)(2,1)S(1)} collective-permute-done((bf16[2,128,128]{2,1,0:T(8,128)(2,1)S(1)}, bf16[2,128,128]{2,1,0:T(8,128)(2,1)S(1)}, u32[]{:S(2)}, u32[]{:S(2)}) %collective-permute-start.17) | collective-permute-done | bytes 65568 | tf_op jit(solution)/shard_map/ppermute | solution.py:31
  18.7 1.7 %collective-permute-done.16 = bf16[2,128,128]{2,1,0:T(8,128)(2,1)S(1)} collective-permute-done((bf16[2,128,128]{2,1,0:T(8,128)(2,1)S(1)}, bf16[2,128,128]{2,1,0:T(8,128)(2,1)S(1)}, u32[]{:S(2)}, u32[]{:S(2)}) %collective-permute-start.16) | collective-permute-done | bytes 65568 | tf_op jit(solution)/shard_map/ppermute | solution.py:31
  21.3 1.8 %collective-permute-start.1 = (bf16[27,32,128]{2,1,0:T(8,128)(2,1)}, bf16[27,32,128]{2,1,0:T(8,128)(2,1)S(1)}, u32[]{:S(2)}, u32[]{:S(2)}) collective-permute-start(bf16[27,32,128]{2,1,0:T(8,128)(2,1)} %param.4), channel_id=1, source_target_pairs={{0,8},{8,0},{16,24},{24,16},{32,40},{40,32},{48,56},{56,48},{64,72... | collective-permute-start | bytes 663560 | tf_op jit(solution)/shard_map/ppermute | solution.py:31
  23.1 1.1 copy.26
  24.2 1.5 collective-permute-start.24
  25.7 1.7 collective-permute-start.23
  28.1 2.6 %collective-permute-start.20 = (bf16[4,2,128,128]{3,2,1,0:T(8,128)(2,1)S(1)}, bf16[4,2,128,128]{3,2,1,0:T(8,128)(2,1)S(1)}, u32[]{:S(2)}, u32[]{:S(2)}) collective-permute-start(bf16[4,2,128,128]{3,2,1,0:T(8,128)(2,1)S(1)} %pad_maximum_fusion.refs_0_), channel_id=1, source_target_pairs={{0,128},{8,136},{16,144},{24,152},{32,160},{40,168},{48,176},{56,1... | collective-permute-start | bytes 786440 | tf_op jit(solution)/shard_map/ppermute | solution.py:31
  32.6 2.4 %collective-permute-start.26 = (bf16[4,2,128,128]{3,2,1,0:T(8,128)(2,1)S(1)}, bf16[4,2,128,128]{3,2,1,0:T(8,128)(2,1)S(1)}, u32[]{:S(2)}, u32[]{:S(2)}) collective-permute-start(bf16[4,2,128,128]{3,2,1,0:T(8,128)(2,1)S(1)} %pad_maximum_fusion.1.refs_4_), channel_id=1, source_target_pairs={{0,32},{8,40},{16,48},{24,56},{32,0},{40,8},{48,16},{56,24},{64,96... | collective-permute-start | bytes 786440 | tf_op jit(solution)/shard_map/ppermute | solution.py:31
  35.5 12.5 %all-gather.2.cloned.1.call-done = bf16[8,32,2048]{2,1,0:T(8,128)(2,1)} async-done(((bf16[1,32,2048]{2,1,0:T(8,128)(2,1)}), bf16[8,32,2048]{2,1,0:T(8,128)(2,1)}) %all-gather.2.cloned.1.call-update) | async-done | bytes 1048592 | tf_op jit(solution)/shard_map/all_gather | solution.py:201
  48.0 2.3 %constant_dynamic-slice_fusion.4 = (bf16[4,32,2048]{2,1,0:T(8,128)(2,1)}, bf16[4,32,2048]{2,1,0:T(8,128)(2,1)}) fusion(bf16[8,32,2048]{2,1,0:T(8,128)(2,1)} %all-gather.2.cloned.1.call-done, s32[]{:T(128)S(6)} %select_n.88, s32[]{:T(128)S(6)} %select_n.89), kind=kLoop, calls=%fused_computation.70 | loop fusion | bytes 2097160 | tf_op jit(solution)/shard_map/dynamic_slice | solution.py:190
  50.3 4.9 %collective-permute-start = (bf16[4,32,2048]{2,1,0:T(8,128)(2,1)}, bf16[4,32,2048]{2,1,0:T(8,128)(2,1)}, u32[]{:S(2)}, u32[]{:S(2)}) collective-permute-start(bf16[4,32,2048]{2,1,0:T(8,128)(2,1)} %get-tuple-element.36), channel_id=1, source_target_pairs={{0,8},{8,0},{16,24},{24,16},{32,40},{40,32},{48,56},{56,48},{64,72... | collective-permute-start | bytes 1572872 | tf_op jit(solution)/shard_map/ppermute | solution.py:31
  55.7 9.3 %dgrad.1 = (bf16[4,2048,384]{2,1,0:T(8,128)(2,1)S(1)}, f32[4,64,2048]{2,1,0:T(8,128)S(1)}) custom-call(s32[2]{0:T(128)S(1)} %pad_add_fusion.place, bf16[4,2,128,128]{3,2,1,0:T(8,128)(2,1)S(1)} %pad_maximum_fusion.refs_0_, bf16[4,2,128,128]{3,2,1,0:T(8,128)(2,1)S(1)} %collective-permute-done.19.refs_1_, ...), custom_call_target="tpu_custom_call" | custom-call | tf_op jit(solution)/shard_map/dgrad/pallas_call | solution.py:221
  65.0 2.6 %copy-done = bf16[4,2048,384]{2,1,0:T(8,128)(2,1)} copy-done((bf16[4,2048,384]{2,1,0:T(8,128)(2,1)}, bf16[4,2048,384]{2,1,0:T(8,128)(2,1)S(1)}, u32[]{:S(2)}) %copy-start) | copy-done | bytes 6291480
  67.6 1.6 constant_dynamic-slice_fusion.2
  69.4 1.6 maximum_select_fusion.1.in_ref
  71.0 10.1 %forward.1 = (bf16[4,576,2048]{2,1,0:T(8,128)(2,1)}, f32[4,4,2,128,128]{4,3,2,1,0:T(8,128)S(1)}, f32[4,4,2,128,128]{4,3,2,1,0:T(8,128)S(1)}, f32[128,128]{1,0:T(8,128)S(1)}) custom-call(s32[2]{0:T(128)S(1)} %pad_add_fusion.place, bf16[4,64,2048]{2,1,0:T(8,128)(2,1)S(1)} %maximum_select_fusion.1.in_ref, bf16[384,576]{1,0:T(8,128)(2,1)S(1)} %bitcast.109), custom_call_target="tpu_custom_call" | custom-call | tf_op jit(solution)/shard_map/forward/pallas_call | solution.py:244
  81.1 1.3 copy-done.2
  83.8 2.7 %multiply_convert_fusion.2 = (f16[1,4,2,128,128]{4,3,2,1,0:T(8,128)(2,1)S(1)}, f16[1,4,2,128,128]{4,3,2,1,0:T(8,128)(2,1)}, f16[1,4,2,128,128]{4,3,2,1,0:T(8,128...) fusion(f32[4,4,2,128,128]{4,3,2,1,0:T(8,128)S(1)} %get-tuple-el, ...), kind=kLoop, calls=%fused_computation.14 | loop fusion | flops 1572864 | bytes 4718596 | tf_op jit(solution)/shard_map/convert_element_type | solution.py:161
  87.2 1.2 collective-permute-start.2
  88.4 1.7 concatenate.84
  90.1 1.5 collective-permute-start.4
  91.6 1.7 concatenate.83
  93.3 1.5 collective-permute-start.3
  94.8 1.7 %concatenate.90 = f16[1040,128]{1,0:T(8,128)(2,1)} pad(f16[1024,128]{1,0:T(8,128)(2,1)} %bitcast.122, f16[]{:T(256)S(6)} %convert_element_type.195), padding=0_16x0_0 | pad | bytes 528386 | tf_op jit(solution)/shard_map/concatenate | solution.py:163
  96.5 2.5 %collective-permute-start.10 = (f16[1040,128]{1,0:T(8,128)(2,1)}, f16[1040,128]{1,0:T(8,128)(2,1)}, u32[]{:S(2)}, u32[]{:S(2)}) collective-permute-start(f16[1040,128]{1,0:T(8,128)(2,1)} %concatenate.90), channel_id=1, source_target_pairs={{0,192},{8,200},{16,208},{24,216},{32,224},{40,232},{48,240},{56,2... | collective-permute-start | bytes 798728 | tf_op jit(solution)/shard_map/ppermute | solution.py:31
  99.0 1.7 concatenate.89
  102.6 3.1 %maximum_select_fusion = f32[8,32,2048]{2,1,0:T(8,128)} fusion(f32[4,32,2048]{2,1,0:T(8,128)} %collective-permute-done.28, f32[4,32,2048]{2,1,0:T(8,128)S(1)} %copy-done.3, pred[]{:T(512)S(6)} %eq.6), kind=kLoop, calls=%fused_computation | loop fusion | flops 1572864 | bytes 4194305 | tf_op jit(solution)/shard_map/jit(_where)/select_n | solution.py:195
  105.7 2.8 %copy-done.1 = bf16[4,2048,384]{2,1,0:T(8,128)(2,1)S(1)} copy-done((bf16[4,2048,384]{2,1,0:T(8,128)(2,1)S(1)}, bf16[4,2048,384]{2,1,0:T(8,128)(2,1)}, u32[]{:S(2)}) %copy-start.1) | copy-done | bytes 6291480
  108.5 7.7 %wgrad.1 = f32[576,384]{1,0:T(8,128)S(1)} custom-call(bf16[4,576,2048]{2,1,0:T(8,128)(2,1)} %get-tuple-element.13.cols_ref, bf16[4,2048,384]{2,1,0:T(8,128)(2,1)S(1)} %copy-done.1), custom_call_target="tpu_custom_call" | custom-call | tf_op jit(solution)/shard_map/wgrad/pallas_call | solution.py:272
  116.2 1.4 reshape.159
  117.6 1.4 copy.31
  119.0 1.2 slice.169
  120.8 1.2 slice.173
  122.7 1.2 slice.171
  124.5 1.2 slice.185
  126.4 1.2 slice.189
  132.7 1.2 fusion.3
  134.5 2.0 %collective-permute-start.7 = (f16[272,128]{1,0:T(8,128)(2,1)}, f16[272,128]{1,0:T(8,128)(2,1)}, u32[]{:S(2)}, u32[]{:S(2)}) collective-permute-start(f16[272,128]{1,0:T(8,128)(2,1)} %concatenate.87), channel_id=1, source_target_pairs={{0,192},{8,200},{16,208},{24,216},{32,224},{40,232},{48,240},{56,2... | collective-permute-start | bytes 208904 | tf_op jit(solution)/shard_map/ppermute | solution.py:31
  137.2 1.3 collective-permute-start.6
  143.5 1.3 collective-permute-start.12
  145.1 1.2 slice.183
  147.0 3.7 %collective-permute-start.29 = (f32[27,32,128]{2,1,0:T(8,128)S(1)}, f32[27,32,128]{2,1,0:T(8,128)S(1)}, u32[]{:S(2)}, u32[]{:S(2)}) collective-permute-start(f32[27,32,128]{2,1,0:T(8,128)S(1)} %constant_dynamic-slice_fusion), channel_id=1, source_target_pairs={{0,8},{8,0},{16,24},{24,16},{32,40},{40,32},{48,56},{56,48},{64,72... | collective-permute-start | bytes 1327112 | tf_op jit(solution)/shard_map/ppermute | solution.py:31
  150.7 1.2 slice.180
  152.6 1.2 slice.177
  161.1 1.3 collective-permute-done.14
  164.2 1.6 convert_element_type.250
  (100 shorter events, 29.0 us)
Async XLA Ops:
  7.2 40.9 %all-gather.2.cloned.1.call-start = ((), (), s32[]{:S(2)}) async-start(), calls=%async_computation.1 | async-start | bytes 1179648 | tf_op jit(solution)/shard_map/all_gather | solution.py:201
  7.9 156.3 %reduce-scatter.2.cloned.1.call-start = ((), (), s32[]{:S(2)}) async-start(), calls=%async_computation.2 | async-start | bytes 2359296 | tf_op jit(solution)/shard_map/reduce_scatter | solution.py:239
  8.9 4.2 %collective-permute-start.15 = (bf16[4,64,128]{2,1,0:T(8,128)(2,1)S(1)}, bf16[4,64,128]{2,1,0:T(8,128)(2,1)S(1)}, u32[]{:S(2)}, u32[]{:S(2)}) collective-permute-start(bf16[4,64,128]{2,1,0:T(8,128)(2,1)S(1)} %get-tuple-element.48), channel_id=1, source_target_pairs={{0,8},{8,0},{16,24},{24,16},{32,40},{40,32},{48,56},{56,48},{64,72... | collective-permute-start | bytes 196616 | tf_op jit(solution)/shard_map/ppermute | solution.py:31
  13.2 3.2 %collective-permute-start.18 = (bf16[2,128,128]{2,1,0:T(8,128)(2,1)S(1)}, bf16[2,128,128]{2,1,0:T(8,128)(2,1)S(1)}, u32[]{:S(2)}, u32[]{:S(2)}) collective-permute-start(bf16[2,128,128]{2,1,0:T(8,128)(2,1)S(1)} %get-tuple-element.46), channel_id=1, source_target_pairs={{0,48},{8,56},{16,0},{24,8},{32,16},{40,24},{48,32},{56,40},{64,11... | collective-permute-start | bytes 196616 | tf_op jit(solution)/shard_map/ppermute | solution.py:31
  14.0 4.7 %collective-permute-start.17 = (bf16[2,128,128]{2,1,0:T(8,128)(2,1)S(1)}, bf16[2,128,128]{2,1,0:T(8,128)(2,1)S(1)}, u32[]{:S(2)}, u32[]{:S(2)}) collective-permute-start(bf16[2,128,128]{2,1,0:T(8,128)(2,1)S(1)} %get-tuple-element.46), channel_id=1, source_target_pairs={{0,32},{8,40},{16,48},{24,56},{32,0},{40,8},{48,16},{56,24},{64,96... | collective-permute-start | bytes 196616 | tf_op jit(solution)/shard_map/ppermute | solution.py:31
  14.5 5.9 %collective-permute-start.16 = (bf16[2,128,128]{2,1,0:T(8,128)(2,1)S(1)}, bf16[2,128,128]{2,1,0:T(8,128)(2,1)S(1)}, u32[]{:S(2)}, u32[]{:S(2)}) collective-permute-start(bf16[2,128,128]{2,1,0:T(8,128)(2,1)S(1)} %get-tuple-element.46), channel_id=1, source_target_pairs={{0,16},{8,24},{16,32},{24,40},{32,48},{40,56},{48,0},{56,8},{64,80... | collective-permute-start | bytes 196616 | tf_op jit(solution)/shard_map/ppermute | solution.py:31
  20.4 14.8 %collective-permute-start.19 = (bf16[4,2,128,128]{3,2,1,0:T(8,128)(2,1)S(1)}, bf16[4,2,128,128]{3,2,1,0:T(8,128)(2,1)S(1)}, u32[]{:S(2)}, u32[]{:S(2)}) collective-permute-start(bf16[4,2,128,128]{3,2,1,0:T(8,128)(2,1)S(1)} %pad_maximum_fusion.refs_0_), channel_id=1, source_target_pairs={{0,64},{8,72},{16,80},{24,88},{32,96},{40,104},{48,112},{56,120},{... | collective-permute-start | bytes 786440 | tf_op jit(solution)/shard_map/ppermute | solution.py:31
  21.3 11.3 %collective-permute-start.1 = (bf16[27,32,128]{2,1,0:T(8,128)(2,1)}, bf16[27,32,128]{2,1,0:T(8,128)(2,1)S(1)}, u32[]{:S(2)}, u32[]{:S(2)}) collective-permute-start(bf16[27,32,128]{2,1,0:T(8,128)(2,1)} %param.4), channel_id=1, source_target_pairs={{0,8},{8,0},{16,24},{24,16},{32,40},{40,32},{48,56},{56,48},{64,72... | collective-permute-start | bytes 663560 | tf_op jit(solution)/shard_map/ppermute | solution.py:31
  24.2 3.9 %collective-permute-start.24 = (bf16[2,128,128]{2,1,0:T(8,128)(2,1)S(1)}, bf16[2,128,128]{2,1,0:T(8,128)(2,1)S(1)}, u32[]{:S(2)}, u32[]{:S(2)}) collective-permute-start(bf16[2,128,128]{2,1,0:T(8,128)(2,1)S(1)} %get-tuple-element.45), channel_id=1, source_target_pairs={{0,192},{8,200},{16,208},{24,216},{32,224},{40,232},{48,240},{56,2... | collective-permute-start | bytes 196616 | tf_op jit(solution)/shard_map/ppermute | solution.py:31
  25.7 5.4 %collective-permute-start.23 = (bf16[2,128,128]{2,1,0:T(8,128)(2,1)S(1)}, bf16[2,128,128]{2,1,0:T(8,128)(2,1)S(1)}, u32[]{:S(2)}, u32[]{:S(2)}) collective-permute-start(bf16[2,128,128]{2,1,0:T(8,128)(2,1)S(1)} %get-tuple-element.45), channel_id=1, source_target_pairs={{0,128},{8,136},{16,144},{24,152},{32,160},{40,168},{48,176},{56,1... | collective-permute-start | bytes 196616 | tf_op jit(solution)/shard_map/ppermute | solution.py:31
  27.4 5.1 %collective-permute-start.22 = (bf16[2,128,128]{2,1,0:T(8,128)(2,1)S(1)}, bf16[2,128,128]{2,1,0:T(8,128)(2,1)S(1)}, u32[]{:S(2)}, u32[]{:S(2)}) collective-permute-start(bf16[2,128,128]{2,1,0:T(8,128)(2,1)S(1)} %get-tuple-element.45), channel_id=1, source_target_pairs={{0,64},{8,72},{16,80},{24,88},{32,96},{40,104},{48,112},{56,120},{... | collective-permute-start | bytes 196616 | tf_op jit(solution)/shard_map/ppermute | solution.py:31
  28.1 22.2 %collective-permute-start.20 = (bf16[4,2,128,128]{3,2,1,0:T(8,128)(2,1)S(1)}, bf16[4,2,128,128]{3,2,1,0:T(8,128)(2,1)S(1)}, u32[]{:S(2)}, u32[]{:S(2)}) collective-permute-start(bf16[4,2,128,128]{3,2,1,0:T(8,128)(2,1)S(1)} %pad_maximum_fusion.refs_0_), channel_id=1, source_target_pairs={{0,128},{8,136},{16,144},{24,152},{32,160},{40,168},{48,176},{56,1... | collective-permute-start | bytes 786440 | tf_op jit(solution)/shard_map/ppermute | solution.py:31
  31.1 24.6 %collective-permute-start.21 = (bf16[4,2,128,128]{3,2,1,0:T(8,128)(2,1)S(1)}, bf16[4,2,128,128]{3,2,1,0:T(8,128)(2,1)S(1)}, u32[]{:S(2)}, u32[]{:S(2)}) collective-permute-start(bf16[4,2,128,128]{3,2,1,0:T(8,128)(2,1)S(1)} %pad_maximum_fusion.refs_0_), channel_id=1, source_target_pairs={{0,192},{8,200},{16,208},{24,216},{32,224},{40,232},{48,240},{56,2... | collective-permute-start | bytes 786440 | tf_op jit(solution)/shard_map/ppermute | solution.py:31
  32.5 23.2 %collective-permute-start.25 = (bf16[4,2,128,128]{3,2,1,0:T(8,128)(2,1)S(1)}, bf16[4,2,128,128]{3,2,1,0:T(8,128)(2,1)S(1)}, u32[]{:S(2)}, u32[]{:S(2)}) collective-permute-start(bf16[4,2,128,128]{3,2,1,0:T(8,128)(2,1)S(1)} %pad_maximum_fusion.1.refs_4_), channel_id=1, source_target_pairs={{0,16},{8,24},{16,32},{24,40},{32,48},{40,56},{48,0},{56,8},{64,80... | collective-permute-start | bytes 786440 | tf_op jit(solution)/shard_map/ppermute | solution.py:31
  32.6 23.1 %collective-permute-start.26 = (bf16[4,2,128,128]{3,2,1,0:T(8,128)(2,1)S(1)}, bf16[4,2,128,128]{3,2,1,0:T(8,128)(2,1)S(1)}, u32[]{:S(2)}, u32[]{:S(2)}) collective-permute-start(bf16[4,2,128,128]{3,2,1,0:T(8,128)(2,1)S(1)} %pad_maximum_fusion.1.refs_4_), channel_id=1, source_target_pairs={{0,32},{8,40},{16,48},{24,56},{32,0},{40,8},{48,16},{56,24},{64,96... | collective-permute-start | bytes 786440 | tf_op jit(solution)/shard_map/ppermute | solution.py:31
  35.2 20.5 %collective-permute-start.27 = (bf16[4,2,128,128]{3,2,1,0:T(8,128)(2,1)S(1)}, bf16[4,2,128,128]{3,2,1,0:T(8,128)(2,1)S(1)}, u32[]{:S(2)}, u32[]{:S(2)}) collective-permute-start(bf16[4,2,128,128]{3,2,1,0:T(8,128)(2,1)S(1)} %pad_maximum_fusion.1.refs_4_), channel_id=1, source_target_pairs={{0,48},{8,56},{16,0},{24,8},{32,16},{40,24},{48,32},{56,40},{64,11... | collective-permute-start | bytes 786440 | tf_op jit(solution)/shard_map/ppermute | solution.py:31
  50.3 19.1 %collective-permute-start = (bf16[4,32,2048]{2,1,0:T(8,128)(2,1)}, bf16[4,32,2048]{2,1,0:T(8,128)(2,1)}, u32[]{:S(2)}, u32[]{:S(2)}) collective-permute-start(bf16[4,32,2048]{2,1,0:T(8,128)(2,1)} %get-tuple-element.36), channel_id=1, source_target_pairs={{0,8},{8,0},{16,24},{24,16},{32,40},{40,32},{48,56},{56,48},{64,72... | collective-permute-start | bytes 1572872 | tf_op jit(solution)/shard_map/ppermute | solution.py:31
  65.0 2.6 %copy-start = (bf16[4,2048,384]{2,1,0:T(8,128)(2,1)}, bf16[4,2048,384]{2,1,0:T(8,128)(2,1)S(1)}, u32[]{:S(2)}) copy-start(bf16[4,2048,384]{2,1,0:T(8,128)(2,1)S(1)} %get-tuple-element.14.taps_ref) | copy-start | bytes 18874372
  67.6 1.9 %copy-start.4 = (bf16[4,32,2048]{2,1,0:T(8,128)(2,1)S(1)}, bf16[4,32,2048]{2,1,0:T(8,128)(2,1)}, u32[]{:S(2)}) copy-start(bf16[4,32,2048]{2,1,0:T(8,128)(2,1)} %get-tuple-element.35) | copy-start | bytes 1572868
  69.1 32.4 %collective-permute-start.28 = (f32[4,32,2048]{2,1,0:T(8,128)}, f32[4,32,2048]{2,1,0:T(8,128)}, u32[]{:S(2)}, u32[]{:S(2)}) collective-permute-start(f32[4,32,2048]{2,1,0:T(8,128)} %get-tuple-element.28), channel_id=1, source_target_pairs={{0,8},{8,0},{16,24},{24,16},{32,40},{40,32},{48,56},{56,48},{64,72... | collective-permute-start | bytes 3145736 | tf_op jit(solution)/shard_map/ppermute | solution.py:31
  81.1 1.3 copy-start.2
  86.5 16.1 %copy-start.3 = (f32[4,32,2048]{2,1,0:T(8,128)S(1)}, f32[4,32,2048]{2,1,0:T(8,128)}, u32[]{:S(2)}) copy-start(f32[4,32,2048]{2,1,0:T(8,128)} %get-tuple-element.27) | copy-start | bytes 3145732
  87.2 14.7 %collective-permute-start.2 = (f16[1040,128]{1,0:T(8,128)(2,1)}, f16[1040,128]{1,0:T(8,128)(2,1)}, u32[]{:S(2)}, u32[]{:S(2)}) collective-permute-start(f16[1040,128]{1,0:T(8,128)(2,1)} %concatenate.82), channel_id=1, source_target_pairs={{0,16},{8,24},{16,32},{24,40},{32,48},{40,56},{48,0},{56,8},{64,80... | collective-permute-start | bytes 798728 | tf_op jit(solution)/shard_map/ppermute | solution.py:31
  90.1 30.7 %collective-permute-start.4 = (f16[1040,128]{1,0:T(8,128)(2,1)}, f16[1040,128]{1,0:T(8,128)(2,1)}, u32[]{:S(2)}, u32[]{:S(2)}) collective-permute-start(f16[1040,128]{1,0:T(8,128)(2,1)} %concatenate.84), channel_id=1, source_target_pairs={{0,48},{8,56},{16,0},{24,8},{32,16},{40,24},{48,32},{56,40},{64,11... | collective-permute-start | bytes 798728 | tf_op jit(solution)/shard_map/ppermute | solution.py:31
  93.3 29.3 %collective-permute-start.3 = (f16[1040,128]{1,0:T(8,128)(2,1)}, f16[1040,128]{1,0:T(8,128)(2,1)}, u32[]{:S(2)}, u32[]{:S(2)}) collective-permute-start(f16[1040,128]{1,0:T(8,128)(2,1)} %concatenate.83), channel_id=1, source_target_pairs={{0,32},{8,40},{16,48},{24,56},{32,0},{40,8},{48,16},{56,24},{64,96... | collective-permute-start | bytes 798728 | tf_op jit(solution)/shard_map/ppermute | solution.py:31
  96.5 29.8 %collective-permute-start.10 = (f16[1040,128]{1,0:T(8,128)(2,1)}, f16[1040,128]{1,0:T(8,128)(2,1)}, u32[]{:S(2)}, u32[]{:S(2)}) collective-permute-start(f16[1040,128]{1,0:T(8,128)(2,1)} %concatenate.90), channel_id=1, source_target_pairs={{0,192},{8,200},{16,208},{24,216},{32,224},{40,232},{48,240},{56,2... | collective-permute-start | bytes 798728 | tf_op jit(solution)/shard_map/ppermute | solution.py:31
  101.5 26.7 %collective-permute-start.9 = (f16[1040,128]{1,0:T(8,128)(2,1)}, f16[1040,128]{1,0:T(8,128)(2,1)S(1)}, u32[]{:S(2)}, u32[]{:S(2)}) collective-permute-start(f16[1040,128]{1,0:T(8,128)(2,1)} %concatenate.89), channel_id=1, source_target_pairs={{0,128},{8,136},{16,144},{24,152},{32,160},{40,168},{48,176},{56,1... | collective-permute-start | bytes 798728 | tf_op jit(solution)/shard_map/ppermute | solution.py:31
  102.0 22.5 %collective-permute-start.8 = (f16[1040,128]{1,0:T(8,128)(2,1)}, f16[1040,128]{1,0:T(8,128)(2,1)}, u32[]{:S(2)}, u32[]{:S(2)}) collective-permute-start(f16[1040,128]{1,0:T(8,128)(2,1)} %concatenate.88), channel_id=1, source_target_pairs={{0,64},{8,72},{16,80},{24,88},{32,96},{40,104},{48,112},{56,120},{... | collective-permute-start | bytes 798728 | tf_op jit(solution)/shard_map/ppermute | solution.py:31
  105.7 2.8 %copy-start.1 = (bf16[4,2048,384]{2,1,0:T(8,128)(2,1)S(1)}, bf16[4,2048,384]{2,1,0:T(8,128)(2,1)}, u32[]{:S(2)}) copy-start(bf16[4,2048,384]{2,1,0:T(8,128)(2,1)} %copy-done) | copy-start | bytes 18874372
  128.2 4.4 %copy-start.5 = (f16[1040,128]{1,0:T(8,128)(2,1)}, f16[1040,128]{1,0:T(8,128)(2,1)S(1)}, u32[]{:S(2)}) copy-start(f16[1040,128]{1,0:T(8,128)(2,1)S(1)} %collective-permute-done.9) | copy-start | bytes 798724
  134.5 10.2 %collective-permute-start.7 = (f16[272,128]{1,0:T(8,128)(2,1)}, f16[272,128]{1,0:T(8,128)(2,1)}, u32[]{:S(2)}, u32[]{:S(2)}) collective-permute-start(f16[272,128]{1,0:T(8,128)(2,1)} %concatenate.87), channel_id=1, source_target_pairs={{0,192},{8,200},{16,208},{24,216},{32,224},{40,232},{48,240},{56,2... | collective-permute-start | bytes 208904 | tf_op jit(solution)/shard_map/ppermute | solution.py:31
  137.2 9.8 %collective-permute-start.6 = (f16[272,128]{1,0:T(8,128)(2,1)}, f16[272,128]{1,0:T(8,128)(2,1)}, u32[]{:S(2)}, u32[]{:S(2)}) collective-permute-start(f16[272,128]{1,0:T(8,128)(2,1)} %concatenate.86), channel_id=1, source_target_pairs={{0,128},{8,136},{16,144},{24,152},{32,160},{40,168},{48,176},{56,1... | collective-permute-start | bytes 208904 | tf_op jit(solution)/shard_map/ppermute | solution.py:31
  139.1 13.5 %collective-permute-start.5 = (f16[272,128]{1,0:T(8,128)(2,1)}, f16[272,128]{1,0:T(8,128)(2,1)}, u32[]{:S(2)}, u32[]{:S(2)}) collective-permute-start(f16[272,128]{1,0:T(8,128)(2,1)} %concatenate.85), channel_id=1, source_target_pairs={{0,64},{8,72},{16,80},{24,88},{32,96},{40,104},{48,112},{56,120},{... | collective-permute-start | bytes 208904 | tf_op jit(solution)/shard_map/ppermute | solution.py:31
  142.5 12.0 %collective-permute-start.13 = (f16[272,128]{1,0:T(8,128)(2,1)S(1)}, f16[272,128]{1,0:T(8,128)(2,1)S(1)}, u32[]{:S(2)}, u32[]{:S(2)}) collective-permute-start(f16[272,128]{1,0:T(8,128)(2,1)S(1)} %concatenate.93), channel_id=1, source_target_pairs={{0,48},{8,56},{16,0},{24,8},{32,16},{40,24},{48,32},{56,40},{64,11... | collective-permute-start | bytes 208904 | tf_op jit(solution)/shard_map/ppermute | solution.py:31
  143.5 12.3 %collective-permute-start.12 = (f16[272,128]{1,0:T(8,128)(2,1)S(1)}, f16[272,128]{1,0:T(8,128)(2,1)S(1)}, u32[]{:S(2)}, u32[]{:S(2)}) collective-permute-start(f16[272,128]{1,0:T(8,128)(2,1)S(1)} %concatenate.92), channel_id=1, source_target_pairs={{0,32},{8,40},{16,48},{24,56},{32,0},{40,8},{48,16},{56,24},{64,96... | collective-permute-start | bytes 208904 | tf_op jit(solution)/shard_map/ppermute | solution.py:31
  144.8 12.2 %collective-permute-start.11 = (f16[272,128]{1,0:T(8,128)(2,1)S(1)}, f16[272,128]{1,0:T(8,128)(2,1)S(1)}, u32[]{:S(2)}, u32[]{:S(2)}) collective-permute-start(f16[272,128]{1,0:T(8,128)(2,1)S(1)} %concatenate.91), channel_id=1, source_target_pairs={{0,16},{8,24},{16,32},{24,40},{32,48},{40,56},{48,0},{56,8},{64,80... | collective-permute-start | bytes 208904 | tf_op jit(solution)/shard_map/ppermute | solution.py:31
  147.0 16.3 %collective-permute-start.29 = (f32[27,32,128]{2,1,0:T(8,128)S(1)}, f32[27,32,128]{2,1,0:T(8,128)S(1)}, u32[]{:S(2)}, u32[]{:S(2)}) collective-permute-start(f32[27,32,128]{2,1,0:T(8,128)S(1)} %constant_dynamic-slice_fusion), channel_id=1, source_target_pairs={{0,8},{8,0},{16,24},{24,16},{32,40},{40,32},{48,56},{56,48},{64,72... | collective-permute-start | bytes 1327112 | tf_op jit(solution)/shard_map/ppermute | solution.py:31
  161.0 1.4 collective-permute-start.14
Sparse Core Ops, SparseCore 0:
  9.8 38.1 all-gather.1
  105.9 35.3 reduce-scatter.1

commit v2 on v1

v2 whole, which is shorter than its diff:
```python
import functools
import math

import jax
import jax.numpy as jnp
from jax import lax
from jax.experimental import pallas as pl
from jax.experimental.pallas import tpu as pltpu
from jax.sharding import PartitionSpec as P

SX = 16
SY = 16
SZ = 8
PLANE = SY * SZ
SIDE = 4
BF16 = jnp.bfloat16
F16 = jnp.float16
F32 = jnp.float32

in_plane = [(b, c) for b in (-1, 0, 1) for c in (-1, 0, 1)]
VMEM_LIMIT = 24 * 1024 * 1024
NOTE = 16
TINY = 1e-32


def move_xy(value, dy, dx, flip=0):
    pairs = []
    for y in range(SIDE):
        for x in range(SIDE):
            for core in range(2):
                target = ((y + dy) % SIDE * SIDE + (x + dx) % SIDE) * 2 + (core ^ flip)
                pairs.append(((y * SIDE + x) * 2 + core, target))
    return lax.ppermute(value, "cin", pairs)


def swap_cores(value):
    return move_xy(value, 0, 0, 1)


def plane_mask(rows, b, c):
    lane = lax.broadcasted_iota(jnp.int32, (rows, PLANE), 1)
    y = (lane >> 3) + b
    z = (lane & 7) + c
    return (y >= 0) & (y < SY) & (z >= 0) & (z < SZ)


def dgrad_kernel(place, *refs):
    half_a, half_b = refs[0:4], refs[4:8]
    wd_ref, taps_ref, own_ref, other_ref = refs[8:12]
    ci = own_ref.shape[1]
    co = taps_ref.shape[2] // 3
    n = pl.program_id(0)
    my_y, my_x, core = place[0], place[1], place[2]

    def fill(parts, y_first):
        for first in range(SIDE):
            for second in range(SIDE):
                step_y, step_x = (first, second) if y_first else (second, first)
                y = lax.rem(my_y - step_y + SIDE, SIDE)
                x = lax.rem(my_x - step_x + SIDE, SIDE)
                p = y * SIDE + x
                cells = parts[first][second, lax.rem(n, 2)]

                def put(q, column):
                    row = pl.multiple_of(q * PLANE, PLANE)
                    taps_ref[0, pl.ds(row, PLANE), column * co : (column + 1) * co] = cells

                put(p, 1)
                pl.when(p > 0)(lambda: put(p - 1, 0))
                pl.when(p < SX - 1)(lambda: put(p + 1, 2))

    taps_ref[0, (SX - 1) * PLANE :, 0:co] = jnp.zeros((PLANE, co), BF16)
    taps_ref[0, 0:PLANE, 2 * co :] = jnp.zeros((PLANE, co), BF16)
    pl.when(n < 2)(lambda: fill(half_a, True))
    pl.when(n >= 2)(lambda: fill(half_b, False))

    wd = wd_ref[...]
    masks = [plane_mask(2 * ci, -b, -c) for b, c in in_plane]
    step = 4
    for first in range(0, SX, step):
        rows = taps_ref[0, first * PLANE : (first + step) * PLANE, :]
        product = lax.dot_general(wd, rows, (((1,), (1,)), ((), ())), preferred_element_type=F32)
        for j in range(step):
            total = None
            for index, (b, c) in enumerate(in_plane):
                term = product[index * 2 * ci : (index + 1) * 2 * ci, j * PLANE : (j + 1) * PLANE]
                shift = (b * SZ + c) % PLANE
                if shift:
                    term = jnp.where(masks[index], pltpu.roll(term, shift, 1), 0.0)
                total = term if total is None else total + term
            lanes = slice((first + j) * PLANE, (first + j + 1) * PLANE)
            low, high = total[:ci], total[ci:]
            own_ref[0, :, lanes] = jnp.where(core == 0, low, high)
            other_ref[0, :, lanes] = jnp.where(core == 0, high, low)


def fwd_kernel(place, own_ref, other_ref, wa_ref, cols_ref, msg_a, msg_b, own_a, own_b, stage, sums):
    ci = own_ref.shape[1]
    co = wa_ref.shape[0] // 3
    n = pl.program_id(0)
    my_y, my_x, core = place[0], place[1], place[2]
    masks = [plane_mask(2 * ci, b, c) for b, c in in_plane]

    @pl.when(n == 0)
    def _():
        stage[0] = jnp.zeros(stage.shape[1:], F32)
        stage[SX + 1] = jnp.zeros(stage.shape[1:], F32)

    for p in range(SX):
        lanes = slice(p * PLANE, (p + 1) * PLANE)
        mine = own_ref[0, :, lanes].astype(F32)
        got = other_ref[0, :, lanes].astype(F32)
        cells = jnp.concatenate([jnp.where(core == 0, mine, got), jnp.where(core == 0, got, mine)], axis=0)
        for index, (b, c) in enumerate(in_plane):
            shift = -(b * SZ + c) % PLANE
            term = cells
            if shift:
                term = jnp.where(masks[index], pltpu.roll(term, shift, 1), 0.0)
            cols_ref[0, index * 2 * ci : (index + 1) * 2 * ci, lanes] = term.astype(BF16)

    step = 4
    for first in range(0, SX, step):
        lanes = slice(first * PLANE, (first + step) * PLANE)
        product = jnp.dot(wa_ref[...], cols_ref[0, :, lanes], preferred_element_type=F32)
        for j in range(step):
            stage[first + j + 1] = product[:, j * PLANE : (j + 1) * PLANE]

    peak = jnp.zeros((co, PLANE), F32)
    for p in range(SX):
        total = stage[p, 0:co] + stage[p + 1, co : 2 * co] + stage[p + 2, 2 * co :]
        sums[p] = total
        peak = jnp.maximum(peak, jnp.abs(total))
    peak = jnp.full((NOTE, PLANE), jnp.maximum(jnp.max(peak), TINY), F32)
    power = 14.0 - jnp.ceil(jnp.log2(peak))
    factor = jnp.exp2(power[0:1])
    rows = SIDE * co
    at = lax.rem(n, 2)

    def send(msg, own, y_first):
        for first in range(SIDE):
            if first == 0:
                own[at, rows:] = power
            else:
                msg[first - 1, at, rows:] = power
            for second in range(SIDE):
                step_y, step_x = (first, second) if y_first else (second, first)
                y = lax.rem(my_y + step_y, SIDE)
                x = lax.rem(my_x + step_x, SIDE)
                total = sums[y * SIDE + x]
                if first == 0:
                    own[at, second * co : (second + 1) * co] = total
                else:
                    msg[first - 1, at, second * co : (second + 1) * co] = total * factor

    pl.when(n < 2)(lambda: send(msg_a, own_a, False))
    pl.when(n >= 2)(lambda: send(msg_b, own_b, True))


def arrived(own, messages, rows):
    total, least = own[:, :rows], own[:, rows:]
    for message in messages:
        power = message[:, rows:]
        total = total + message[:, :rows] * jnp.exp2(-power[:, 0:1])
        least = jnp.minimum(least, power)
    return total, least


def turn_kernel(*refs):
    ins, outs = refs[:8], refs[8:]
    for half in range(2):
        own, messages = ins[4 * half], ins[4 * half + 1 : 4 * half + 4]
        msg, mine = outs[2 * half : 2 * half + 2]
        rows = own.shape[1] - NOTE
        size = rows // SIDE
        total, least = arrived(own[...], [m[...] for m in messages], rows)
        power = least - 2.0
        mine[:, :size] = total[:, :size]
        mine[:, size:] = power
        for step in range(1, SIDE):
            msg[step - 1, :, :size] = total[:, step * size : (step + 1) * size] * jnp.exp2(power[:, 0:1])
            msg[step - 1, :, size:] = power


def last_kernel(place, *refs):
    ins, own_ref, other_ref = refs[:8], refs[8], refs[9]
    part = PLANE // 2
    for half in range(2):
        own, messages = ins[4 * half], ins[4 * half + 1 : 4 * half + 4]
        rows = own.shape[1] - NOTE
        total, _ = arrived(own[...], [m[...] for m in messages], rows)
        for at in range(total.shape[0]):
            cells = total[at].T.astype(BF16)
            low, high = cells[:part], cells[part:]
            own_ref[half * total.shape[0] + at] = jnp.where(place[2] == 0, low, high)
            other_ref[half * total.shape[0] + at] = jnp.where(place[2] == 0, high, low)


def wgrad_kernel(place, cols_ref, taps_ref, own_ref, other_ref, acc):
    ci, co = own_ref.shape[1:]
    n = pl.program_id(0)

    @pl.when(n == 0)
    def _():
        acc[...] = jnp.zeros_like(acc)

    acc[...] += jnp.dot(cols_ref[0], taps_ref[0], preferred_element_type=F32)

    @pl.when(n == pl.num_programs(0) - 1)
    def _():
        for tap in range(27):
            first, column = tap % 9 * 2 * ci, tap // 9 * co
            low = acc[first : first + ci, column : column + co]
            high = acc[first + ci : first + 2 * ci, column : column + co]
            own_ref[tap] = jnp.where(place[2] == 0, low, high)
            other_ref[tap] = jnp.where(place[2] == 0, high, low)


def whole(shape):
    return pl.BlockSpec(shape, lambda *_: (0,) * len(shape))


def per_sample(shape):
    return pl.BlockSpec((1,) + shape, lambda n, *_: (n,) + (0,) * len(shape))


def body(inputs, weight, grad_out):
    ci, co = weight.shape[1], weight.shape[2]
    where_cin = lax.axis_index("cin")
    core = where_cin % 2
    place = jnp.stack([where_cin // 2 // SIDE, where_cin // 2 % SIDE, core]).astype(jnp.int32)
    batch = grad_out.shape[0]
    mine = batch // 2
    pairs = mine // 2
    first_core = core == 0

    def taken(value, which, size, axis):
        return lax.dynamic_slice_in_dim(value, which * size, size, axis)

    def in_order(own, other, axis):
        return jnp.where(
            first_core,
            jnp.concatenate([own, other], axis),
            jnp.concatenate([other, own], axis),
        )

    gathered = lax.all_gather(inputs, "cout", axis=0, tiled=True)

    cotangent = jnp.transpose(grad_out, (0, 2, 1))
    got = swap_cores(taken(cotangent, 1 - core, mine, 0))
    plane = in_order(taken(cotangent, core, mine, 0), got, 1)
    along_x = [functools.partial(move_xy, dy=0, dx=s) for s in (1, 2, 3)]
    along_y = [functools.partial(move_xy, dy=s, dx=0) for s in (1, 2, 3)]

    def gather_stage(value, moves):
        return [value] + [move(value) for move in moves]

    near_a, near_b = lax.optimization_barrier(
        (gather_stage(plane[:pairs], along_x), gather_stage(plane[pairs:], along_y))
    )
    row_a, row_b = lax.optimization_barrier((jnp.stack(near_a), jnp.stack(near_b)))
    parts = gather_stage(row_a, along_y) + gather_stage(row_b, along_x)

    sample = swap_cores(taken(gathered, 1 - core, mine, 0))

    pair = in_order(weight, swap_cores(weight), 1)
    wd = jnp.transpose(pair.reshape(3, 9, 2 * ci, co), (1, 2, 0, 3)).reshape(9 * 2 * ci, 3 * co)
    wa = wd.T

    cells = inputs.shape[2]
    params = pltpu.CompilerParams(vmem_limit_bytes=VMEM_LIMIT)
    taps, terms, other = pl.pallas_call(
        dgrad_kernel,
        grid_spec=pltpu.PrefetchScalarGridSpec(
            num_scalar_prefetch=1,
            grid=(mine,),
            in_specs=[whole(p.shape) for p in parts] + [whole(wd.shape)],
            out_specs=[
                per_sample((cells, 3 * co)),
                pl.BlockSpec((1, ci, cells), lambda n, place: (place[2] * mine + n, 0, 0)),
                per_sample((ci, cells)),
            ],
        ),
        out_shape=[
            pltpu.HBM((mine, cells, 3 * co), BF16),
            pltpu.HBM((batch, ci, cells), F32),
            pltpu.HBM((mine, ci, cells), F32),
        ],
        compiler_params=params,
        name="dgrad",
    )(place, *parts, wd)
    taps = pltpu.with_memory_space_constraint(taps, pltpu.HBM)

    terms = lax.dynamic_update_slice_in_dim(terms, swap_cores(other), (1 - core) * mine, 0)
    grad_input = lax.psum_scatter(terms, "cout", scatter_dimension=0, tiled=True).astype(BF16)

    rows = SIDE * co + NOTE
    sent = jax.ShapeDtypeStruct((SIDE - 1, pairs, rows, PLANE), F32)
    kept = jax.ShapeDtypeStruct((pairs, rows, PLANE), F32)
    columns, msg_a, msg_b, own_a, own_b = pl.pallas_call(
        fwd_kernel,
        grid_spec=pltpu.PrefetchScalarGridSpec(
            num_scalar_prefetch=1,
            grid=(mine,),
            in_specs=[
                pl.BlockSpec((1, ci, cells), lambda n, place: (place[2] * mine + n, 0, 0)),
                per_sample((ci, cells)),
                whole(wa.shape),
            ],
            out_specs=[per_sample((9 * 2 * ci, cells))] + [whole(o.shape) for o in (sent, sent, kept, kept)],
            scratch_shapes=[pltpu.VMEM((SX + 2, 3 * co, PLANE), F32), pltpu.VMEM((SX, co, PLANE), F32)],
        ),
        out_shape=[pltpu.HBM((mine, 9 * 2 * ci, cells), BF16), sent, sent, kept, kept],
        compiler_params=params,
        name="forward",
    )(place, gathered, sample, wa)
    columns = pltpu.with_memory_space_constraint(columns, pltpu.HBM)

    def reduce_stage(msg, moves):
        return [move(msg[i].astype(F16)).astype(F32) for i, move in enumerate(moves)]

    rows = co + NOTE
    sent = jax.ShapeDtypeStruct((SIDE - 1, pairs, rows, PLANE), F32)
    kept = jax.ShapeDtypeStruct((pairs, rows, PLANE), F32)
    msg_a, own_a, msg_b, own_b = pl.pallas_call(
        turn_kernel, out_shape=[sent, kept, sent, kept], compiler_params=params, name="turn"
    )(own_a, *reduce_stage(msg_a, along_x), own_b, *reduce_stage(msg_b, along_y))
    ends = [own_a, *reduce_stage(msg_a, along_y), own_b, *reduce_stage(msg_b, along_x)]
    own, other = pl.pallas_call(
        last_kernel,
        grid_spec=pltpu.PrefetchScalarGridSpec(
            num_scalar_prefetch=1,
            grid=(1,),
            in_specs=[whole(e.shape) for e in ends],
            out_specs=[whole((mine, PLANE // 2, co))] * 2,
        ),
        out_shape=[jax.ShapeDtypeStruct((mine, PLANE // 2, co), BF16)] * 2,
        compiler_params=params,
        name="last",
    )(place, *ends)
    output = jnp.transpose(in_order(own, swap_cores(other), 0), (0, 2, 1))

    own, other = pl.pallas_call(
        wgrad_kernel,
        grid_spec=pltpu.PrefetchScalarGridSpec(
            num_scalar_prefetch=1,
            grid=(mine,),
            in_specs=[per_sample((9 * 2 * ci, cells)), per_sample((cells, 3 * co))],
            out_specs=[whole((27, ci, co))] * 2,
            scratch_shapes=[pltpu.VMEM((9 * 2 * ci, 3 * co), F32)],
        ),
        out_shape=[jax.ShapeDtypeStruct((27, ci, co), F32)] * 2,
        compiler_params=params,
        name="wgrad",
    )(place, columns, taps)
    grad_weight = (own + swap_cores(other)) / math.sqrt(batch * cells)
    return output, grad_input, grad_weight


def solution(mesh):
    placed = (P("cout", "cin", None), P(None, "cin", "cout"), P(None, "cout", "cin"))
    return jax.shard_map(
        body,
        mesh=mesh,
        in_specs=placed,
        out_specs=(P(None, "cout", "cin"), P("cout", "cin", None), P(None, "cin", "cout")),
        check_vma=False,
    )
```

time: 174 us -> 124 us (0.71)
  local copies, waits for them, and re-layouts: 38.6 us -> 4.23 us
  other arithmetic: 21.3 us -> 4.3 us
  between operations: 23.7 us -> 14.4 us
  starting transfers between devices: 40 us -> 44.2 us
  Pallas kernels: 27 us -> 30.3 us
  waiting for transfers between devices: 22 us -> 24.2 us
    ppermute x30, waiting for transfers between devices: 8.83 us -> 24.2 us  [move_xy(): return lax.ppermute(value, 'cin', pairs)]
    all_gather x1, waiting for transfers between devices: 12.5 us -> 0.02 us  [body(): gathered = lax.all_gather(inputs, 'cout', axis=0, tiled=True)]
    slice x12 -> x1, local copies, waits for them, and re-layouts: 11.7 us -> 0.01 us  [body(): plane[pairs:]]
    concatenate x12 -> x0, local copies, waits for them, and re-layouts: 10.4 us -> none  [coded(): return jnp.concatenate([rows, note], axis=0)]
    mul x12 -> x0, other arithmetic: 8.55 us -> none  [decoded(): return (message[:-16].astype(F32).reshape(shape) * jnp.exp2(-power), power)]
    unnamed x14 -> x5, local copies, waits for them, and re-layouts: 7.56 us -> 0.08 us
    select_n x4 -> x2, other arithmetic: 5.17 us -> 0.46 us  [in_order(): jnp.where(first_core, jnp.concatenate([own, other], axis), jnp.concatenat...]
    ppermute x30, starting transfers between devices: 40 us -> 44.2 us  [move_xy(): return lax.ppermute(value, 'cin', pairs)]
  transfers between devices with their start and end apart: 32 -> 32, of which waited for: 9 -> 15; matrix products, arithmetic and copies ran while one was open for 30% -> 5% of each run, Pallas kernels for 16% -> 25%
where the time goes in v2:
time: 124 us; the launch traced here: 122 us
  starting transfers between devices  44.2 us (36%)
  Pallas kernels  30.3 us (24%)
  waiting for transfers between devices  24.2 us (20%)
  between operations  14.4 us (12%)
  other arithmetic  4.3 us (3%)
  local copies, waits for them, and re-layouts  4.23 us (3%)
    ppermute x30, starting transfers between devices, move_xy(): return lax.ppermute(value, 'cin', pairs)  44.2 us
    ppermute x30, waiting for transfers between devices, move_xy(): return lax.ppermute(value, 'cin', pairs)  24.2 us
    pallas_call x1, Pallas kernels, body(): pl.pallas_call(fwd_kernel, grid_spec=pltpu.PrefetchScalarGridSpec(num_sca...  10 us
    pallas_call x1, Pallas kernels, body(): pl.pallas_call(dgrad_kernel, grid_spec=pltpu.PrefetchScalarGridSpec(num_s...  9.99 us
    pallas_call x1, Pallas kernels, body(): pl.pallas_call(wgrad_kernel, grid_spec=pltpu.PrefetchScalarGridSpec(num_s...  9.38 us
  transfers between devices with their start and end apart: 32, of which 15 were waited for; matrix products, arithmetic and copies ran while one was open for 5% of the time, Pallas kernels for 25%

profile of v2, /device:TPU:1, one launch (start us, length us, event | category | flops | bytes accessed | tf_op | source)
XLA Modules:
  0.0 121.8 jit_solution(9697999395463594827)
XLA Ops:
  7.2 0.9 dynamic-slice_bitcast_fusion.1
  8.2 3.3 %collective-permute-start.15 = (bf16[4,64,128]{2,1,0:T(8,128)(2,1)S(1)}, bf16[4,64,128]{2,1,0:T(8,128)(2,1)S(1)}, u32[]{:S(2)}, u32[]{:S(2)}) collective-permute-start(bf16[4,64,128]{2,1,0:T(8,128)(2,1)S(1)} %get-tuple-element.70), channel_id=1, source_target_pairs={{0,8},{8,0},{16,24},{24,16},{32,40},{40,32},{48,56},{56,48},{64,72... | collective-permute-start | bytes 196616 | tf_op jit(solution)/shard_map/ppermute | solution.py:33
  11.5 0.9 collective-permute-done.15
  12.5 1.9 %collective-permute-start.17 = (bf16[2,128,128]{2,1,0:T(8,128)(2,1)S(1)}, bf16[2,128,128]{2,1,0:T(8,128)(2,1)S(1)}, u32[]{:S(2)}, u32[]{:S(2)}) collective-permute-start(bf16[2,128,128]{2,1,0:T(8,128)(2,1)S(1)} %get-tuple-element.39), channel_id=1, source_target_pairs={{0,32},{8,40},{16,48},{24,56},{32,0},{40,8},{48,16},{56,24},{64,96... | collective-permute-start | bytes 196616 | tf_op jit(solution)/shard_map/ppermute | solution.py:33
  14.5 1.2 collective-permute-start.18
  15.6 1.3 %collective-permute-start.19 = (bf16[2,128,128]{2,1,0:T(8,128)(2,1)S(1)}, bf16[2,128,128]{2,1,0:T(8,128)(2,1)S(1)}, u32[]{:S(2)}, u32[]{:S(2)}) collective-permute-start(bf16[2,128,128]{2,1,0:T(8,128)(2,1)S(1)} %get-tuple-element.43), channel_id=1, source_target_pairs={{0,64},{8,72},{16,80},{24,88},{32,96},{40,104},{48,112},{56,120},{... | collective-permute-start | bytes 196616 | tf_op jit(solution)/shard_map/ppermute | solution.py:33
  16.9 2.6 %collective-permute-start.20 = (bf16[2,128,128]{2,1,0:T(8,128)(2,1)S(1)}, bf16[2,128,128]{2,1,0:T(8,128)(2,1)S(1)}, u32[]{:S(2)}, u32[]{:S(2)}) collective-permute-start(bf16[2,128,128]{2,1,0:T(8,128)(2,1)S(1)} %get-tuple-element.43), channel_id=1, source_target_pairs={{0,128},{8,136},{16,144},{24,152},{32,160},{40,168},{48,176},{56,1... | collective-permute-start | bytes 196616 | tf_op jit(solution)/shard_map/ppermute | solution.py:33
  19.5 1.1 collective-permute-start.21
  20.7 1.3 %collective-permute-done.20 = bf16[2,128,128]{2,1,0:T(8,128)(2,1)S(1)} collective-permute-done((bf16[2,128,128]{2,1,0:T(8,128)(2,1)S(1)}, bf16[2,128,128]{2,1,0:T(8,128)(2,1)S(1)}, u32[]{:S(2)}, u32[]{:S(2)}) %collective-permute-start.20) | collective-permute-done | bytes 65568 | tf_op jit(solution)/shard_map/ppermute | solution.py:33
  22.0 1.5 %collective-permute-done.21 = bf16[2,128,128]{2,1,0:T(8,128)(2,1)S(1)} collective-permute-done((bf16[2,128,128]{2,1,0:T(8,128)(2,1)S(1)}, bf16[2,128,128]{2,1,0:T(8,128)(2,1)S(1)}, u32[]{:S(2)}, u32[]{:S(2)}) %collective-permute-start.21) | collective-permute-done | bytes 65568 | tf_op jit(solution)/shard_map/ppermute | solution.py:33
  23.6 2.4 %collective-permute-start.1 = (bf16[27,32,128]{2,1,0:T(8,128)(2,1)}, bf16[27,32,128]{2,1,0:T(8,128)(2,1)S(1)}, u32[]{:S(2)}, u32[]{:S(2)}) collective-permute-start(bf16[27,32,128]{2,1,0:T(8,128)(2,1)} %param.4), channel_id=1, source_target_pairs={{0,8},{8,0},{16,24},{24,16},{32,40},{40,32},{48,56},{56,48},{64,72... | collective-permute-start | bytes 663560 | tf_op jit(solution)/shard_map/ppermute | solution.py:33
  26.0 3.4 %collective-permute-start.23 = (bf16[4,2,128,128]{3,2,1,0:T(8,128)(2,1)S(1)}, bf16[4,2,128,128]{3,2,1,0:T(8,128)(2,1)S(1)}, u32[]{:S(2)}, u32[]{:S(2)}) collective-permute-start(bf16[4,2,128,128]{3,2,1,0:T(8,128)(2,1)S(1)} %get-tuple-element.47.refs_0_), channel_id=1, source_target_pairs={{0,128},{8,136},{16,144},{24,152},{32,160},{40,168},{48,176},{56,1... | collective-permute-start | bytes 786440 | tf_op jit(solution)/shard_map/ppermute | solution.py:33
  29.8 0.6 collective-permute-start.26
  30.5 1.9 %collective-permute-start.27 = (bf16[4,2,128,128]{3,2,1,0:T(8,128)(2,1)S(1)}, bf16[4,2,128,128]{3,2,1,0:T(8,128)(2,1)S(1)}, u32[]{:S(2)}, u32[]{:S(2)}) collective-permute-start(bf16[4,2,128,128]{3,2,1,0:T(8,128)(2,1)S(1)} %get-tuple-element.48.refs_4_), channel_id=1, source_target_pairs={{0,48},{8,56},{16,0},{24,8},{32,16},{40,24},{48,32},{56,40},{64,11... | collective-permute-start | bytes 786440 | tf_op jit(solution)/shard_map/ppermute | solution.py:33
  33.3 3.4 %collective-permute-done.23.refs_2_ = bf16[4,2,128,128]{3,2,1,0:T(8,128)(2,1)S(1)} collective-permute-done((bf16[4,2,128,128]{3,2,1,0:T(8,128)(2,1)S(1)}, bf16[4,2,128,128]{3,2,1,0:T(8,128)(2,1)S(1)}, u32[]{:S(2)}, u32[]{:S(2)}) %collective-permute-start.23) | collective-permute-done | bytes 262176 | tf_op jit(solution)/shard_map/ppermute | solution.py:33
  36.7 4.6 %collective-permute-done.24.refs_3_ = bf16[4,2,128,128]{3,2,1,0:T(8,128)(2,1)S(1)} collective-permute-done((bf16[4,2,128,128]{3,2,1,0:T(8,128)(2,1)S(1)}, bf16[4,2,128,128]{3,2,1,0:T(8,128)(2,1)S(1)}, u32[]{:S(2)}, u32[]{:S(2)}) %collective-permute-start.24) | collective-permute-done | bytes 262176 | tf_op jit(solution)/shard_map/ppermute | solution.py:33
  41.4 2.4 %collective-permute-done.25.refs_5_ = bf16[4,2,128,128]{3,2,1,0:T(8,128)(2,1)S(1)} collective-permute-done((bf16[4,2,128,128]{3,2,1,0:T(8,128)(2,1)S(1)}, bf16[4,2,128,128]{3,2,1,0:T(8,128)(2,1)S(1)}, u32[]{:S(2)}, u32[]{:S(2)}) %collective-permute-start.25) | collective-permute-done | bytes 262176 | tf_op jit(solution)/shard_map/ppermute | solution.py:33
  44.2 10.0 %dgrad.1 = (bf16[4,2048,384]{2,1,0:T(8,128)(2,1)}, f32[8,32,2048]{2,1,0:T(8,128)}, f32[4,32,2048]{2,1,0:T(8,128)}) custom-call(s32[3]{0:T(128)S(1)} %pad_add_fusion.place, bf16[4,2,128,128]{3,2,1,0:T(8,128)(2,1)S(1)} %get-tuple-element.47.refs_0_, bf16[4,2,128,128]{3,2,1,0:T(8,128)(2,1)S(1)} %collective-permute-done.22.refs_1_, ...), custom_call_target="tpu_custom_call" | custom-call | tf_op jit(solution)/shard_map/dgrad/pallas_call | solution.py:271
  54.2 1.5 %collective-permute-start.28 = (f32[4,32,2048]{2,1,0:T(8,128)}, f32[4,32,2048]{2,1,0:T(8,128)S(1)}, u32[]{:S(2)}, u32[]{:S(2)}) collective-permute-start(f32[4,32,2048]{2,1,0:T(8,128)} %get-tuple-element.50), channel_id=1, source_target_pairs={{0,8},{8,0},{16,24},{24,16},{32,40},{40,32},{48,56},{56,48},{64,72... | collective-permute-start | bytes 3145736 | tf_op jit(solution)/shard_map/ppermute | solution.py:33
  55.7 2.5 %collective-permute-done.28 = f32[4,32,2048]{2,1,0:T(8,128)S(1)} collective-permute-done((f32[4,32,2048]{2,1,0:T(8,128)}, f32[4,32,2048]{2,1,0:T(8,128)S(1)}, u32[]{:S(2)}, u32[]{:S(2)}) %collective-permute-start.28) | collective-permute-done | bytes 1048608 | tf_op jit(solution)/shard_map/ppermute | solution.py:33
  58.2 1.1 constant_dynamic-update-slice_fusion
  59.3 1.2 constant_dynamic-slice_fusion
  60.4 0.5 collective-permute-start
  61.2 1.3 %collective-permute-done.other_ref = bf16[4,32,2048]{2,1,0:T(8,128)(2,1)S(1)} collective-permute-done((bf16[4,32,2048]{2,1,0:T(8,128)(2,1)S(1)}, bf16[4,32,2048]{2,1,0:T(8,128)(2,1)S(1)}, u32[]{:S(2)}, u32[]{:S(2)}) %collective-permute-start) | collective-permute-done | bytes 524320 | tf_op jit(solution)/shard_map/ppermute | solution.py:33
  62.5 10.0 %forward.1 = (bf16[4,576,2048]{2,1,0:T(8,128)(2,1)}, f32[3,2,528,128]{3,2,1,0:T(8,128)S(1)}, f32[3,2,528,128]{3,2,1,0:T(8,128)S(1)}, f32[2,528,128]{2,1,0:T(8,128)S(1)}, f32[2,528,128]{2,1,0:T(8,128)S(1)}) custom-call(s32[3]{0:T(128)S(1)} %pad_add_fusion.place, bf16[8,32,2048]{2,1,0:T(8,128)(2,1)S(1)} %copy-done, ...), custom_call_target="tpu_custom_call" | custom-call | tf_op jit(solution)/shard_map/forward/pallas_call | solution.py:299
  72.8 1.0 collective-permute-start.2
  73.8 2.6 %collective-permute-start.3 = (f16[2,528,128]{2,1,0:T(8,128)(2,1)S(1)}, f16[2,528,128]{2,1,0:T(8,128)(2,1)S(1)}, u32[]{:S(2)}, u32[]{:S(2)}) collective-permute-start(f16[2,528,128]{2,1,0:T(8,128)(2,1)S(1)} %get-tuple-element.59), channel_id=1, source_target_pairs={{0,32},{8,40},{16,48},{24,56},{32,0},{40,8},{48,16},{56,24},{64,96... | collective-permute-start | bytes 811016 | tf_op jit(solution)/shard_map/ppermute | solution.py:33
  76.3 1.0 collective-permute-start.4
  77.6 1.3 %collective-permute-start.5 = (f16[2,528,128]{2,1,0:T(8,128)(2,1)S(1)}, f16[2,528,128]{2,1,0:T(8,128)(2,1)S(1)}, u32[]{:S(2)}, u32[]{:S(2)}) collective-permute-start(f16[2,528,128]{2,1,0:T(8,128)(2,1)S(1)} %get-tuple-element.57), channel_id=1, source_target_pairs={{0,64},{8,72},{16,80},{24,88},{32,96},{40,104},{48,112},{56,120},{... | collective-permute-start | bytes 811016 | tf_op jit(solution)/shard_map/ppermute | solution.py:33
  78.9 2.4 %collective-permute-start.6 = (f16[2,528,128]{2,1,0:T(8,128)(2,1)S(1)}, f16[2,528,128]{2,1,0:T(8,128)(2,1)S(1)}, u32[]{:S(2)}, u32[]{:S(2)}) collective-permute-start(f16[2,528,128]{2,1,0:T(8,128)(2,1)S(1)} %get-tuple-element.56), channel_id=1, source_target_pairs={{0,128},{8,136},{16,144},{24,152},{32,160},{40,168},{48,176},{56,1... | collective-permute-start | bytes 811016 | tf_op jit(solution)/shard_map/ppermute | solution.py:33
  81.3 0.5 collective-permute-done.2
  81.8 2.2 %collective-permute-start.7 = (f16[2,528,128]{2,1,0:T(8,128)(2,1)S(1)}, f16[2,528,128]{2,1,0:T(8,128)(2,1)S(1)}, u32[]{:S(2)}, u32[]{:S(2)}) collective-permute-start(f16[2,528,128]{2,1,0:T(8,128)(2,1)S(1)} %get-tuple-element.55), channel_id=1, source_target_pairs={{0,192},{8,200},{16,208},{24,216},{32,224},{40,232},{48,240},{56,2... | collective-permute-start | bytes 811016 | tf_op jit(solution)/shard_map/ppermute | solution.py:33
  84.0 9.4 %wgrad.1 = (f32[27,32,128]{2,1,0:T(8,128)S(1)}, f32[27,32,128]{2,1,0:T(8,128)S(1)}) custom-call(s32[3]{0:T(128)S(1)} %pad_add_fusion.place, bf16[4,576,2048]{2,1,0:T(8,128)(2,1)} %get-tuple-element.51.cols_ref, bf16[4,2048,384]{2,1,0:T(8,128)(2,1)} %get-tuple-element.52.taps_ref), custom_call_target="tpu_custom_call" | custom-call | tf_op jit(solution)/shard_map/wgrad/pallas_call | solution.py:342
  93.5 1.4 %collective-permute-start.29 = (f32[27,32,128]{2,1,0:T(8,128)S(1)}, f32[27,32,128]{2,1,0:T(8,128)S(1)}, u32[]{:S(2)}, u32[]{:S(2)}) collective-permute-start(f32[27,32,128]{2,1,0:T(8,128)S(1)} %get-tuple-element.54), channel_id=1, source_target_pairs={{0,8},{8,0},{16,24},{24,16},{32,40},{40,32},{48,56},{56,48},{64,72... | collective-permute-start | bytes 1327112 | tf_op jit(solution)/shard_map/ppermute | solution.py:33
  95.5 0.9 collective-permute-start.8
  96.4 0.9 collective-permute-start.9
  97.3 1.6 %collective-permute-start.10 = (f16[2,144,128]{2,1,0:T(8,128)(2,1)S(1)}, f16[2,144,128]{2,1,0:T(8,128)(2,1)S(1)}, u32[]{:S(2)}, u32[]{:S(2)}) collective-permute-start(f16[2,144,128]{2,1,0:T(8,128)(2,1)S(1)} %get-tuple-element.64), channel_id=1, source_target_pairs={{0,192},{8,200},{16,208},{24,216},{32,224},{40,232},{48,240},{56,2... | collective-permute-start | bytes 221192 | tf_op jit(solution)/shard_map/ppermute | solution.py:33
  99.3 1.4 %collective-permute-done.8 = f16[2,144,128]{2,1,0:T(8,128)(2,1)S(1)} collective-permute-done((f16[2,144,128]{2,1,0:T(8,128)(2,1)S(1)}, f16[2,144,128]{2,1,0:T(8,128)(2,1)S(1)}, u32[]{:S(2)}, u32[]{:S(2)}) %collective-permute-start.8) | collective-permute-done | bytes 73760 | tf_op jit(solution)/shard_map/ppermute | solution.py:33
  100.7 3.9 %collective-permute-start.12 = (f16[2,144,128]{2,1,0:T(8,128)(2,1)S(1)}, f16[2,144,128]{2,1,0:T(8,128)(2,1)S(1)}, u32[]{:S(2)}, u32[]{:S(2)}) collective-permute-start(f16[2,144,128]{2,1,0:T(8,128)(2,1)S(1)} %get-tuple-element.62), channel_id=1, source_target_pairs={{0,32},{8,40},{16,48},{24,56},{32,0},{40,8},{48,16},{56,24},{64,96... | collective-permute-start | bytes 221192 | tf_op jit(solution)/shard_map/ppermute | solution.py:33
  104.6 0.9 collective-permute-start.13
  105.6 0.8 collective-permute-done.12
  106.4 2.2 %collective-permute-done.13 = f16[2,144,128]{2,1,0:T(8,128)(2,1)S(1)} collective-permute-done((f16[2,144,128]{2,1,0:T(8,128)(2,1)S(1)}, f16[2,144,128]{2,1,0:T(8,128)(2,1)S(1)}, u32[]{:S(2)}, u32[]{:S(2)}) %collective-permute-start.13) | collective-permute-done | bytes 73760 | tf_op jit(solution)/shard_map/ppermute | solution.py:33
  108.6 0.7 last.1
  109.3 1.6 %collective-permute-start.14 = (bf16[4,64,128]{2,1,0:T(8,128)(2,1)S(1)}, bf16[4,64,128]{2,1,0:T(8,128)(2,1)S(1)}, u32[]{:S(2)}, u32[]{:S(2)}) collective-permute-start(bf16[4,64,128]{2,1,0:T(8,128)(2,1)S(1)} %get-tuple-element.38), channel_id=1, source_target_pairs={{0,8},{8,0},{16,24},{24,16},{32,40},{40,32},{48,56},{56,48},{64,72... | collective-permute-start | bytes 196616 | tf_op jit(solution)/shard_map/ppermute | solution.py:33
  110.9 0.9 collective-permute-done.14
  111.8 0.7 fusion
  112.5 0.8 add_multiply_fusion
  113.3 1.6 %convert_element_type.111 = bf16[1,32,2048]{2,1,0:T(8,128)(2,1)} convert(f32[1,32,2048]{2,1,0:T(8,128)} %reduce-scatter.2.cloned.1.call-done) | non-fusion elementwise | flops 65536 | bytes 393216 | tf_op jit(solution)/shard_map/convert_element_type | solution.py:294
  (62 shorter events, 4.0 us)
Async XLA Ops:
  7.2 25.2 %copy-start.1 = (bf16[27,32,128]{2,1,0:T(8,128)(2,1)S(1)}, bf16[27,32,128]{2,1,0:T(8,128)(2,1)}, u32[]{:S(2)}) copy-start(bf16[27,32,128]{2,1,0:T(8,128)(2,1)} %param.4) | copy-start | bytes 663556
  7.2 52.1 %all-gather.2.cloned.1.call-start = ((), (), s32[]{:S(2)}) async-start(), calls=%async_computation.1 | async-start | bytes 1179648 | tf_op jit(solution)/shard_map/all_gather | solution.py:246
  8.2 4.2 %collective-permute-start.15 = (bf16[4,64,128]{2,1,0:T(8,128)(2,1)S(1)}, bf16[4,64,128]{2,1,0:T(8,128)(2,1)S(1)}, u32[]{:S(2)}, u32[]{:S(2)}) collective-permute-start(bf16[4,64,128]{2,1,0:T(8,128)(2,1)S(1)} %get-tuple-element.70), channel_id=1, source_target_pairs={{0,8},{8,0},{16,24},{24,16},{32,40},{40,32},{48,56},{56,48},{64,72... | collective-permute-start | bytes 196616 | tf_op jit(solution)/shard_map/ppermute | solution.py:33
  12.5 7.1 %collective-permute-start.16 = (bf16[2,128,128]{2,1,0:T(8,128)(2,1)S(1)}, bf16[2,128,128]{2,1,0:T(8,128)(2,1)S(1)}, u32[]{:S(2)}, u32[]{:S(2)}) collective-permute-start(bf16[2,128,128]{2,1,0:T(8,128)(2,1)S(1)} %get-tuple-element.39), channel_id=1, source_target_pairs={{0,16},{8,24},{16,32},{24,40},{32,48},{40,56},{48,0},{56,8},{64,80... | collective-permute-start | bytes 196616 | tf_op jit(solution)/shard_map/ppermute | solution.py:33
  12.5 8.1 %collective-permute-start.17 = (bf16[2,128,128]{2,1,0:T(8,128)(2,1)S(1)}, bf16[2,128,128]{2,1,0:T(8,128)(2,1)S(1)}, u32[]{:S(2)}, u32[]{:S(2)}) collective-permute-start(bf16[2,128,128]{2,1,0:T(8,128)(2,1)S(1)} %get-tuple-element.39), channel_id=1, source_target_pairs={{0,32},{8,40},{16,48},{24,56},{32,0},{40,8},{48,16},{56,24},{64,96... | collective-permute-start | bytes 196616 | tf_op jit(solution)/shard_map/ppermute | solution.py:33
  14.5 6.2 %collective-permute-start.18 = (bf16[2,128,128]{2,1,0:T(8,128)(2,1)S(1)}, bf16[2,128,128]{2,1,0:T(8,128)(2,1)S(1)}, u32[]{:S(2)}, u32[]{:S(2)}) collective-permute-start(bf16[2,128,128]{2,1,0:T(8,128)(2,1)S(1)} %get-tuple-element.39), channel_id=1, source_target_pairs={{0,48},{8,56},{16,0},{24,8},{32,16},{40,24},{48,32},{56,40},{64,11... | collective-permute-start | bytes 196616 | tf_op jit(solution)/shard_map/ppermute | solution.py:33
  15.6 5.1 %collective-permute-start.19 = (bf16[2,128,128]{2,1,0:T(8,128)(2,1)S(1)}, bf16[2,128,128]{2,1,0:T(8,128)(2,1)S(1)}, u32[]{:S(2)}, u32[]{:S(2)}) collective-permute-start(bf16[2,128,128]{2,1,0:T(8,128)(2,1)S(1)} %get-tuple-element.43), channel_id=1, source_target_pairs={{0,64},{8,72},{16,80},{24,88},{32,96},{40,104},{48,112},{56,120},{... | collective-permute-start | bytes 196616 | tf_op jit(solution)/shard_map/ppermute | solution.py:33
  16.9 5.1 %collective-permute-start.20 = (bf16[2,128,128]{2,1,0:T(8,128)(2,1)S(1)}, bf16[2,128,128]{2,1,0:T(8,128)(2,1)S(1)}, u32[]{:S(2)}, u32[]{:S(2)}) collective-permute-start(bf16[2,128,128]{2,1,0:T(8,128)(2,1)S(1)} %get-tuple-element.43), channel_id=1, source_target_pairs={{0,128},{8,136},{16,144},{24,152},{32,160},{40,168},{48,176},{56,1... | collective-permute-start | bytes 196616 | tf_op jit(solution)/shard_map/ppermute | solution.py:33
  19.5 3.9 %collective-permute-start.21 = (bf16[2,128,128]{2,1,0:T(8,128)(2,1)S(1)}, bf16[2,128,128]{2,1,0:T(8,128)(2,1)S(1)}, u32[]{:S(2)}, u32[]{:S(2)}) collective-permute-start(bf16[2,128,128]{2,1,0:T(8,128)(2,1)S(1)} %get-tuple-element.43), channel_id=1, source_target_pairs={{0,192},{8,200},{16,208},{24,216},{32,224},{40,232},{48,240},{56,2... | collective-permute-start | bytes 196616 | tf_op jit(solution)/shard_map/ppermute | solution.py:33
  20.6 92.7 %reduce-scatter.2.cloned.1.call-start = ((), (), s32[]{:S(2)}) async-start(), calls=%async_computation.2 | async-start | bytes 2359296 | tf_op jit(solution)/shard_map/reduce_scatter | solution.py:294
  23.5 7.0 %collective-permute-start.22 = (bf16[4,2,128,128]{3,2,1,0:T(8,128)(2,1)S(1)}, bf16[4,2,128,128]{3,2,1,0:T(8,128)(2,1)S(1)}, u32[]{:S(2)}, u32[]{:S(2)}) collective-permute-start(bf16[4,2,128,128]{3,2,1,0:T(8,128)(2,1)S(1)} %get-tuple-element.47.refs_0_), channel_id=1, source_target_pairs={{0,64},{8,72},{16,80},{24,88},{32,96},{40,104},{48,112},{56,120},{... | collective-permute-start | bytes 786440 | tf_op jit(solution)/shard_map/ppermute | solution.py:33
  23.6 6.2 %collective-permute-start.1 = (bf16[27,32,128]{2,1,0:T(8,128)(2,1)}, bf16[27,32,128]{2,1,0:T(8,128)(2,1)S(1)}, u32[]{:S(2)}, u32[]{:S(2)}) collective-permute-start(bf16[27,32,128]{2,1,0:T(8,128)(2,1)} %param.4), channel_id=1, source_target_pairs={{0,8},{8,0},{16,24},{24,16},{32,40},{40,32},{48,56},{56,48},{64,72... | collective-permute-start | bytes 663560 | tf_op jit(solution)/shard_map/ppermute | solution.py:33
  26.0 10.7 %collective-permute-start.23 = (bf16[4,2,128,128]{3,2,1,0:T(8,128)(2,1)S(1)}, bf16[4,2,128,128]{3,2,1,0:T(8,128)(2,1)S(1)}, u32[]{:S(2)}, u32[]{:S(2)}) collective-permute-start(bf16[4,2,128,128]{3,2,1,0:T(8,128)(2,1)S(1)} %get-tuple-element.47.refs_0_), channel_id=1, source_target_pairs={{0,128},{8,136},{16,144},{24,152},{32,160},{40,168},{48,176},{56,1... | collective-permute-start | bytes 786440 | tf_op jit(solution)/shard_map/ppermute | solution.py:33
  29.4 11.9 %collective-permute-start.24 = (bf16[4,2,128,128]{3,2,1,0:T(8,128)(2,1)S(1)}, bf16[4,2,128,128]{3,2,1,0:T(8,128)(2,1)S(1)}, u32[]{:S(2)}, u32[]{:S(2)}) collective-permute-start(bf16[4,2,128,128]{3,2,1,0:T(8,128)(2,1)S(1)} %get-tuple-element.47.refs_0_), channel_id=1, source_target_pairs={{0,192},{8,200},{16,208},{24,216},{32,224},{40,232},{48,240},{56,2... | collective-permute-start | bytes 786440 | tf_op jit(solution)/shard_map/ppermute | solution.py:33
  29.4 14.4 %collective-permute-start.25 = (bf16[4,2,128,128]{3,2,1,0:T(8,128)(2,1)S(1)}, bf16[4,2,128,128]{3,2,1,0:T(8,128)(2,1)S(1)}, u32[]{:S(2)}, u32[]{:S(2)}) collective-permute-start(bf16[4,2,128,128]{3,2,1,0:T(8,128)(2,1)S(1)} %get-tuple-element.48.refs_4_), channel_id=1, source_target_pairs={{0,16},{8,24},{16,32},{24,40},{32,48},{40,56},{48,0},{56,8},{64,80... | collective-permute-start | bytes 786440 | tf_op jit(solution)/shard_map/ppermute | solution.py:33
  29.8 14.1 %collective-permute-start.26 = (bf16[4,2,128,128]{3,2,1,0:T(8,128)(2,1)S(1)}, bf16[4,2,128,128]{3,2,1,0:T(8,128)(2,1)S(1)}, u32[]{:S(2)}, u32[]{:S(2)}) collective-permute-start(bf16[4,2,128,128]{3,2,1,0:T(8,128)(2,1)S(1)} %get-tuple-element.48.refs_4_), channel_id=1, source_target_pairs={{0,32},{8,40},{16,48},{24,56},{32,0},{40,8},{48,16},{56,24},{64,96... | collective-permute-start | bytes 786440 | tf_op jit(solution)/shard_map/ppermute | solution.py:33
  30.5 13.7 %collective-permute-start.27 = (bf16[4,2,128,128]{3,2,1,0:T(8,128)(2,1)S(1)}, bf16[4,2,128,128]{3,2,1,0:T(8,128)(2,1)S(1)}, u32[]{:S(2)}, u32[]{:S(2)}) collective-permute-start(bf16[4,2,128,128]{3,2,1,0:T(8,128)(2,1)S(1)} %get-tuple-element.48.refs_4_), channel_id=1, source_target_pairs={{0,48},{8,56},{16,0},{24,8},{32,16},{40,24},{48,32},{56,40},{64,11... | collective-permute-start | bytes 786440 | tf_op jit(solution)/shard_map/ppermute | solution.py:33
  54.2 4.0 %collective-permute-start.28 = (f32[4,32,2048]{2,1,0:T(8,128)}, f32[4,32,2048]{2,1,0:T(8,128)S(1)}, u32[]{:S(2)}, u32[]{:S(2)}) collective-permute-start(f32[4,32,2048]{2,1,0:T(8,128)} %get-tuple-element.50), channel_id=1, source_target_pairs={{0,8},{8,0},{16,24},{24,16},{32,40},{40,32},{48,56},{56,48},{64,72... | collective-permute-start | bytes 3145736 | tf_op jit(solution)/shard_map/ppermute | solution.py:33
  59.3 3.2 %copy-start = (bf16[8,32,2048]{2,1,0:T(8,128)(2,1)S(1)}, bf16[8,32,2048]{2,1,0:T(8,128)(2,1)}, u32[]{:S(2)}) copy-start(bf16[8,32,2048]{2,1,0:T(8,128)(2,1)} %all-gather.2.cloned.1.call-done.own_ref) | copy-start | bytes 3145732
  60.4 2.0 %collective-permute-start = (bf16[4,32,2048]{2,1,0:T(8,128)(2,1)S(1)}, bf16[4,32,2048]{2,1,0:T(8,128)(2,1)S(1)}, u32[]{:S(2)}, u32[]{:S(2)}) collective-permute-start(bf16[4,32,2048]{2,1,0:T(8,128)(2,1)S(1)} %constant_dynamic-slice_fusion), channel_id=1, source_target_pairs={{0,8},{8,0},{16,24},{24,16},{32,40},{40,32},{48,56},{56,48},{64,72... | collective-permute-start | bytes 1572872 | tf_op jit(solution)/shard_map/ppermute | solution.py:33
  72.8 9.1 %collective-permute-start.2 = (f16[2,528,128]{2,1,0:T(8,128)(2,1)S(1)}, f16[2,528,128]{2,1,0:T(8,128)(2,1)S(1)}, u32[]{:S(2)}, u32[]{:S(2)}) collective-permute-start(f16[2,528,128]{2,1,0:T(8,128)(2,1)S(1)} %get-tuple-element.60), channel_id=1, source_target_pairs={{0,16},{8,24},{16,32},{24,40},{32,48},{40,56},{48,0},{56,8},{64,80... | collective-permute-start | bytes 811016 | tf_op jit(solution)/shard_map/ppermute | solution.py:33
  73.8 19.7 %collective-permute-start.3 = (f16[2,528,128]{2,1,0:T(8,128)(2,1)S(1)}, f16[2,528,128]{2,1,0:T(8,128)(2,1)S(1)}, u32[]{:S(2)}, u32[]{:S(2)}) collective-permute-start(f16[2,528,128]{2,1,0:T(8,128)(2,1)S(1)} %get-tuple-element.59), channel_id=1, source_target_pairs={{0,32},{8,40},{16,48},{24,56},{32,0},{40,8},{48,16},{56,24},{64,96... | collective-permute-start | bytes 811016 | tf_op jit(solution)/shard_map/ppermute | solution.py:33
  76.3 18.6 %collective-permute-start.4 = (f16[2,528,128]{2,1,0:T(8,128)(2,1)S(1)}, f16[2,528,128]{2,1,0:T(8,128)(2,1)S(1)}, u32[]{:S(2)}, u32[]{:S(2)}) collective-permute-start(f16[2,528,128]{2,1,0:T(8,128)(2,1)S(1)} %get-tuple-element.58), channel_id=1, source_target_pairs={{0,48},{8,56},{16,0},{24,8},{32,16},{40,24},{48,32},{56,40},{64,11... | collective-permute-start | bytes 811016 | tf_op jit(solution)/shard_map/ppermute | solution.py:33
  77.6 17.4 %collective-permute-start.5 = (f16[2,528,128]{2,1,0:T(8,128)(2,1)S(1)}, f16[2,528,128]{2,1,0:T(8,128)(2,1)S(1)}, u32[]{:S(2)}, u32[]{:S(2)}) collective-permute-start(f16[2,528,128]{2,1,0:T(8,128)(2,1)S(1)} %get-tuple-element.57), channel_id=1, source_target_pairs={{0,64},{8,72},{16,80},{24,88},{32,96},{40,104},{48,112},{56,120},{... | collective-permute-start | bytes 811016 | tf_op jit(solution)/shard_map/ppermute | solution.py:33
  78.9 16.1 %collective-permute-start.6 = (f16[2,528,128]{2,1,0:T(8,128)(2,1)S(1)}, f16[2,528,128]{2,1,0:T(8,128)(2,1)S(1)}, u32[]{:S(2)}, u32[]{:S(2)}) collective-permute-start(f16[2,528,128]{2,1,0:T(8,128)(2,1)S(1)} %get-tuple-element.56), channel_id=1, source_target_pairs={{0,128},{8,136},{16,144},{24,152},{32,160},{40,168},{48,176},{56,1... | collective-permute-start | bytes 811016 | tf_op jit(solution)/shard_map/ppermute | solution.py:33
  81.8 13.3 %collective-permute-start.7 = (f16[2,528,128]{2,1,0:T(8,128)(2,1)S(1)}, f16[2,528,128]{2,1,0:T(8,128)(2,1)S(1)}, u32[]{:S(2)}, u32[]{:S(2)}) collective-permute-start(f16[2,528,128]{2,1,0:T(8,128)(2,1)S(1)} %get-tuple-element.55), channel_id=1, source_target_pairs={{0,192},{8,200},{16,208},{24,216},{32,224},{40,232},{48,240},{56,2... | collective-permute-start | bytes 811016 | tf_op jit(solution)/shard_map/ppermute | solution.py:33
  93.5 19.0 %collective-permute-start.29 = (f32[27,32,128]{2,1,0:T(8,128)S(1)}, f32[27,32,128]{2,1,0:T(8,128)S(1)}, u32[]{:S(2)}, u32[]{:S(2)}) collective-permute-start(f32[27,32,128]{2,1,0:T(8,128)S(1)} %get-tuple-element.54), channel_id=1, source_target_pairs={{0,8},{8,0},{16,24},{24,16},{32,40},{40,32},{48,56},{56,48},{64,72... | collective-permute-start | bytes 1327112 | tf_op jit(solution)/shard_map/ppermute | solution.py:33
  95.5 5.2 %collective-permute-start.8 = (f16[2,144,128]{2,1,0:T(8,128)(2,1)S(1)}, f16[2,144,128]{2,1,0:T(8,128)(2,1)S(1)}, u32[]{:S(2)}, u32[]{:S(2)}) collective-permute-start(f16[2,144,128]{2,1,0:T(8,128)(2,1)S(1)} %get-tuple-element.66), channel_id=1, source_target_pairs={{0,64},{8,72},{16,80},{24,88},{32,96},{40,104},{48,112},{56,120},{... | collective-permute-start | bytes 221192 | tf_op jit(solution)/shard_map/ppermute | solution.py:33
  96.4 8.2 %collective-permute-start.9 = (f16[2,144,128]{2,1,0:T(8,128)(2,1)S(1)}, f16[2,144,128]{2,1,0:T(8,128)(2,1)S(1)}, u32[]{:S(2)}, u32[]{:S(2)}) collective-permute-start(f16[2,144,128]{2,1,0:T(8,128)(2,1)S(1)} %get-tuple-element.65), channel_id=1, source_target_pairs={{0,128},{8,136},{16,144},{24,152},{32,160},{40,168},{48,176},{56,1... | collective-permute-start | bytes 221192 | tf_op jit(solution)/shard_map/ppermute | solution.py:33
  97.3 8.2 %collective-permute-start.10 = (f16[2,144,128]{2,1,0:T(8,128)(2,1)S(1)}, f16[2,144,128]{2,1,0:T(8,128)(2,1)S(1)}, u32[]{:S(2)}, u32[]{:S(2)}) collective-permute-start(f16[2,144,128]{2,1,0:T(8,128)(2,1)S(1)} %get-tuple-element.64), channel_id=1, source_target_pairs={{0,192},{8,200},{16,208},{24,216},{32,224},{40,232},{48,240},{56,2... | collective-permute-start | bytes 221192 | tf_op jit(solution)/shard_map/ppermute | solution.py:33
  99.0 6.5 %collective-permute-start.11 = (f16[2,144,128]{2,1,0:T(8,128)(2,1)S(1)}, f16[2,144,128]{2,1,0:T(8,128)(2,1)S(1)}, u32[]{:S(2)}, u32[]{:S(2)}) collective-permute-start(f16[2,144,128]{2,1,0:T(8,128)(2,1)S(1)} %get-tuple-element.63), channel_id=1, source_target_pairs={{0,16},{8,24},{16,32},{24,40},{32,48},{40,56},{48,0},{56,8},{64,80... | collective-permute-start | bytes 221192 | tf_op jit(solution)/shard_map/ppermute | solution.py:33
  100.7 5.6 %collective-permute-start.12 = (f16[2,144,128]{2,1,0:T(8,128)(2,1)S(1)}, f16[2,144,128]{2,1,0:T(8,128)(2,1)S(1)}, u32[]{:S(2)}, u32[]{:S(2)}) collective-permute-start(f16[2,144,128]{2,1,0:T(8,128)(2,1)S(1)} %get-tuple-element.62), channel_id=1, source_target_pairs={{0,32},{8,40},{16,48},{24,56},{32,0},{40,8},{48,16},{56,24},{64,96... | collective-permute-start | bytes 221192 | tf_op jit(solution)/shard_map/ppermute | solution.py:33
  104.6 3.9 %collective-permute-start.13 = (f16[2,144,128]{2,1,0:T(8,128)(2,1)S(1)}, f16[2,144,128]{2,1,0:T(8,128)(2,1)S(1)}, u32[]{:S(2)}, u32[]{:S(2)}) collective-permute-start(f16[2,144,128]{2,1,0:T(8,128)(2,1)S(1)} %get-tuple-element.61), channel_id=1, source_target_pairs={{0,48},{8,56},{16,0},{24,8},{32,16},{40,24},{48,32},{56,40},{64,11... | collective-permute-start | bytes 221192 | tf_op jit(solution)/shard_map/ppermute | solution.py:33
  109.3 2.5 %collective-permute-start.14 = (bf16[4,64,128]{2,1,0:T(8,128)(2,1)S(1)}, bf16[4,64,128]{2,1,0:T(8,128)(2,1)S(1)}, u32[]{:S(2)}, u32[]{:S(2)}) collective-permute-start(bf16[4,64,128]{2,1,0:T(8,128)(2,1)S(1)} %get-tuple-element.38), channel_id=1, source_target_pairs={{0,8},{8,0},{16,24},{24,16},{32,40},{40,32},{48,56},{56,48},{64,72... | collective-permute-start | bytes 196616 | tf_op jit(solution)/shard_map/ppermute | solution.py:33
Sparse Core Ops, SparseCore 0:
  20.7 33.8 all-gather.1
  59.4 38.9 reduce-scatter.1

commit v3 on v2

--- a/solution.py
+++ b/solution.py
@@ -44,22 +44,22 @@
     return (y >= 0) & (y < SY) & (z >= 0) & (z < SZ)
 
 
-def dgrad_kernel(place, *refs):
-    half_a, half_b = refs[0:4], refs[4:8]
-    wd_ref, taps_ref, own_ref, other_ref = refs[8:12]
+def dgrad_kernel(half, place, *refs):
+    parts, wd_ref = refs[:SIDE], refs[SIDE]
+    taps_ref, own_ref, other_ref = refs[-3:]
     ci = own_ref.shape[1]
     co = taps_ref.shape[2] // 3
     n = pl.program_id(0)
     my_y, my_x, core = place[0], place[1], place[2]
 
-    def fill(parts, y_first):
+    def fill(y_first):
         for first in range(SIDE):
             for second in range(SIDE):
                 step_y, step_x = (first, second) if y_first else (second, first)
                 y = lax.rem(my_y - step_y + SIDE, SIDE)
                 x = lax.rem(my_x - step_x + SIDE, SIDE)
                 p = y * SIDE + x
-                cells = parts[first][second, lax.rem(n, 2)]
+                cells = parts[first][second, n]
 
                 def put(q, column):
                     row = pl.multiple_of(q * PLANE, PLANE)
@@ -71,8 +71,7 @@
 
     taps_ref[0, (SX - 1) * PLANE :, 0:co] = jnp.zeros((PLANE, co), BF16)
     taps_ref[0, 0:PLANE, 2 * co :] = jnp.zeros((PLANE, co), BF16)
-    pl.when(n < 2)(lambda: fill(half_a, True))
-    pl.when(n >= 2)(lambda: fill(half_b, False))
+    fill(half == 0)
 
     wd = wd_ref[...]
     masks = [plane_mask(2 * ci, -b, -c) for b, c in in_plane]
@@ -94,7 +93,7 @@
             other_ref[0, :, lanes] = jnp.where(core == 0, high, low)
 
 
-def fwd_kernel(place, own_ref, other_ref, wa_ref, cols_ref, msg_a, msg_b, own_a, own_b, stage, sums):
+def fwd_kernel(half, place, own_ref, other_ref, wa_ref, cols_ref, msg, own, stage, sums):
     ci = own_ref.shape[1]
     co = wa_ref.shape[0] // 3
     n = pl.program_id(0)
@@ -116,12 +115,12 @@
             term = cells
             if shift:
                 term = jnp.where(masks[index], pltpu.roll(term, shift, 1), 0.0)
-            cols_ref[0, index * 2 * ci : (index + 1) * 2 * ci, lanes] = term.astype(BF16)
+            cols_ref[n, index * 2 * ci : (index + 1) * 2 * ci, lanes] = term.astype(BF16)
 
     step = 4
     for first in range(0, SX, step):
         lanes = slice(first * PLANE, (first + step) * PLANE)
-        product = jnp.dot(wa_ref[...], cols_ref[0, :, lanes], preferred_element_type=F32)
+        product = jnp.dot(wa_ref[...], cols_ref[n, :, lanes], preferred_element_type=F32)
         for j in range(step):
             stage[first + j + 1] = product[:, j * PLANE : (j + 1) * PLANE]
 
@@ -134,26 +133,24 @@
     power = 14.0 - jnp.ceil(jnp.log2(peak))
     factor = jnp.exp2(power[0:1])
     rows = SIDE * co
-    at = lax.rem(n, 2)
-
-    def send(msg, own, y_first):
+
+    def send(y_first):
         for first in range(SIDE):
             if first == 0:
-                own[at, rows:] = power
+                own[n, rows:] = power
             else:
-                msg[first - 1, at, rows:] = power
+                msg[first - 1, n, rows:] = power
             for second in range(SIDE):
                 step_y, step_x = (first, second) if y_first else (second, first)
                 y = lax.rem(my_y + step_y, SIDE)
                 x = lax.rem(my_x + step_x, SIDE)
                 total = sums[y * SIDE + x]
                 if first == 0:
-                    own[at, second * co : (second + 1) * co] = total
+                    own[n, second * co : (second + 1) * co] = total
                 else:
-                    msg[first - 1, at, second * co : (second + 1) * co] = total * factor
-
-    pl.when(n < 2)(lambda: send(msg_a, own_a, False))
-    pl.when(n >= 2)(lambda: send(msg_b, own_b, True))
+                    msg[first - 1, n, second * co : (second + 1) * co] = total * factor
+
+    send(half == 1)
 
 
 def arrived(own, messages, rows):
@@ -165,20 +162,16 @@
     return total, least
 
 
-def turn_kernel(*refs):
-    ins, outs = refs[:8], refs[8:]
-    for half in range(2):
-        own, messages = ins[4 * half], ins[4 * half + 1 : 4 * half + 4]
-        msg, mine = outs[2 * half : 2 * half + 2]
-        rows = own.shape[1] - NOTE
-        size = rows // SIDE
-        total, least = arrived(own[...], [m[...] for m in messages], rows)
-        power = least - 2.0
-        mine[:, :size] = total[:, :size]
-        mine[:, size:] = power
-        for step in range(1, SIDE):
-            msg[step - 1, :, :size] = total[:, step * size : (step + 1) * size] * jnp.exp2(power[:, 0:1])
-            msg[step - 1, :, size:] = power
+def turn_kernel(own, one, two, three, msg, mine):
+    rows = own.shape[1] - NOTE
+    size = rows // SIDE
+    total, least = arrived(own[...], [one[...], two[...], three[...]], rows)
+    power = least - 2.0
+    mine[:, :size] = total[:, :size]
+    mine[:, size:] = power
+    for step in range(1, SIDE):
+        msg[step - 1, :, :size] = total[:, step * size : (step + 1) * size] * jnp.exp2(power[:, 0:1])
+        msg[step - 1, :, size:] = power
 
 
 def last_kernel(place, *refs):
@@ -195,7 +188,7 @@
             other_ref[half * total.shape[0] + at] = jnp.where(place[2] == 0, high, low)
 
 
-def wgrad_kernel(place, cols_ref, taps_ref, own_ref, other_ref, acc):
+def wgrad_kernel(place, cols_a, cols_b, taps_a, taps_b, own_ref, other_ref, acc):
     ci, co = own_ref.shape[1:]
     n = pl.program_id(0)
 
@@ -203,7 +196,8 @@
     def _():
         acc[...] = jnp.zeros_like(acc)
 
-    acc[...] += jnp.dot(cols_ref[0], taps_ref[0], preferred_element_type=F32)
+    acc[...] += jnp.dot(cols_a[n], taps_a[0], preferred_element_type=F32)
+    acc[...] += jnp.dot(cols_b[n], taps_b[0], preferred_element_type=F32)
 
     @pl.when(n == pl.num_programs(0) - 1)
     def _():
@@ -258,9 +252,7 @@
         (gather_stage(plane[:pairs], along_x), gather_stage(plane[pairs:], along_y))
     )
     row_a, row_b = lax.optimization_barrier((jnp.stack(near_a), jnp.stack(near_b)))
-    parts = gather_stage(row_a, along_y) + gather_stage(row_b, along_x)
-
-    sample = swap_cores(taken(gathered, 1 - core, mine, 0))
+    parts = gather_stage(row_a, along_y), gather_stage(row_b, along_x)
 
     pair = in_order(weight, swap_cores(weight), 1)
     wd = jnp.transpose(pair.reshape(3, 9, 2 * ci, co), (1, 2, 0, 3)).reshape(9 * 2 * ci, 3 * co)
@@ -268,52 +260,68 @@
 
     cells = inputs.shape[2]
     params = pltpu.CompilerParams(vmem_limit_bytes=VMEM_LIMIT)
-    taps, terms, other = pl.pallas_call(
-        dgrad_kernel,
-        grid_spec=pltpu.PrefetchScalarGridSpec(
-            num_scalar_prefetch=1,
-            grid=(mine,),
-            in_specs=[whole(p.shape) for p in parts] + [whole(wd.shape)],
-            out_specs=[
-                per_sample((cells, 3 * co)),
-                pl.BlockSpec((1, ci, cells), lambda n, place: (place[2] * mine + n, 0, 0)),
-                per_sample((ci, cells)),
+    def dgrad(half, earlier):
+        place_of = lambda n, place: (place[2] * mine + half * pairs + n, 0, 0)
+        taps, terms, other = pl.pallas_call(
+            functools.partial(dgrad_kernel, half),
+            grid_spec=pltpu.PrefetchScalarGridSpec(
+                num_scalar_prefetch=1,
+                grid=(pairs,),
+                in_specs=[whole(p.shape) for p in parts[half]]
+                + [whole(wd.shape)]
+                + [pl.BlockSpec(memory_space=pl.ANY)] * len(earlier),
+                out_specs=[
+                    per_sample((cells, 3 * co)),
+                    pl.BlockSpec((1, ci, cells), place_of),
+                    per_sample((ci, cells)),
+                ],
+            ),
+            out_shape=[
+                pltpu.HBM((pairs, cells, 3 * co), BF16),
+                pltpu.HBM((batch, ci, cells), F32),
+                pltpu.HBM((pairs, ci, cells), F32),
             ],
-        ),
-        out_shape=[
-            pltpu.HBM((mine, cells, 3 * co), BF16),
-            pltpu.HBM((batch, ci, cells), F32),
-            pltpu.HBM((mine, ci, cells), F32),
-        ],
-        compiler_params=params,
-        name="dgrad",
-    )(place, *parts, wd)
-    taps = pltpu.with_memory_space_constraint(taps, pltpu.HBM)
-
-    terms = lax.dynamic_update_slice_in_dim(terms, swap_cores(other), (1 - core) * mine, 0)
+            input_output_aliases={SIDE + 2: 1} if earlier else {},
+            compiler_params=params,
+            name="dgrad",
+        )(place, *parts[half], wd, *earlier)
+        return pltpu.with_memory_space_constraint(taps, pltpu.HBM), terms, swap_cores(other)
+
+    taps_a, terms, term_a = dgrad(0, [])
+    taps_b, terms, term_b = dgrad(1, [terms])
+    samples = [taken(gathered, (1 - core) * 2 + half, pairs, 0) for half in range(2)]
+    samples, term_a, term_b = lax.optimization_barrier((samples, term_a, term_b))
+    samples = [swap_cores(sample) for sample in samples]
+    terms = lax.dynamic_update_slice_in_dim(terms, term_a, (1 - core) * mine, 0)
+    terms = lax.dynamic_update_slice_in_dim(terms, term_b, (1 - core) * mine + pairs, 0)
     grad_input = lax.psum_scatter(terms, "cout", scatter_dimension=0, tiled=True).astype(BF16)
 
     rows = SIDE * co + NOTE
     sent = jax.ShapeDtypeStruct((SIDE - 1, pairs, rows, PLANE), F32)
     kept = jax.ShapeDtypeStruct((pairs, rows, PLANE), F32)
-    columns, msg_a, msg_b, own_a, own_b = pl.pallas_call(
-        fwd_kernel,
-        grid_spec=pltpu.PrefetchScalarGridSpec(
-            num_scalar_prefetch=1,
-            grid=(mine,),
-            in_specs=[
-                pl.BlockSpec((1, ci, cells), lambda n, place: (place[2] * mine + n, 0, 0)),
-                per_sample((ci, cells)),
-                whole(wa.shape),
-            ],
-            out_specs=[per_sample((9 * 2 * ci, cells))] + [whole(o.shape) for o in (sent, sent, kept, kept)],
-            scratch_shapes=[pltpu.VMEM((SX + 2, 3 * co, PLANE), F32), pltpu.VMEM((SX, co, PLANE), F32)],
-        ),
-        out_shape=[pltpu.HBM((mine, 9 * 2 * ci, cells), BF16), sent, sent, kept, kept],
-        compiler_params=params,
-        name="forward",
-    )(place, gathered, sample, wa)
-    columns = pltpu.with_memory_space_constraint(columns, pltpu.HBM)
+
+    def forward(half):
+        columns, msg, own = pl.pallas_call(
+            functools.partial(fwd_kernel, half),
+            grid_spec=pltpu.PrefetchScalarGridSpec(
+                num_scalar_prefetch=1,
+                grid=(pairs,),
+                in_specs=[
+                    pl.BlockSpec((1, ci, cells), lambda n, place: (place[2] * mine + half * pairs + n, 0, 0)),
+                    per_sample((ci, cells)),
+                    whole(wa.shape),
+                ],
+                out_specs=[pl.BlockSpec(memory_space=pltpu.VMEM), whole(sent.shape), whole(kept.shape)],
+                scratch_shapes=[pltpu.VMEM((SX + 2, 3 * co, PLANE), F32), pltpu.VMEM((SX, co, PLANE), F32)],
+            ),
+            out_shape=[pltpu.VMEM((pairs, 9 * 2 * ci, cells), BF16), sent, kept],
+            compiler_params=params,
+            name="forward",
+        )(place, gathered, samples[half], wa)
+        return columns, msg, own
+
+    columns_a, msg_a, own_a = forward(0)
+    columns_b, msg_b, own_b = forward(1)
 
     def reduce_stage(msg, moves):
         return [move(msg[i].astype(F16)).astype(F32) for i, move in enumerate(moves)]
@@ -321,10 +329,32 @@
     rows = co + NOTE
     sent = jax.ShapeDtypeStruct((SIDE - 1, pairs, rows, PLANE), F32)
     kept = jax.ShapeDtypeStruct((pairs, rows, PLANE), F32)
-    msg_a, own_a, msg_b, own_b = pl.pallas_call(
-        turn_kernel, out_shape=[sent, kept, sent, kept], compiler_params=params, name="turn"
-    )(own_a, *reduce_stage(msg_a, along_x), own_b, *reduce_stage(msg_b, along_y))
-    ends = [own_a, *reduce_stage(msg_a, along_y), own_b, *reduce_stage(msg_b, along_x)]
+
+    def turn(own, msg, moves):
+        return pl.pallas_call(turn_kernel, out_shape=[sent, kept], compiler_params=params, name="turn")(
+            own, *reduce_stage(msg, moves)
+        )
+
+    msg_a, own_a = turn(own_a, msg_a, along_x)
+    ends_a = [own_a, *reduce_stage(msg_a, along_y)]
+    msg_b, own_b = turn(own_b, msg_b, along_y)
+    ends_b = [own_b, *reduce_stage(msg_b, along_x)]
+    ends = ends_a + ends_b
+    own, other = pl.pallas_call(
+        wgrad_kernel,
+        grid_spec=pltpu.PrefetchScalarGridSpec(
+            num_scalar_prefetch=1,
+            grid=(pairs,),
+            in_specs=[pl.BlockSpec(memory_space=pltpu.VMEM)] * 2 + [per_sample((cells, 3 * co))] * 2,
+            out_specs=[whole((27, ci, co))] * 2,
+            scratch_shapes=[pltpu.VMEM((9 * 2 * ci, 3 * co), F32)],
+        ),
+        out_shape=[jax.ShapeDtypeStruct((27, ci, co), F32)] * 2,
+        compiler_params=params,
+        name="wgrad",
+    )(place, columns_a, columns_b, taps_a, taps_b)
+    grad_weight = (own + swap_cores(other)) / math.sqrt(batch * cells)
+    ends, grad_weight = lax.optimization_barrier((ends, grad_weight))
     own, other = pl.pallas_call(
         last_kernel,
         grid_spec=pltpu.PrefetchScalarGridSpec(
@@ -338,21 +368,6 @@
         name="last",
     )(place, *ends)
     output = jnp.transpose(in_order(own, swap_cores(other), 0), (0, 2, 1))
-
-    own, other = pl.pallas_call(
-        wgrad_kernel,
-        grid_spec=pltpu.PrefetchScalarGridSpec(
-            num_scalar_prefetch=1,
-            grid=(mine,),
-            in_specs=[per_sample((9 * 2 * ci, cells)), per_sample((cells, 3 * co))],
-            out_specs=[whole((27, ci, co))] * 2,
-            scratch_shapes=[pltpu.VMEM((9 * 2 * ci, 3 * co), F32)],
-        ),
-        out_shape=[jax.ShapeDtypeStruct((27, ci, co), F32)] * 2,
-        compiler_params=params,
-        name="wgrad",
-    )(place, columns, taps)
-    grad_weight = (own + swap_cores(other)) / math.sqrt(batch * cells)
     return output, grad_input, grad_weight
 
 

time: 124 us -> 112 us (0.903); the launches traced: 122 us -> 112 us
  starting transfers between devices: 44.2 us -> 34.7 us
    ppermute x30 -> x32, starting transfers between devices: 44.2 us -> 34.6 us  [move_xy(): return lax.ppermute(value, 'cin', pairs)]
    pallas_call x1, Pallas kernels: 9.38 us -> 7.84 us  [body(): pl.pallas_call(wgrad_kernel, grid_spec=pltpu.PrefetchScalarGridSpec(num_s...]
    ppermute x30 -> x32, waiting for transfers between devices: 24.2 us -> 23.2 us  [move_xy(): return lax.ppermute(value, 'cin', pairs)]
    pallas_call x3 -> x6, Pallas kernels: 20.3 us -> 21.1 us  [the longest x2 11.8 us: dgrad(): pl.pallas_call(functools.partial(dgrad_kernel, half), grid_spec=pltpu.Pre...]
  transfers between devices with their start and end apart: 32 -> 34, of which waited for: 15 -> 12; matrix products, arithmetic and copies ran while one was open for 5% -> 5% of each run, Pallas kernels for 25% -> 27%
where the time goes in v3:
time: 112 us
  starting transfers between devices  34.7 us (31%)
  Pallas kernels  29.6 us (26%)
  waiting for transfers between devices  23.9 us (21%)
  between operations  14.4 us (13%)
  local copies, waits for them, and re-layouts  4.71 us (4%)
  other arithmetic  4.3 us (4%)
    ppermute x32, starting transfers between devices, move_xy(): return lax.ppermute(value, 'cin', pairs)  34.6 us
    ppermute x32, waiting for transfers between devices, move_xy(): return lax.ppermute(value, 'cin', pairs)  23.2 us
    pallas_call x2, Pallas kernels, dgrad(): pl.pallas_call(functools.partial(dgrad_kernel, half), grid_spec=pltpu.Pre...  11.8 us
    pallas_call x2, Pallas kernels, forward(): pl.pallas_call(functools.partial(fwd_kernel, half), grid_spec=pltpu.Prefe...  9.01 us
    pallas_call x1, Pallas kernels, body(): pl.pallas_call(wgrad_kernel, grid_spec=pltpu.PrefetchScalarGridSpec(num_s...  7.84 us
  transfers between devices with their start and end apart: 34, of which 12 were waited for; matrix products, arithmetic and copies ran while one was open for 5% of the time, Pallas kernels for 27%

profile of v3, /device:TPU:1, one launch (start us, length us, event | category | flops | bytes accessed | tf_op | source)
XLA Modules:
  0.0 111.6 jit_solution(5980431702557554548)
XLA Ops:
  7.2 0.7 all-gather.2.cloned.1.call-update
  8.0 0.9 dynamic-slice_bitcast_fusion.1
  8.9 3.3 %collective-permute-start = (bf16[4,64,128]{2,1,0:T(8,128)(2,1)S(1)}, bf16[4,64,128]{2,1,0:T(8,128)(2,1)S(1)}, u32[]{:S(2)}, u32[]{:S(2)}) collective-permute-start(bf16[4,64,128]{2,1,0:T(8,128)(2,1)S(1)} %get-tuple-element.106), channel_id=1, source_target_pairs={{0,8},{8,0},{16,24},{24,16},{32,40},{40,32},{48,56},{56,48},{64,72... | collective-permute-start | bytes 196616 | tf_op jit(solution)/shard_map/ppermute | solution.py:33
  12.2 0.9 collective-permute-done
  13.2 1.1 collective-permute-start.6
  14.6 0.7 collective-permute-start.4
  15.3 2.5 %collective-permute-start.3 = (bf16[2,128,128]{2,1,0:T(8,128)(2,1)S(1)}, bf16[2,128,128]{2,1,0:T(8,128)(2,1)S(1)}, u32[]{:S(2)}, u32[]{:S(2)}) collective-permute-start(bf16[2,128,128]{2,1,0:T(8,128)(2,1)S(1)} %get-tuple-element.46), channel_id=1, source_target_pairs={{0,48},{8,56},{16,0},{24,8},{32,16},{40,24},{48,32},{56,40},{64,11... | collective-permute-start | bytes 196616 | tf_op jit(solution)/shard_map/ppermute | solution.py:33
  18.3 0.6 collective-permute-start.1
  18.9 1.4 %collective-permute-done.4 = bf16[2,128,128]{2,1,0:T(8,128)(2,1)S(1)} collective-permute-done((bf16[2,128,128]{2,1,0:T(8,128)(2,1)S(1)}, bf16[2,128,128]{2,1,0:T(8,128)(2,1)S(1)}, u32[]{:S(2)}, u32[]{:S(2)}) %collective-permute-start.4) | collective-permute-done | bytes 65568 | tf_op jit(solution)/shard_map/ppermute | solution.py:33
  20.3 2.1 %collective-permute-done.2 = bf16[2,128,128]{2,1,0:T(8,128)(2,1)S(1)} collective-permute-done((bf16[2,128,128]{2,1,0:T(8,128)(2,1)S(1)}, bf16[2,128,128]{2,1,0:T(8,128)(2,1)S(1)}, u32[]{:S(2)}, u32[]{:S(2)}) %collective-permute-start.2) | collective-permute-done | bytes 65568 | tf_op jit(solution)/shard_map/ppermute | solution.py:33
  22.4 0.7 collective-permute-done.1
  23.1 2.1 %collective-permute-start.9 = (bf16[4,2,128,128]{3,2,1,0:T(8,128)(2,1)S(1)}, bf16[4,2,128,128]{3,2,1,0:T(8,128)(2,1)S(1)}, u32[]{:S(2)}, u32[]{:S(2)}) collective-permute-start(bf16[4,2,128,128]{3,2,1,0:T(8,128)(2,1)S(1)} %get-tuple-element.54.refs_0_), channel_id=1, source_target_pairs={{0,192},{8,200},{16,208},{24,216},{32,224},{40,232},{48,240},{56,2... | collective-permute-start | bytes 786440 | tf_op jit(solution)/shard_map/ppermute | solution.py:33
  25.2 2.9 %collective-permute-start.10 = (bf16[27,32,128]{2,1,0:T(8,128)(2,1)}, bf16[27,32,128]{2,1,0:T(8,128)(2,1)S(1)}, u32[]{:S(2)}, u32[]{:S(2)}) collective-permute-start(bf16[27,32,128]{2,1,0:T(8,128)(2,1)} %param.4), channel_id=1, source_target_pairs={{0,8},{8,0},{16,24},{24,16},{32,40},{40,32},{48,56},{56,48},{64,72... | collective-permute-start | bytes 663560 | tf_op jit(solution)/shard_map/ppermute | solution.py:33
  28.1 1.4 %collective-permute-start.8 = (bf16[4,2,128,128]{3,2,1,0:T(8,128)(2,1)S(1)}, bf16[4,2,128,128]{3,2,1,0:T(8,128)(2,1)S(1)}, u32[]{:S(2)}, u32[]{:S(2)}) collective-permute-start(bf16[4,2,128,128]{3,2,1,0:T(8,128)(2,1)S(1)} %get-tuple-element.54.refs_0_), channel_id=1, source_target_pairs={{0,128},{8,136},{16,144},{24,152},{32,160},{40,168},{48,176},{56,1... | collective-permute-start | bytes 786440 | tf_op jit(solution)/shard_map/ppermute | solution.py:33
  29.8 0.9 collective-permute-start.13
  30.7 0.8 collective-permute-start.12
  32.4 5.2 %collective-permute-done.8.refs_2_ = bf16[4,2,128,128]{3,2,1,0:T(8,128)(2,1)S(1)} collective-permute-done((bf16[4,2,128,128]{3,2,1,0:T(8,128)(2,1)S(1)}, bf16[4,2,128,128]{3,2,1,0:T(8,128)(2,1)S(1)}, u32[]{:S(2)}, u32[]{:S(2)}) %collective-permute-start.8) | collective-permute-done | bytes 262176 | tf_op jit(solution)/shard_map/ppermute | solution.py:33
  37.6 5.9 %collective-permute-done.7.refs_1_ = bf16[4,2,128,128]{3,2,1,0:T(8,128)(2,1)S(1)} collective-permute-done((bf16[4,2,128,128]{3,2,1,0:T(8,128)(2,1)S(1)}, bf16[4,2,128,128]{3,2,1,0:T(8,128)(2,1)S(1)}, u32[]{:S(2)}, u32[]{:S(2)}) %collective-permute-start.7) | collective-permute-done | bytes 262176 | tf_op jit(solution)/shard_map/ppermute | solution.py:33
  43.5 5.9 %dgrad.2 = (bf16[2,2048,384]{2,1,0:T(8,128)(2,1)}, f32[8,32,2048]{2,1,0:T(8,128)}, f32[2,32,2048]{2,1,0:T(8,128)}) custom-call(s32[3]{0:T(128)S(1)} %pad_add_fusion.place, bf16[4,2,128,128]{3,2,1,0:T(8,128)(2,1)S(1)} %get-tuple-element.54.refs_0_, bf16[4,2,128,128]{3,2,1,0:T(8,128)(2,1)S(1)} %collective-permute-done.7.refs_1_, ...), custom_call_target="tpu_custom_call" | custom-call | tf_op jit(solution)/shard_map/dgrad/pallas_call | solution.py:265
  49.8 5.9 %dgrad.3 = (bf16[2,2048,384]{2,1,0:T(8,128)(2,1)}, f32[8,32,2048]{2,1,0:T(8,128)}, f32[2,32,2048]{2,1,0:T(8,128)}) custom-call(s32[3]{0:T(128)S(1)} %pad_add_fusion.place, bf16[4,2,128,128]{3,2,1,0:T(8,128)(2,1)S(1)} %get-tuple-element.56.refs_0_, bf16[4,2,128,128]{3,2,1,0:T(8,128)(2,1)S(1)} %collective-permute-done.12.refs_1_, ...), custom_call_target="tpu_custom_call", output_to_operand_aliasing={{1}: (6, {})} | custom-call | tf_op jit(solution)/shard_map/dgrad/pallas_call | solution.py:265
  55.8 1.1 constant_dynamic-slice_fusion
  56.8 1.0 collective-permute-done.15
  57.9 0.8 constant_dynamic-update-slice_fusion.1
  58.7 0.8 constant_dynamic-update-slice_fusion
  60.5 0.7 collective-permute-done.23.other_ref
  61.2 4.5 %forward.3 = (bf16[2,576,2048]{2,1,0:T(8,128)(2,1)S(1)}, f32[3,2,528,128]{3,2,1,0:T(8,128)S(1)}, f32[2,528,128]{2,1,0:T(8,128)S(1)}) custom-call(s32[3]{0:T(128)S(1)} %pad_add_fusion.place, bf16[8,32,2048]{2,1,0:T(8,128)(2,1)S(1)} %copy-done, bf16[2,32,2048]{2,1,0:T(8,128)(2,1)S(1)} %collective-permute-done.23.other_ref, bf16[384,576]{1,0:T(8,128)(2,1)S(1)} %bitcast.53), custom_call_target="tpu_custom_call" | custom-call | tf_op jit(solution)/shard_map/forward/pallas_call | solution.py:304
  66.4 1.4 %collective-permute-start.25 = (f16[2,528,128]{2,1,0:T(8,128)(2,1)S(1)}, f16[2,528,128]{2,1,0:T(8,128)(2,1)S(1)}, u32[]{:S(2)}, u32[]{:S(2)}) collective-permute-start(f16[2,528,128]{2,1,0:T(8,128)(2,1)S(1)} %get-tuple-element.92), channel_id=1, source_target_pairs={{0,128},{8,136},{16,144},{24,152},{32,160},{40,168},{48,176},{56,1... | collective-permute-start | bytes 811016 | tf_op jit(solution)/shard_map/ppermute | solution.py:33
  67.8 0.5 collective-permute-start.24
  68.4 4.5 %forward.2 = (bf16[2,576,2048]{2,1,0:T(8,128)(2,1)S(1)}, f32[3,2,528,128]{3,2,1,0:T(8,128)S(1)}, f32[2,528,128]{2,1,0:T(8,128)S(1)}) custom-call(s32[3]{0:T(128)S(1)} %pad_add_fusion.place, bf16[8,32,2048]{2,1,0:T(8,128)(2,1)S(1)} %copy-done, bf16[2,32,2048]{2,1,0:T(8,128)(2,1)S(1)} %collective-permute-done.16.other_ref, bf16[384,576]{1,0:T(8,128)(2,1)S(1)} %bitcast.54), custom_call_target="tpu_custom_call" | custom-call | tf_op jit(solution)/shard_map/forward/pallas_call | solution.py:304
  73.5 0.9 collective-permute-start.18
  74.4 0.8 collective-permute-start.17
  75.2 7.8 %wgrad.1 = (f32[27,32,128]{2,1,0:T(8,128)S(1)}, f32[27,32,128]{2,1,0:T(8,128)S(1)}) custom-call(s32[3]{0:T(128)S(1)} %pad_add_fusion.place, bf16[2,576,2048]{2,1,0:T(8,128)(2,1)S(1)} %get-tuple-element.69.cols_a, bf16[2,576,2048]{2,1,0:T(8,128)(2,1)S(1)} %get-tuple-element.70.cols_b, bf16[2,2048,384]{2,1,0:T(8,128)(2,1)} %get-tuple-element.71.taps_a, ...), custom_call_target="tpu_custom_call" | custom-call | tf_op jit(solution)/shard_map/wgrad/pallas_call | solution.py:343
  83.1 2.0 %collective-permute-start.30 = (f32[27,32,128]{2,1,0:T(8,128)S(1)}, f32[27,32,128]{2,1,0:T(8,128)S(1)}, u32[]{:S(2)}, u32[]{:S(2)}) collective-permute-start(f32[27,32,128]{2,1,0:T(8,128)S(1)} %get-tuple-element.74), channel_id=1, source_target_pairs={{0,8},{8,0},{16,24},{24,16},{32,40},{40,32},{48,56},{56,48},{64,72... | collective-permute-start | bytes 1327112 | tf_op jit(solution)/shard_map/ppermute | solution.py:33
  85.4 1.8 %collective-permute-start.29 = (f16[2,144,128]{2,1,0:T(8,128)(2,1)S(1)}, f16[2,144,128]{2,1,0:T(8,128)(2,1)S(1)}, u32[]{:S(2)}, u32[]{:S(2)}) collective-permute-start(f16[2,144,128]{2,1,0:T(8,128)(2,1)S(1)} %get-tuple-element.97), channel_id=1, source_target_pairs={{0,48},{8,56},{16,0},{24,8},{32,16},{40,24},{48,32},{56,40},{64,11... | collective-permute-start | bytes 221192 | tf_op jit(solution)/shard_map/ppermute | solution.py:33
  87.3 1.5 %collective-permute-start.28 = (f16[2,144,128]{2,1,0:T(8,128)(2,1)S(1)}, f16[2,144,128]{2,1,0:T(8,128)(2,1)S(1)}, u32[]{:S(2)}, u32[]{:S(2)}) collective-permute-start(f16[2,144,128]{2,1,0:T(8,128)(2,1)S(1)} %get-tuple-element.98), channel_id=1, source_target_pairs={{0,32},{8,40},{16,48},{24,56},{32,0},{40,8},{48,16},{56,24},{64,96... | collective-permute-start | bytes 221192 | tf_op jit(solution)/shard_map/ppermute | solution.py:33
  88.8 0.8 collective-permute-start.27
  89.9 2.2 %collective-permute-start.22 = (f16[2,144,128]{2,1,0:T(8,128)(2,1)S(1)}, f16[2,144,128]{2,1,0:T(8,128)(2,1)S(1)}, u32[]{:S(2)}, u32[]{:S(2)}) collective-permute-start(f16[2,144,128]{2,1,0:T(8,128)(2,1)S(1)} %get-tuple-element.100), channel_id=1, source_target_pairs={{0,192},{8,200},{16,208},{24,216},{32,224},{40,232},{48,240},{56,2... | collective-permute-start | bytes 221192 | tf_op jit(solution)/shard_map/ppermute | solution.py:33
  92.2 0.7 collective-permute-start.21
  92.9 0.8 collective-permute-start.20
  93.7 0.8 collective-permute-done.27
  94.6 2.4 %collective-permute-done.21 = f16[2,144,128]{2,1,0:T(8,128)(2,1)S(1)} collective-permute-done((f16[2,144,128]{2,1,0:T(8,128)(2,1)S(1)}, f16[2,144,128]{2,1,0:T(8,128)(2,1)S(1)}, u32[]{:S(2)}, u32[]{:S(2)}) %collective-permute-start.21) | collective-permute-done | bytes 73760 | tf_op jit(solution)/shard_map/ppermute | solution.py:33
  96.9 1.1 %collective-permute-done.20 = f16[2,144,128]{2,1,0:T(8,128)(2,1)S(1)} collective-permute-done((f16[2,144,128]{2,1,0:T(8,128)(2,1)S(1)}, f16[2,144,128]{2,1,0:T(8,128)(2,1)S(1)}, u32[]{:S(2)}, u32[]{:S(2)}) %collective-permute-start.20) | collective-permute-done | bytes 73760 | tf_op jit(solution)/shard_map/ppermute | solution.py:33
  98.1 0.8 add_multiply_fusion
  98.9 0.7 last.1
  99.6 2.0 %collective-permute-start.31 = (bf16[4,64,128]{2,1,0:T(8,128)(2,1)S(1)}, bf16[4,64,128]{2,1,0:T(8,128)(2,1)S(1)}, u32[]{:S(2)}, u32[]{:S(2)}) collective-permute-start(bf16[4,64,128]{2,1,0:T(8,128)(2,1)S(1)} %get-tuple-element.84), channel_id=1, source_target_pairs={{0,8},{8,0},{16,24},{24,16},{32,40},{40,32},{48,56},{56,48},{64,72... | collective-permute-start | bytes 196616 | tf_op jit(solution)/shard_map/ppermute | solution.py:33
  101.6 0.9 collective-permute-done.31
  102.5 0.7 fusion
  103.2 1.6 %convert_element_type.111 = bf16[1,32,2048]{2,1,0:T(8,128)(2,1)} convert(f32[1,32,2048]{2,1,0:T(8,128)} %reduce-scatter.2.cloned.1.call-done) | non-fusion elementwise | flops 65536 | bytes 393216 | tf_op jit(solution)/shard_map/convert_element_type | solution.py:297
  (70 shorter events, 5.8 us)
Async XLA Ops:
  7.2 24.3 %copy-start.1 = (bf16[27,32,128]{2,1,0:T(8,128)(2,1)S(1)}, bf16[27,32,128]{2,1,0:T(8,128)(2,1)}, u32[]{:S(2)}) copy-start(bf16[27,32,128]{2,1,0:T(8,128)(2,1)} %param.4) | copy-start | bytes 663556
  7.2 48.6 %all-gather.2.cloned.1.call-start = ((), (), s32[]{:S(2)}) async-start(), calls=%async_computation.1 | async-start | bytes 1179648 | tf_op jit(solution)/shard_map/all_gather | solution.py:240
  7.9 95.3 %reduce-scatter.2.cloned.1.call-start = ((), (), s32[]{:S(2)}) async-start(), calls=%async_computation.2 | async-start | bytes 2359296 | tf_op jit(solution)/shard_map/reduce_scatter | solution.py:297
  8.9 4.2 %collective-permute-start = (bf16[4,64,128]{2,1,0:T(8,128)(2,1)S(1)}, bf16[4,64,128]{2,1,0:T(8,128)(2,1)S(1)}, u32[]{:S(2)}, u32[]{:S(2)}) collective-permute-start(bf16[4,64,128]{2,1,0:T(8,128)(2,1)S(1)} %get-tuple-element.106), channel_id=1, source_target_pairs={{0,8},{8,0},{16,24},{24,16},{32,40},{40,32},{48,56},{56,48},{64,72... | collective-permute-start | bytes 196616 | tf_op jit(solution)/shard_map/ppermute | solution.py:33
  13.2 5.1 %collective-permute-start.6 = (bf16[2,128,128]{2,1,0:T(8,128)(2,1)S(1)}, bf16[2,128,128]{2,1,0:T(8,128)(2,1)S(1)}, u32[]{:S(2)}, u32[]{:S(2)}) collective-permute-start(bf16[2,128,128]{2,1,0:T(8,128)(2,1)S(1)} %get-tuple-element.50), channel_id=1, source_target_pairs={{0,192},{8,200},{16,208},{24,216},{32,224},{40,232},{48,240},{56,2... | collective-permute-start | bytes 196616 | tf_op jit(solution)/shard_map/ppermute | solution.py:33
  14.2 4.7 %collective-permute-start.5 = (bf16[2,128,128]{2,1,0:T(8,128)(2,1)S(1)}, bf16[2,128,128]{2,1,0:T(8,128)(2,1)S(1)}, u32[]{:S(2)}, u32[]{:S(2)}) collective-permute-start(bf16[2,128,128]{2,1,0:T(8,128)(2,1)S(1)} %get-tuple-element.50), channel_id=1, source_target_pairs={{0,128},{8,136},{16,144},{24,152},{32,160},{40,168},{48,176},{56,1... | collective-permute-start | bytes 196616 | tf_op jit(solution)/shard_map/ppermute | solution.py:33
  14.6 5.8 %collective-permute-start.4 = (bf16[2,128,128]{2,1,0:T(8,128)(2,1)S(1)}, bf16[2,128,128]{2,1,0:T(8,128)(2,1)S(1)}, u32[]{:S(2)}, u32[]{:S(2)}) collective-permute-start(bf16[2,128,128]{2,1,0:T(8,128)(2,1)S(1)} %get-tuple-element.50), channel_id=1, source_target_pairs={{0,64},{8,72},{16,80},{24,88},{32,96},{40,104},{48,112},{56,120},{... | collective-permute-start | bytes 196616 | tf_op jit(solution)/shard_map/ppermute | solution.py:33
  15.3 5.1 %collective-permute-start.3 = (bf16[2,128,128]{2,1,0:T(8,128)(2,1)S(1)}, bf16[2,128,128]{2,1,0:T(8,128)(2,1)S(1)}, u32[]{:S(2)}, u32[]{:S(2)}) collective-permute-start(bf16[2,128,128]{2,1,0:T(8,128)(2,1)S(1)} %get-tuple-element.46), channel_id=1, source_target_pairs={{0,48},{8,56},{16,0},{24,8},{32,16},{40,24},{48,32},{56,40},{64,11... | collective-permute-start | bytes 196616 | tf_op jit(solution)/shard_map/ppermute | solution.py:33
  17.8 4.7 %collective-permute-start.2 = (bf16[2,128,128]{2,1,0:T(8,128)(2,1)S(1)}, bf16[2,128,128]{2,1,0:T(8,128)(2,1)S(1)}, u32[]{:S(2)}, u32[]{:S(2)}) collective-permute-start(bf16[2,128,128]{2,1,0:T(8,128)(2,1)S(1)} %get-tuple-element.46), channel_id=1, source_target_pairs={{0,32},{8,40},{16,48},{24,56},{32,0},{40,8},{48,16},{56,24},{64,96... | collective-permute-start | bytes 196616 | tf_op jit(solution)/shard_map/ppermute | solution.py:33
  18.3 4.8 %collective-permute-start.1 = (bf16[2,128,128]{2,1,0:T(8,128)(2,1)S(1)}, bf16[2,128,128]{2,1,0:T(8,128)(2,1)S(1)}, u32[]{:S(2)}, u32[]{:S(2)}) collective-permute-start(bf16[2,128,128]{2,1,0:T(8,128)(2,1)S(1)} %get-tuple-element.46), channel_id=1, source_target_pairs={{0,16},{8,24},{16,32},{24,40},{32,48},{40,56},{48,0},{56,8},{64,80... | collective-permute-start | bytes 196616 | tf_op jit(solution)/shard_map/ppermute | solution.py:33
  23.1 7.5 %collective-permute-start.9 = (bf16[4,2,128,128]{3,2,1,0:T(8,128)(2,1)S(1)}, bf16[4,2,128,128]{3,2,1,0:T(8,128)(2,1)S(1)}, u32[]{:S(2)}, u32[]{:S(2)}) collective-permute-start(bf16[4,2,128,128]{3,2,1,0:T(8,128)(2,1)S(1)} %get-tuple-element.54.refs_0_), channel_id=1, source_target_pairs={{0,192},{8,200},{16,208},{24,216},{32,224},{40,232},{48,240},{56,2... | collective-permute-start | bytes 786440 | tf_op jit(solution)/shard_map/ppermute | solution.py:33
  25.2 4.6 %collective-permute-start.10 = (bf16[27,32,128]{2,1,0:T(8,128)(2,1)}, bf16[27,32,128]{2,1,0:T(8,128)(2,1)S(1)}, u32[]{:S(2)}, u32[]{:S(2)}) collective-permute-start(bf16[27,32,128]{2,1,0:T(8,128)(2,1)} %param.4), channel_id=1, source_target_pairs={{0,8},{8,0},{16,24},{24,16},{32,40},{40,32},{48,56},{56,48},{64,72... | collective-permute-start | bytes 663560 | tf_op jit(solution)/shard_map/ppermute | solution.py:33
  28.1 9.5 %collective-permute-start.8 = (bf16[4,2,128,128]{3,2,1,0:T(8,128)(2,1)S(1)}, bf16[4,2,128,128]{3,2,1,0:T(8,128)(2,1)S(1)}, u32[]{:S(2)}, u32[]{:S(2)}) collective-permute-start(bf16[4,2,128,128]{3,2,1,0:T(8,128)(2,1)S(1)} %get-tuple-element.54.refs_0_), channel_id=1, source_target_pairs={{0,128},{8,136},{16,144},{24,152},{32,160},{40,168},{48,176},{56,1... | collective-permute-start | bytes 786440 | tf_op jit(solution)/shard_map/ppermute | solution.py:33
  29.5 14.0 %collective-permute-start.7 = (bf16[4,2,128,128]{3,2,1,0:T(8,128)(2,1)S(1)}, bf16[4,2,128,128]{3,2,1,0:T(8,128)(2,1)S(1)}, u32[]{:S(2)}, u32[]{:S(2)}) collective-permute-start(bf16[4,2,128,128]{3,2,1,0:T(8,128)(2,1)S(1)} %get-tuple-element.54.refs_0_), channel_id=1, source_target_pairs={{0,64},{8,72},{16,80},{24,88},{32,96},{40,104},{48,112},{56,120},{... | collective-permute-start | bytes 786440 | tf_op jit(solution)/shard_map/ppermute | solution.py:33
  29.5 20.3 %collective-permute-start.14 = (bf16[4,2,128,128]{3,2,1,0:T(8,128)(2,1)S(1)}, bf16[4,2,128,128]{3,2,1,0:T(8,128)(2,1)S(1)}, u32[]{:S(2)}, u32[]{:S(2)}) collective-permute-start(bf16[4,2,128,128]{3,2,1,0:T(8,128)(2,1)S(1)} %get-tuple-element.56.refs_0_), channel_id=1, source_target_pairs={{0,48},{8,56},{16,0},{24,8},{32,16},{40,24},{48,32},{56,40},{64,11... | collective-permute-start | bytes 786440 | tf_op jit(solution)/shard_map/ppermute | solution.py:33
  29.8 20.0 %collective-permute-start.13 = (bf16[4,2,128,128]{3,2,1,0:T(8,128)(2,1)S(1)}, bf16[4,2,128,128]{3,2,1,0:T(8,128)(2,1)S(1)}, u32[]{:S(2)}, u32[]{:S(2)}) collective-permute-start(bf16[4,2,128,128]{3,2,1,0:T(8,128)(2,1)S(1)} %get-tuple-element.56.refs_0_), channel_id=1, source_target_pairs={{0,32},{8,40},{16,48},{24,56},{32,0},{40,8},{48,16},{56,24},{64,96... | collective-permute-start | bytes 786440 | tf_op jit(solution)/shard_map/ppermute | solution.py:33
  30.7 19.2 %collective-permute-start.12 = (bf16[4,2,128,128]{3,2,1,0:T(8,128)(2,1)S(1)}, bf16[4,2,128,128]{3,2,1,0:T(8,128)(2,1)S(1)}, u32[]{:S(2)}, u32[]{:S(2)}) collective-permute-start(bf16[4,2,128,128]{3,2,1,0:T(8,128)(2,1)S(1)} %get-tuple-element.56.refs_0_), channel_id=1, source_target_pairs={{0,16},{8,24},{16,32},{24,40},{32,48},{40,56},{48,0},{56,8},{64,80... | collective-permute-start | bytes 786440 | tf_op jit(solution)/shard_map/ppermute | solution.py:33
  49.3 7.5 %collective-permute-start.11 = (f32[2,32,2048]{2,1,0:T(8,128)}, f32[2,32,2048]{2,1,0:T(8,128)S(1)}, u32[]{:S(2)}, u32[]{:S(2)}) collective-permute-start(f32[2,32,2048]{2,1,0:T(8,128)} %get-tuple-element.55), channel_id=1, source_target_pairs={{0,8},{8,0},{16,24},{24,16},{32,40},{40,32},{48,56},{56,48},{64,72... | collective-permute-start | bytes 1572872 | tf_op jit(solution)/shard_map/ppermute | solution.py:33
  55.8 2.1 %collective-permute-start.15 = (f32[2,32,2048]{2,1,0:T(8,128)}, f32[2,32,2048]{2,1,0:T(8,128)S(1)}, u32[]{:S(2)}, u32[]{:S(2)}) collective-permute-start(f32[2,32,2048]{2,1,0:T(8,128)} %get-tuple-element.58), channel_id=1, source_target_pairs={{0,8},{8,0},{16,24},{24,16},{32,40},{40,32},{48,56},{56,48},{64,72... | collective-permute-start | bytes 1572872 | tf_op jit(solution)/shard_map/ppermute | solution.py:33
  58.7 2.5 %copy-start = (bf16[8,32,2048]{2,1,0:T(8,128)(2,1)S(1)}, bf16[8,32,2048]{2,1,0:T(8,128)(2,1)}, u32[]{:S(2)}) copy-start(bf16[8,32,2048]{2,1,0:T(8,128)(2,1)} %all-gather.2.cloned.1.call-done.own_ref) | copy-start | bytes 3145732
  59.6 1.6 %collective-permute-start.23 = (bf16[2,32,2048]{2,1,0:T(8,128)(2,1)S(1)}, bf16[2,32,2048]{2,1,0:T(8,128)(2,1)S(1)}, u32[]{:S(2)}, u32[]{:S(2)}) collective-permute-start(bf16[2,32,2048]{2,1,0:T(8,128)(2,1)S(1)} %get-tuple-element.64), channel_id=1, source_target_pairs={{0,8},{8,0},{16,24},{24,16},{32,40},{40,32},{48,56},{56,48},{64,72... | collective-permute-start | bytes 786440 | tf_op jit(solution)/shard_map/ppermute | solution.py:33
  60.2 8.2 %collective-permute-start.16 = (bf16[2,32,2048]{2,1,0:T(8,128)(2,1)S(1)}, bf16[2,32,2048]{2,1,0:T(8,128)(2,1)S(1)}, u32[]{:S(2)}, u32[]{:S(2)}) collective-permute-start(bf16[2,32,2048]{2,1,0:T(8,128)(2,1)S(1)} %get-tuple-element.59), channel_id=1, source_target_pairs={{0,8},{8,0},{16,24},{24,16},{32,40},{40,32},{48,56},{56,48},{64,72... | collective-permute-start | bytes 786440 | tf_op jit(solution)/shard_map/ppermute | solution.py:33
  66.0 8.4 %collective-permute-start.26 = (f16[2,528,128]{2,1,0:T(8,128)(2,1)S(1)}, f16[2,528,128]{2,1,0:T(8,128)(2,1)S(1)}, u32[]{:S(2)}, u32[]{:S(2)}) collective-permute-start(f16[2,528,128]{2,1,0:T(8,128)(2,1)S(1)} %get-tuple-element.91), channel_id=1, source_target_pairs={{0,192},{8,200},{16,208},{24,216},{32,224},{40,232},{48,240},{56,2... | collective-permute-start | bytes 811016 | tf_op jit(solution)/shard_map/ppermute | solution.py:33
  66.4 16.6 %collective-permute-start.25 = (f16[2,528,128]{2,1,0:T(8,128)(2,1)S(1)}, f16[2,528,128]{2,1,0:T(8,128)(2,1)S(1)}, u32[]{:S(2)}, u32[]{:S(2)}) collective-permute-start(f16[2,528,128]{2,1,0:T(8,128)(2,1)S(1)} %get-tuple-element.92), channel_id=1, source_target_pairs={{0,128},{8,136},{16,144},{24,152},{32,160},{40,168},{48,176},{56,1... | collective-permute-start | bytes 811016 | tf_op jit(solution)/shard_map/ppermute | solution.py:33
  67.8 17.3 %collective-permute-start.24 = (f16[2,528,128]{2,1,0:T(8,128)(2,1)S(1)}, f16[2,528,128]{2,1,0:T(8,128)(2,1)S(1)}, u32[]{:S(2)}, u32[]{:S(2)}) collective-permute-start(f16[2,528,128]{2,1,0:T(8,128)(2,1)S(1)} %get-tuple-element.93), channel_id=1, source_target_pairs={{0,64},{8,72},{16,80},{24,88},{32,96},{40,104},{48,112},{56,120},{... | collective-permute-start | bytes 811016 | tf_op jit(solution)/shard_map/ppermute | solution.py:33
  73.2 14.1 %collective-permute-start.19 = (f16[2,528,128]{2,1,0:T(8,128)(2,1)S(1)}, f16[2,528,128]{2,1,0:T(8,128)(2,1)S(1)}, u32[]{:S(2)}, u32[]{:S(2)}) collective-permute-start(f16[2,528,128]{2,1,0:T(8,128)(2,1)S(1)} %get-tuple-element.94), channel_id=1, source_target_pairs={{0,48},{8,56},{16,0},{24,8},{32,16},{40,24},{48,32},{56,40},{64,11... | collective-permute-start | bytes 811016 | tf_op jit(solution)/shard_map/ppermute | solution.py:33
  73.5 15.2 %collective-permute-start.18 = (f16[2,528,128]{2,1,0:T(8,128)(2,1)S(1)}, f16[2,528,128]{2,1,0:T(8,128)(2,1)S(1)}, u32[]{:S(2)}, u32[]{:S(2)}) collective-permute-start(f16[2,528,128]{2,1,0:T(8,128)(2,1)S(1)} %get-tuple-element.95), channel_id=1, source_target_pairs={{0,32},{8,40},{16,48},{24,56},{32,0},{40,8},{48,16},{56,24},{64,96... | collective-permute-start | bytes 811016 | tf_op jit(solution)/shard_map/ppermute | solution.py:33
  74.4 15.3 %collective-permute-start.17 = (f16[2,528,128]{2,1,0:T(8,128)(2,1)S(1)}, f16[2,528,128]{2,1,0:T(8,128)(2,1)S(1)}, u32[]{:S(2)}, u32[]{:S(2)}) collective-permute-start(f16[2,528,128]{2,1,0:T(8,128)(2,1)S(1)} %get-tuple-element.96), channel_id=1, source_target_pairs={{0,16},{8,24},{16,32},{24,40},{32,48},{40,56},{48,0},{56,8},{64,80... | collective-permute-start | bytes 811016 | tf_op jit(solution)/shard_map/ppermute | solution.py:33
  83.1 15.0 %collective-permute-start.30 = (f32[27,32,128]{2,1,0:T(8,128)S(1)}, f32[27,32,128]{2,1,0:T(8,128)S(1)}, u32[]{:S(2)}, u32[]{:S(2)}) collective-permute-start(f32[27,32,128]{2,1,0:T(8,128)S(1)} %get-tuple-element.74), channel_id=1, source_target_pairs={{0,8},{8,0},{16,24},{24,16},{32,40},{40,32},{48,56},{56,48},{64,72... | collective-permute-start | bytes 1327112 | tf_op jit(solution)/shard_map/ppermute | solution.py:33
  85.4 6.8 %collective-permute-start.29 = (f16[2,144,128]{2,1,0:T(8,128)(2,1)S(1)}, f16[2,144,128]{2,1,0:T(8,128)(2,1)S(1)}, u32[]{:S(2)}, u32[]{:S(2)}) collective-permute-start(f16[2,144,128]{2,1,0:T(8,128)(2,1)S(1)} %get-tuple-element.97), channel_id=1, source_target_pairs={{0,48},{8,56},{16,0},{24,8},{32,16},{40,24},{48,32},{56,40},{64,11... | collective-permute-start | bytes 221192 | tf_op jit(solution)/shard_map/ppermute | solution.py:33
  87.3 5.6 %collective-permute-start.28 = (f16[2,144,128]{2,1,0:T(8,128)(2,1)S(1)}, f16[2,144,128]{2,1,0:T(8,128)(2,1)S(1)}, u32[]{:S(2)}, u32[]{:S(2)}) collective-permute-start(f16[2,144,128]{2,1,0:T(8,128)(2,1)S(1)} %get-tuple-element.98), channel_id=1, source_target_pairs={{0,32},{8,40},{16,48},{24,56},{32,0},{40,8},{48,16},{56,24},{64,96... | collective-permute-start | bytes 221192 | tf_op jit(solution)/shard_map/ppermute | solution.py:33
  88.8 5.7 %collective-permute-start.27 = (f16[2,144,128]{2,1,0:T(8,128)(2,1)S(1)}, f16[2,144,128]{2,1,0:T(8,128)(2,1)S(1)}, u32[]{:S(2)}, u32[]{:S(2)}) collective-permute-start(f16[2,144,128]{2,1,0:T(8,128)(2,1)S(1)} %get-tuple-element.99), channel_id=1, source_target_pairs={{0,16},{8,24},{16,32},{24,40},{32,48},{40,56},{48,0},{56,8},{64,80... | collective-permute-start | bytes 221192 | tf_op jit(solution)/shard_map/ppermute | solution.py:33
  89.9 4.6 %collective-permute-start.22 = (f16[2,144,128]{2,1,0:T(8,128)(2,1)S(1)}, f16[2,144,128]{2,1,0:T(8,128)(2,1)S(1)}, u32[]{:S(2)}, u32[]{:S(2)}) collective-permute-start(f16[2,144,128]{2,1,0:T(8,128)(2,1)S(1)} %get-tuple-element.100), channel_id=1, source_target_pairs={{0,192},{8,200},{16,208},{24,216},{32,224},{40,232},{48,240},{56,2... | collective-permute-start | bytes 221192 | tf_op jit(solution)/shard_map/ppermute | solution.py:33
  92.2 4.7 %collective-permute-start.21 = (f16[2,144,128]{2,1,0:T(8,128)(2,1)S(1)}, f16[2,144,128]{2,1,0:T(8,128)(2,1)S(1)}, u32[]{:S(2)}, u32[]{:S(2)}) collective-permute-start(f16[2,144,128]{2,1,0:T(8,128)(2,1)S(1)} %get-tuple-element.101), channel_id=1, source_target_pairs={{0,128},{8,136},{16,144},{24,152},{32,160},{40,168},{48,176},{56,1... | collective-permute-start | bytes 221192 | tf_op jit(solution)/shard_map/ppermute | solution.py:33
  92.9 5.2 %collective-permute-start.20 = (f16[2,144,128]{2,1,0:T(8,128)(2,1)S(1)}, f16[2,144,128]{2,1,0:T(8,128)(2,1)S(1)}, u32[]{:S(2)}, u32[]{:S(2)}) collective-permute-start(f16[2,144,128]{2,1,0:T(8,128)(2,1)S(1)} %get-tuple-element.102), channel_id=1, source_target_pairs={{0,64},{8,72},{16,80},{24,88},{32,96},{40,104},{48,112},{56,120},{... | collective-permute-start | bytes 221192 | tf_op jit(solution)/shard_map/ppermute | solution.py:33
  99.6 2.9 %collective-permute-start.31 = (bf16[4,64,128]{2,1,0:T(8,128)(2,1)S(1)}, bf16[4,64,128]{2,1,0:T(8,128)(2,1)S(1)}, u32[]{:S(2)}, u32[]{:S(2)}) collective-permute-start(bf16[4,64,128]{2,1,0:T(8,128)(2,1)S(1)} %get-tuple-element.84), channel_id=1, source_target_pairs={{0,8},{8,0},{16,24},{24,16},{32,40},{40,32},{48,56},{56,48},{64,72... | collective-permute-start | bytes 196616 | tf_op jit(solution)/shard_map/ppermute | solution.py:33
Sparse Core Ops, SparseCore 0:
  9.8 38.1 all-gather.1
  59.7 37.2 reduce-scatter.1

commit v4 on v3

--- a/solution.py
+++ b/solution.py
@@ -20,6 +20,7 @@
 in_plane = [(b, c) for b in (-1, 0, 1) for c in (-1, 0, 1)]
 VMEM_LIMIT = 24 * 1024 * 1024
 NOTE = 16
+CHUNKS = 2
 TINY = 1e-32
 
 
@@ -190,16 +191,18 @@
 
 def wgrad_kernel(place, cols_a, cols_b, taps_a, taps_b, own_ref, other_ref, acc):
     ci, co = own_ref.shape[1:]
-    n = pl.program_id(0)
-
-    @pl.when(n == 0)
+    n, k = pl.program_id(0), pl.program_id(1)
+    depth = taps_a.shape[1]
+    lanes = pl.ds(pl.multiple_of(k * depth, depth), depth)
+
+    @pl.when((n == 0) & (k == 0))
     def _():
         acc[...] = jnp.zeros_like(acc)
 
-    acc[...] += jnp.dot(cols_a[n], taps_a[0], preferred_element_type=F32)
-    acc[...] += jnp.dot(cols_b[n], taps_b[0], preferred_element_type=F32)
-
-    @pl.when(n == pl.num_programs(0) - 1)
+    acc[...] += jnp.dot(cols_a[n, :, lanes], taps_a[0], preferred_element_type=F32)
+    acc[...] += jnp.dot(cols_b[n, :, lanes], taps_b[0], preferred_element_type=F32)
+
+    @pl.when((n == pl.num_programs(0) - 1) & (k == pl.num_programs(1) - 1))
     def _():
         for tap in range(27):
             first, column = tap % 9 * 2 * ci, tap // 9 * co
@@ -209,8 +212,21 @@
             other_ref[tap] = jnp.where(place[2] == 0, high, low)
 
 
+def place_kernel(place, _, term_a, term_b, terms, sems):
+    pairs = term_a.shape[0]
+    first = (1 - place[2]) * 2 * pairs
+    copies = [
+        pltpu.make_async_copy(term, terms.at[pl.ds(first + half * pairs, pairs)], sems.at[half])
+        for half, term in enumerate((term_a, term_b))
+    ]
+    for copy in copies:
+        copy.start()
+    for copy in copies:
+        copy.wait()
+
+
 def whole(shape):
-    return pl.BlockSpec(shape, lambda *_: (0,) * len(shape))
+    return pl.BlockSpec(memory_space=pltpu.VMEM)
 
 
 def per_sample(shape):
@@ -292,8 +308,20 @@
     samples = [taken(gathered, (1 - core) * 2 + half, pairs, 0) for half in range(2)]
     samples, term_a, term_b = lax.optimization_barrier((samples, term_a, term_b))
     samples = [swap_cores(sample) for sample in samples]
-    terms = lax.dynamic_update_slice_in_dim(terms, term_a, (1 - core) * mine, 0)
-    terms = lax.dynamic_update_slice_in_dim(terms, term_b, (1 - core) * mine + pairs, 0)
+    terms = pl.pallas_call(
+        place_kernel,
+        grid_spec=pltpu.PrefetchScalarGridSpec(
+            num_scalar_prefetch=1,
+            grid=(1,),
+            in_specs=[pl.BlockSpec(memory_space=pl.ANY)] * 3,
+            out_specs=pl.BlockSpec(memory_space=pl.ANY),
+            scratch_shapes=[pltpu.SemaphoreType.DMA((2,))],
+        ),
+        out_shape=pltpu.HBM(terms.shape, F32),
+        input_output_aliases={1: 0},
+        compiler_params=params,
+        name="place",
+    )(place, terms, term_a, term_b)
     grad_input = lax.psum_scatter(terms, "cout", scatter_dimension=0, tiled=True).astype(BF16)
 
     rows = SIDE * co + NOTE
@@ -344,8 +372,9 @@
         wgrad_kernel,
         grid_spec=pltpu.PrefetchScalarGridSpec(
             num_scalar_prefetch=1,
-            grid=(pairs,),
-            in_specs=[pl.BlockSpec(memory_space=pltpu.VMEM)] * 2 + [per_sample((cells, 3 * co))] * 2,
+            grid=(pairs, CHUNKS),
+            in_specs=[pl.BlockSpec(memory_space=pltpu.VMEM)] * 2
+            + [pl.BlockSpec((1, cells // CHUNKS, 3 * co), lambda n, k, *_: (n, k, 0))] * 2,
             out_specs=[whole((27, ci, co))] * 2,
             scratch_shapes=[pltpu.VMEM((9 * 2 * ci, 3 * co), F32)],
         ),
@@ -367,7 +396,8 @@
         compiler_params=params,
         name="last",
     )(place, *ends)
-    output = jnp.transpose(in_order(own, swap_cores(other), 0), (0, 2, 1))
+    got, grad_input = lax.optimization_barrier((swap_cores(other), grad_input))
+    output = jnp.transpose(in_order(own, got, 0), (0, 2, 1))
     return output, grad_input, grad_weight
 
 

time: 112 us -> 111 us (level)
  local copies, waits for them, and re-layouts: 4.71 us -> 3.03 us
  Pallas kernels: 29.6 us -> 31 us
    dynamic_update_slice x2 -> x0, local copies, waits for them, and re-layouts: 1.68 us -> none  [the longest x1 0.84 us: body(): lax.dynamic_update_slice_in_dim(terms, term_b, (1 - core) * mine + pairs, 0)]
    pallas_call x0 -> x1, Pallas kernels: none -> 1.53 us  [body(): pl.pallas_call(place_kernel, grid_spec=pltpu.PrefetchScalarGridSpec(num_s...]
  transfers between devices with their start and end apart: 34 -> 34, of which waited for: 12 -> 11; matrix products, arithmetic and copies ran while one was open for 5% -> 6% of each run, Pallas kernels for 27% -> 27%
where the time goes in v4:
time: 111 us; the launch traced here: 110 us
  starting transfers between devices  34.7 us (31%)
  Pallas kernels  31 us (28%)
  waiting for transfers between devices  23 us (21%)
  between operations  14.4 us (13%)
  other arithmetic  4.3 us (4%)
  local copies, waits for them, and re-layouts  3.03 us (3%)
    ppermute x32, starting transfers between devices, move_xy(): return lax.ppermute(value, 'cin', pairs)  34.6 us
    ppermute x32, waiting for transfers between devices, move_xy(): return lax.ppermute(value, 'cin', pairs)  22.3 us
    pallas_call x2, Pallas kernels, dgrad(): pl.pallas_call(functools.partial(dgrad_kernel, half), grid_spec=pltpu.Pre...  11.8 us
    pallas_call x2, Pallas kernels, forward(): pl.pallas_call(functools.partial(fwd_kernel, half), grid_spec=pltpu.Prefe...  9.02 us
    pallas_call x1, Pallas kernels, body(): pl.pallas_call(wgrad_kernel, grid_spec=pltpu.PrefetchScalarGridSpec(num_s...  7.7 us
  transfers between devices with their start and end apart: 34, of which 11 were waited for; matrix products, arithmetic and copies ran while one was open for 6% of the time, Pallas kernels for 27%

profile of v4, /device:TPU:1, one launch (start us, length us, event | category | flops | bytes accessed | tf_op | source)
XLA Modules:
  0.0 110.4 jit_solution(5397921507679126210)
XLA Ops:
  7.2 0.7 all-gather.2.cloned.1.call-update
  8.0 0.9 dynamic-slice_bitcast_fusion.1
  8.9 3.3 %collective-permute-start = (bf16[4,64,128]{2,1,0:T(8,128)(2,1)S(1)}, bf16[4,64,128]{2,1,0:T(8,128)(2,1)S(1)}, u32[]{:S(2)}, u32[]{:S(2)}) collective-permute-start(bf16[4,64,128]{2,1,0:T(8,128)(2,1)S(1)} %get-tuple-element.110), channel_id=1, source_target_pairs={{0,8},{8,0},{16,24},{24,16},{32,40},{40,32},{48,56},{56,48},{64,72... | collective-permute-start | bytes 196616 | tf_op jit(solution)/shard_map/ppermute | solution.py:34
  12.2 0.9 collective-permute-done
  13.2 1.1 collective-permute-start.6
  14.6 0.7 collective-permute-start.4
  15.3 2.5 %collective-permute-start.3 = (bf16[2,128,128]{2,1,0:T(8,128)(2,1)S(1)}, bf16[2,128,128]{2,1,0:T(8,128)(2,1)S(1)}, u32[]{:S(2)}, u32[]{:S(2)}) collective-permute-start(bf16[2,128,128]{2,1,0:T(8,128)(2,1)S(1)} %get-tuple-element.48), channel_id=1, source_target_pairs={{0,48},{8,56},{16,0},{24,8},{32,16},{40,24},{48,32},{56,40},{64,11... | collective-permute-start | bytes 196616 | tf_op jit(solution)/shard_map/ppermute | solution.py:34
  17.8 0.5 collective-permute-start.2
  18.3 0.6 collective-permute-start.1
  18.9 1.4 %collective-permute-done.4 = bf16[2,128,128]{2,1,0:T(8,128)(2,1)S(1)} collective-permute-done((bf16[2,128,128]{2,1,0:T(8,128)(2,1)S(1)}, bf16[2,128,128]{2,1,0:T(8,128)(2,1)S(1)}, u32[]{:S(2)}, u32[]{:S(2)}) %collective-permute-start.4) | collective-permute-done | bytes 65568 | tf_op jit(solution)/shard_map/ppermute | solution.py:34
  20.3 2.1 %collective-permute-done.2 = bf16[2,128,128]{2,1,0:T(8,128)(2,1)S(1)} collective-permute-done((bf16[2,128,128]{2,1,0:T(8,128)(2,1)S(1)}, bf16[2,128,128]{2,1,0:T(8,128)(2,1)S(1)}, u32[]{:S(2)}, u32[]{:S(2)}) %collective-permute-start.2) | collective-permute-done | bytes 65568 | tf_op jit(solution)/shard_map/ppermute | solution.py:34
  22.4 0.7 collective-permute-done.1
  23.1 2.1 %collective-permute-start.9 = (bf16[4,2,128,128]{3,2,1,0:T(8,128)(2,1)S(1)}, bf16[4,2,128,128]{3,2,1,0:T(8,128)(2,1)S(1)}, u32[]{:S(2)}, u32[]{:S(2)}) collective-permute-start(bf16[4,2,128,128]{3,2,1,0:T(8,128)(2,1)S(1)} %get-tuple-element.56.refs_0_), channel_id=1, source_target_pairs={{0,192},{8,200},{16,208},{24,216},{32,224},{40,232},{48,240},{56,2... | collective-permute-start | bytes 786440 | tf_op jit(solution)/shard_map/ppermute | solution.py:34
  25.2 2.9 %collective-permute-start.10 = (bf16[27,32,128]{2,1,0:T(8,128)(2,1)}, bf16[27,32,128]{2,1,0:T(8,128)(2,1)S(1)}, u32[]{:S(2)}, u32[]{:S(2)}) collective-permute-start(bf16[27,32,128]{2,1,0:T(8,128)(2,1)} %param.4), channel_id=1, source_target_pairs={{0,8},{8,0},{16,24},{24,16},{32,40},{40,32},{48,56},{56,48},{64,72... | collective-permute-start | bytes 663560 | tf_op jit(solution)/shard_map/ppermute | solution.py:34
  28.1 1.4 %collective-permute-start.8 = (bf16[4,2,128,128]{3,2,1,0:T(8,128)(2,1)S(1)}, bf16[4,2,128,128]{3,2,1,0:T(8,128)(2,1)S(1)}, u32[]{:S(2)}, u32[]{:S(2)}) collective-permute-start(bf16[4,2,128,128]{3,2,1,0:T(8,128)(2,1)S(1)} %get-tuple-element.56.refs_0_), channel_id=1, source_target_pairs={{0,128},{8,136},{16,144},{24,152},{32,160},{40,168},{48,176},{56,1... | collective-permute-start | bytes 786440 | tf_op jit(solution)/shard_map/ppermute | solution.py:34
  29.8 0.9 collective-permute-start.13
  30.7 0.8 collective-permute-start.12
  32.4 5.2 %collective-permute-done.8.refs_2_ = bf16[4,2,128,128]{3,2,1,0:T(8,128)(2,1)S(1)} collective-permute-done((bf16[4,2,128,128]{3,2,1,0:T(8,128)(2,1)S(1)}, bf16[4,2,128,128]{3,2,1,0:T(8,128)(2,1)S(1)}, u32[]{:S(2)}, u32[]{:S(2)}) %collective-permute-start.8) | collective-permute-done | bytes 262176 | tf_op jit(solution)/shard_map/ppermute | solution.py:34
  37.6 5.9 %collective-permute-done.7.refs_1_ = bf16[4,2,128,128]{3,2,1,0:T(8,128)(2,1)S(1)} collective-permute-done((bf16[4,2,128,128]{3,2,1,0:T(8,128)(2,1)S(1)}, bf16[4,2,128,128]{3,2,1,0:T(8,128)(2,1)S(1)}, u32[]{:S(2)}, u32[]{:S(2)}) %collective-permute-start.7) | collective-permute-done | bytes 262176 | tf_op jit(solution)/shard_map/ppermute | solution.py:34
  43.5 5.9 %dgrad.2 = (bf16[2,2048,384]{2,1,0:T(8,128)(2,1)}, f32[8,32,2048]{2,1,0:T(8,128)}, f32[2,32,2048]{2,1,0:T(8,128)}) custom-call(s32[3]{0:T(128)S(1)} %pad_add_fusion.place, bf16[4,2,128,128]{3,2,1,0:T(8,128)(2,1)S(1)} %get-tuple-element.56.refs_0_, bf16[4,2,128,128]{3,2,1,0:T(8,128)(2,1)S(1)} %collective-permute-done.7.refs_1_, ...), custom_call_target="tpu_custom_call" | custom-call | tf_op jit(solution)/shard_map/dgrad/pallas_call | solution.py:281
  49.3 0.5 collective-permute-start.11
  49.8 5.9 %dgrad.3 = (bf16[2,2048,384]{2,1,0:T(8,128)(2,1)}, f32[8,32,2048]{2,1,0:T(8,128)}, f32[2,32,2048]{2,1,0:T(8,128)}) custom-call(s32[3]{0:T(128)S(1)} %pad_add_fusion.place, bf16[4,2,128,128]{3,2,1,0:T(8,128)(2,1)S(1)} %get-tuple-element.58.refs_0_, bf16[4,2,128,128]{3,2,1,0:T(8,128)(2,1)S(1)} %collective-permute-done.12.refs_1_, ...), custom_call_target="tpu_custom_call", output_to_operand_aliasing={{1}: (6, {})} | custom-call | tf_op jit(solution)/shard_map/dgrad/pallas_call | solution.py:281
  55.8 1.1 constant_dynamic-slice_fusion
  56.8 1.0 collective-permute-done.15.term_b
  57.9 1.5 %place.1 = f32[8,32,2048]{2,1,0:T(8,128)} custom-call(s32[3]{0:T(128)S(1)} %pad_add_fusion.place, f32[8,32,2048]{2,1,0:T(8,128)} %get-tuple-element.87._, f32[2,32,2048]{2,1,0:T(8,128)S(1)} %collective-permute-done.11.term_a, f32[2,32,2048]{2,1,0:T(8,128)S(1)} %collective-permute-done.15.term_b), custom_call_target="tpu_custom_call", output_to_operand_aliasing={{}: (1, {})} | custom-call | tf_op jit(solution)/shard_map/place/pallas_call | solution.py:311
  60.4 0.7 collective-permute-done.23.other_ref
  61.1 4.5 %forward.3 = (bf16[2,576,2048]{2,1,0:T(8,128)(2,1)S(1)}, f32[3,2,528,128]{3,2,1,0:T(8,128)S(1)}, f32[2,528,128]{2,1,0:T(8,128)S(1)}) custom-call(s32[3]{0:T(128)S(1)} %pad_add_fusion.place, bf16[8,32,2048]{2,1,0:T(8,128)(2,1)S(1)} %copy-done, bf16[2,32,2048]{2,1,0:T(8,128)(2,1)S(1)} %collective-permute-done.23.other_ref, bf16[384,576]{1,0:T(8,128)(2,1)S(1)} %bitcast.53), custom_call_target="tpu_custom_call" | custom-call | tf_op jit(solution)/shard_map/forward/pallas_call | solution.py:332
  66.3 1.4 %collective-permute-start.25 = (f16[2,528,128]{2,1,0:T(8,128)(2,1)S(1)}, f16[2,528,128]{2,1,0:T(8,128)(2,1)S(1)}, u32[]{:S(2)}, u32[]{:S(2)}) collective-permute-start(f16[2,528,128]{2,1,0:T(8,128)(2,1)S(1)} %get-tuple-element.96), channel_id=1, source_target_pairs={{0,128},{8,136},{16,144},{24,152},{32,160},{40,168},{48,176},{56,1... | collective-permute-start | bytes 811016 | tf_op jit(solution)/shard_map/ppermute | solution.py:34
  67.7 0.5 collective-permute-start.24
  68.2 4.5 %forward.2 = (bf16[2,576,2048]{2,1,0:T(8,128)(2,1)S(1)}, f32[3,2,528,128]{3,2,1,0:T(8,128)S(1)}, f32[2,528,128]{2,1,0:T(8,128)S(1)}) custom-call(s32[3]{0:T(128)S(1)} %pad_add_fusion.place, bf16[8,32,2048]{2,1,0:T(8,128)(2,1)S(1)} %copy-done, bf16[2,32,2048]{2,1,0:T(8,128)(2,1)S(1)} %collective-permute-done.16.other_ref, bf16[384,576]{1,0:T(8,128)(2,1)S(1)} %bitcast.54), custom_call_target="tpu_custom_call" | custom-call | tf_op jit(solution)/shard_map/forward/pallas_call | solution.py:332
  73.4 0.9 collective-permute-start.18
  74.3 0.8 collective-permute-start.17
  75.0 7.7 %wgrad.1 = (f32[27,32,128]{2,1,0:T(8,128)S(1)}, f32[27,32,128]{2,1,0:T(8,128)S(1)}) custom-call(s32[3]{0:T(128)S(1)} %pad_add_fusion.place, bf16[2,576,2048]{2,1,0:T(8,128)(2,1)S(1)} %get-tuple-element.71.cols_a, bf16[2,576,2048]{2,1,0:T(8,128)(2,1)S(1)} %get-tuple-element.72.cols_b, bf16[2,2048,384]{2,1,0:T(8,128)(2,1)} %get-tuple-element.73.taps_a, ...), custom_call_target="tpu_custom_call" | custom-call | tf_op jit(solution)/shard_map/wgrad/pallas_call | solution.py:371
  82.8 2.0 %collective-permute-start.30 = (f32[27,32,128]{2,1,0:T(8,128)S(1)}, f32[27,32,128]{2,1,0:T(8,128)S(1)}, u32[]{:S(2)}, u32[]{:S(2)}) collective-permute-start(f32[27,32,128]{2,1,0:T(8,128)S(1)} %get-tuple-element.76), channel_id=1, source_target_pairs={{0,8},{8,0},{16,24},{24,16},{32,40},{40,32},{48,56},{56,48},{64,72... | collective-permute-start | bytes 1327112 | tf_op jit(solution)/shard_map/ppermute | solution.py:34
  85.1 1.8 %collective-permute-start.29 = (f16[2,144,128]{2,1,0:T(8,128)(2,1)S(1)}, f16[2,144,128]{2,1,0:T(8,128)(2,1)S(1)}, u32[]{:S(2)}, u32[]{:S(2)}) collective-permute-start(f16[2,144,128]{2,1,0:T(8,128)(2,1)S(1)} %get-tuple-element.101), channel_id=1, source_target_pairs={{0,48},{8,56},{16,0},{24,8},{32,16},{40,24},{48,32},{56,40},{64,11... | collective-permute-start | bytes 221192 | tf_op jit(solution)/shard_map/ppermute | solution.py:34
  87.0 1.5 %collective-permute-start.28 = (f16[2,144,128]{2,1,0:T(8,128)(2,1)S(1)}, f16[2,144,128]{2,1,0:T(8,128)(2,1)S(1)}, u32[]{:S(2)}, u32[]{:S(2)}) collective-permute-start(f16[2,144,128]{2,1,0:T(8,128)(2,1)S(1)} %get-tuple-element.102), channel_id=1, source_target_pairs={{0,32},{8,40},{16,48},{24,56},{32,0},{40,8},{48,16},{56,24},{64,96... | collective-permute-start | bytes 221192 | tf_op jit(solution)/shard_map/ppermute | solution.py:34
  88.5 0.8 collective-permute-start.27
  89.7 2.2 %collective-permute-start.22 = (f16[2,144,128]{2,1,0:T(8,128)(2,1)S(1)}, f16[2,144,128]{2,1,0:T(8,128)(2,1)S(1)}, u32[]{:S(2)}, u32[]{:S(2)}) collective-permute-start(f16[2,144,128]{2,1,0:T(8,128)(2,1)S(1)} %get-tuple-element.104), channel_id=1, source_target_pairs={{0,192},{8,200},{16,208},{24,216},{32,224},{40,232},{48,240},{56,2... | collective-permute-start | bytes 221192 | tf_op jit(solution)/shard_map/ppermute | solution.py:34
  91.9 0.7 collective-permute-start.21
  92.6 0.8 collective-permute-start.20
  93.4 0.8 collective-permute-done.27
  94.3 2.4 %collective-permute-done.21 = f16[2,144,128]{2,1,0:T(8,128)(2,1)S(1)} collective-permute-done((f16[2,144,128]{2,1,0:T(8,128)(2,1)S(1)}, f16[2,144,128]{2,1,0:T(8,128)(2,1)S(1)}, u32[]{:S(2)}, u32[]{:S(2)}) %collective-permute-start.21) | collective-permute-done | bytes 73760 | tf_op jit(solution)/shard_map/ppermute | solution.py:34
  96.6 1.1 %collective-permute-done.20 = f16[2,144,128]{2,1,0:T(8,128)(2,1)S(1)} collective-permute-done((f16[2,144,128]{2,1,0:T(8,128)(2,1)S(1)}, f16[2,144,128]{2,1,0:T(8,128)(2,1)S(1)}, u32[]{:S(2)}, u32[]{:S(2)}) %collective-permute-start.20) | collective-permute-done | bytes 73760 | tf_op jit(solution)/shard_map/ppermute | solution.py:34
  97.8 0.8 add_multiply_fusion
  98.6 0.7 last.1
  99.3 2.0 %collective-permute-start.31 = (bf16[4,64,128]{2,1,0:T(8,128)(2,1)S(1)}, bf16[4,64,128]{2,1,0:T(8,128)(2,1)S(1)}, u32[]{:S(2)}, u32[]{:S(2)}) collective-permute-start(bf16[4,64,128]{2,1,0:T(8,128)(2,1)S(1)} %get-tuple-element.86), channel_id=1, source_target_pairs={{0,8},{8,0},{16,24},{24,16},{32,40},{40,32},{48,56},{56,48},{64,72... | collective-permute-start | bytes 196616 | tf_op jit(solution)/shard_map/ppermute | solution.py:34
  101.3 1.6 %convert_element_type.111 = bf16[1,32,2048]{2,1,0:T(8,128)(2,1)} convert(f32[1,32,2048]{2,1,0:T(8,128)} %reduce-scatter.2.cloned.1.call-done) | non-fusion elementwise | flops 65536 | bytes 393216 | tf_op jit(solution)/shard_map/convert_element_type | solution.py:325
  102.9 0.7 fusion
  (69 shorter events, 4.8 us)
Async XLA Ops:
  7.2 24.3 %copy-start.1 = (bf16[27,32,128]{2,1,0:T(8,128)(2,1)S(1)}, bf16[27,32,128]{2,1,0:T(8,128)(2,1)}, u32[]{:S(2)}) copy-start(bf16[27,32,128]{2,1,0:T(8,128)(2,1)} %param.4) | copy-start | bytes 663556
  7.2 48.6 %all-gather.2.cloned.1.call-start = ((), (), s32[]{:S(2)}) async-start(), calls=%async_computation.1 | async-start | bytes 1179648 | tf_op jit(solution)/shard_map/all_gather | solution.py:256
  7.9 93.4 %reduce-scatter.2.cloned.1.call-start = ((), (), s32[]{:S(2)}) async-start(), calls=%async_computation.2 | async-start | bytes 2359296 | tf_op jit(solution)/shard_map/reduce_scatter | solution.py:325
  8.9 4.2 %collective-permute-start = (bf16[4,64,128]{2,1,0:T(8,128)(2,1)S(1)}, bf16[4,64,128]{2,1,0:T(8,128)(2,1)S(1)}, u32[]{:S(2)}, u32[]{:S(2)}) collective-permute-start(bf16[4,64,128]{2,1,0:T(8,128)(2,1)S(1)} %get-tuple-element.110), channel_id=1, source_target_pairs={{0,8},{8,0},{16,24},{24,16},{32,40},{40,32},{48,56},{56,48},{64,72... | collective-permute-start | bytes 196616 | tf_op jit(solution)/shard_map/ppermute | solution.py:34
  13.2 5.1 %collective-permute-start.6 = (bf16[2,128,128]{2,1,0:T(8,128)(2,1)S(1)}, bf16[2,128,128]{2,1,0:T(8,128)(2,1)S(1)}, u32[]{:S(2)}, u32[]{:S(2)}) collective-permute-start(bf16[2,128,128]{2,1,0:T(8,128)(2,1)S(1)} %get-tuple-element.52), channel_id=1, source_target_pairs={{0,192},{8,200},{16,208},{24,216},{32,224},{40,232},{48,240},{56,2... | collective-permute-start | bytes 196616 | tf_op jit(solution)/shard_map/ppermute | solution.py:34
  14.2 4.7 %collective-permute-start.5 = (bf16[2,128,128]{2,1,0:T(8,128)(2,1)S(1)}, bf16[2,128,128]{2,1,0:T(8,128)(2,1)S(1)}, u32[]{:S(2)}, u32[]{:S(2)}) collective-permute-start(bf16[2,128,128]{2,1,0:T(8,128)(2,1)S(1)} %get-tuple-element.52), channel_id=1, source_target_pairs={{0,128},{8,136},{16,144},{24,152},{32,160},{40,168},{48,176},{56,1... | collective-permute-start | bytes 196616 | tf_op jit(solution)/shard_map/ppermute | solution.py:34
  14.6 5.8 %collective-permute-start.4 = (bf16[2,128,128]{2,1,0:T(8,128)(2,1)S(1)}, bf16[2,128,128]{2,1,0:T(8,128)(2,1)S(1)}, u32[]{:S(2)}, u32[]{:S(2)}) collective-permute-start(bf16[2,128,128]{2,1,0:T(8,128)(2,1)S(1)} %get-tuple-element.52), channel_id=1, source_target_pairs={{0,64},{8,72},{16,80},{24,88},{32,96},{40,104},{48,112},{56,120},{... | collective-permute-start | bytes 196616 | tf_op jit(solution)/shard_map/ppermute | solution.py:34
  15.3 5.1 %collective-permute-start.3 = (bf16[2,128,128]{2,1,0:T(8,128)(2,1)S(1)}, bf16[2,128,128]{2,1,0:T(8,128)(2,1)S(1)}, u32[]{:S(2)}, u32[]{:S(2)}) collective-permute-start(bf16[2,128,128]{2,1,0:T(8,128)(2,1)S(1)} %get-tuple-element.48), channel_id=1, source_target_pairs={{0,48},{8,56},{16,0},{24,8},{32,16},{40,24},{48,32},{56,40},{64,11... | collective-permute-start | bytes 196616 | tf_op jit(solution)/shard_map/ppermute | solution.py:34
  17.8 4.7 %collective-permute-start.2 = (bf16[2,128,128]{2,1,0:T(8,128)(2,1)S(1)}, bf16[2,128,128]{2,1,0:T(8,128)(2,1)S(1)}, u32[]{:S(2)}, u32[]{:S(2)}) collective-permute-start(bf16[2,128,128]{2,1,0:T(8,128)(2,1)S(1)} %get-tuple-element.48), channel_id=1, source_target_pairs={{0,32},{8,40},{16,48},{24,56},{32,0},{40,8},{48,16},{56,24},{64,96... | collective-permute-start | bytes 196616 | tf_op jit(solution)/shard_map/ppermute | solution.py:34
  18.3 4.8 %collective-permute-start.1 = (bf16[2,128,128]{2,1,0:T(8,128)(2,1)S(1)}, bf16[2,128,128]{2,1,0:T(8,128)(2,1)S(1)}, u32[]{:S(2)}, u32[]{:S(2)}) collective-permute-start(bf16[2,128,128]{2,1,0:T(8,128)(2,1)S(1)} %get-tuple-element.48), channel_id=1, source_target_pairs={{0,16},{8,24},{16,32},{24,40},{32,48},{40,56},{48,0},{56,8},{64,80... | collective-permute-start | bytes 196616 | tf_op jit(solution)/shard_map/ppermute | solution.py:34
  23.1 7.5 %collective-permute-start.9 = (bf16[4,2,128,128]{3,2,1,0:T(8,128)(2,1)S(1)}, bf16[4,2,128,128]{3,2,1,0:T(8,128)(2,1)S(1)}, u32[]{:S(2)}, u32[]{:S(2)}) collective-permute-start(bf16[4,2,128,128]{3,2,1,0:T(8,128)(2,1)S(1)} %get-tuple-element.56.refs_0_), channel_id=1, source_target_pairs={{0,192},{8,200},{16,208},{24,216},{32,224},{40,232},{48,240},{56,2... | collective-permute-start | bytes 786440 | tf_op jit(solution)/shard_map/ppermute | solution.py:34
  25.2 4.6 %collective-permute-start.10 = (bf16[27,32,128]{2,1,0:T(8,128)(2,1)}, bf16[27,32,128]{2,1,0:T(8,128)(2,1)S(1)}, u32[]{:S(2)}, u32[]{:S(2)}) collective-permute-start(bf16[27,32,128]{2,1,0:T(8,128)(2,1)} %param.4), channel_id=1, source_target_pairs={{0,8},{8,0},{16,24},{24,16},{32,40},{40,32},{48,56},{56,48},{64,72... | collective-permute-start | bytes 663560 | tf_op jit(solution)/shard_map/ppermute | solution.py:34
  28.1 9.5 %collective-permute-start.8 = (bf16[4,2,128,128]{3,2,1,0:T(8,128)(2,1)S(1)}, bf16[4,2,128,128]{3,2,1,0:T(8,128)(2,1)S(1)}, u32[]{:S(2)}, u32[]{:S(2)}) collective-permute-start(bf16[4,2,128,128]{3,2,1,0:T(8,128)(2,1)S(1)} %get-tuple-element.56.refs_0_), channel_id=1, source_target_pairs={{0,128},{8,136},{16,144},{24,152},{32,160},{40,168},{48,176},{56,1... | collective-permute-start | bytes 786440 | tf_op jit(solution)/shard_map/ppermute | solution.py:34
  29.5 14.0 %collective-permute-start.7 = (bf16[4,2,128,128]{3,2,1,0:T(8,128)(2,1)S(1)}, bf16[4,2,128,128]{3,2,1,0:T(8,128)(2,1)S(1)}, u32[]{:S(2)}, u32[]{:S(2)}) collective-permute-start(bf16[4,2,128,128]{3,2,1,0:T(8,128)(2,1)S(1)} %get-tuple-element.56.refs_0_), channel_id=1, source_target_pairs={{0,64},{8,72},{16,80},{24,88},{32,96},{40,104},{48,112},{56,120},{... | collective-permute-start | bytes 786440 | tf_op jit(solution)/shard_map/ppermute | solution.py:34
  29.5 20.3 %collective-permute-start.14 = (bf16[4,2,128,128]{3,2,1,0:T(8,128)(2,1)S(1)}, bf16[4,2,128,128]{3,2,1,0:T(8,128)(2,1)S(1)}, u32[]{:S(2)}, u32[]{:S(2)}) collective-permute-start(bf16[4,2,128,128]{3,2,1,0:T(8,128)(2,1)S(1)} %get-tuple-element.58.refs_0_), channel_id=1, source_target_pairs={{0,48},{8,56},{16,0},{24,8},{32,16},{40,24},{48,32},{56,40},{64,11... | collective-permute-start | bytes 786440 | tf_op jit(solution)/shard_map/ppermute | solution.py:34
  29.8 20.0 %collective-permute-start.13 = (bf16[4,2,128,128]{3,2,1,0:T(8,128)(2,1)S(1)}, bf16[4,2,128,128]{3,2,1,0:T(8,128)(2,1)S(1)}, u32[]{:S(2)}, u32[]{:S(2)}) collective-permute-start(bf16[4,2,128,128]{3,2,1,0:T(8,128)(2,1)S(1)} %get-tuple-element.58.refs_0_), channel_id=1, source_target_pairs={{0,32},{8,40},{16,48},{24,56},{32,0},{40,8},{48,16},{56,24},{64,96... | collective-permute-start | bytes 786440 | tf_op jit(solution)/shard_map/ppermute | solution.py:34
  30.7 19.2 %collective-permute-start.12 = (bf16[4,2,128,128]{3,2,1,0:T(8,128)(2,1)S(1)}, bf16[4,2,128,128]{3,2,1,0:T(8,128)(2,1)S(1)}, u32[]{:S(2)}, u32[]{:S(2)}) collective-permute-start(bf16[4,2,128,128]{3,2,1,0:T(8,128)(2,1)S(1)} %get-tuple-element.58.refs_0_), channel_id=1, source_target_pairs={{0,16},{8,24},{16,32},{24,40},{32,48},{40,56},{48,0},{56,8},{64,80... | collective-permute-start | bytes 786440 | tf_op jit(solution)/shard_map/ppermute | solution.py:34
  49.3 7.5 %collective-permute-start.11 = (f32[2,32,2048]{2,1,0:T(8,128)}, f32[2,32,2048]{2,1,0:T(8,128)S(1)}, u32[]{:S(2)}, u32[]{:S(2)}) collective-permute-start(f32[2,32,2048]{2,1,0:T(8,128)} %get-tuple-element.57), channel_id=1, source_target_pairs={{0,8},{8,0},{16,24},{24,16},{32,40},{40,32},{48,56},{56,48},{64,72... | collective-permute-start | bytes 1572872 | tf_op jit(solution)/shard_map/ppermute | solution.py:34
  55.8 2.1 %collective-permute-start.15 = (f32[2,32,2048]{2,1,0:T(8,128)}, f32[2,32,2048]{2,1,0:T(8,128)S(1)}, u32[]{:S(2)}, u32[]{:S(2)}) collective-permute-start(f32[2,32,2048]{2,1,0:T(8,128)} %get-tuple-element.60), channel_id=1, source_target_pairs={{0,8},{8,0},{16,24},{24,16},{32,40},{40,32},{48,56},{56,48},{64,72... | collective-permute-start | bytes 1572872 | tf_op jit(solution)/shard_map/ppermute | solution.py:34
  59.4 1.7 %copy-start = (bf16[8,32,2048]{2,1,0:T(8,128)(2,1)S(1)}, bf16[8,32,2048]{2,1,0:T(8,128)(2,1)}, u32[]{:S(2)}) copy-start(bf16[8,32,2048]{2,1,0:T(8,128)(2,1)} %all-gather.2.cloned.1.call-done.own_ref) | copy-start | bytes 3145732
  59.5 1.6 %collective-permute-start.23 = (bf16[2,32,2048]{2,1,0:T(8,128)(2,1)S(1)}, bf16[2,32,2048]{2,1,0:T(8,128)(2,1)S(1)}, u32[]{:S(2)}, u32[]{:S(2)}) collective-permute-start(bf16[2,32,2048]{2,1,0:T(8,128)(2,1)S(1)} %get-tuple-element.66), channel_id=1, source_target_pairs={{0,8},{8,0},{16,24},{24,16},{32,40},{40,32},{48,56},{56,48},{64,72... | collective-permute-start | bytes 786440 | tf_op jit(solution)/shard_map/ppermute | solution.py:34
  60.0 8.2 %collective-permute-start.16 = (bf16[2,32,2048]{2,1,0:T(8,128)(2,1)S(1)}, bf16[2,32,2048]{2,1,0:T(8,128)(2,1)S(1)}, u32[]{:S(2)}, u32[]{:S(2)}) collective-permute-start(bf16[2,32,2048]{2,1,0:T(8,128)(2,1)S(1)} %get-tuple-element.61), channel_id=1, source_target_pairs={{0,8},{8,0},{16,24},{24,16},{32,40},{40,32},{48,56},{56,48},{64,72... | collective-permute-start | bytes 786440 | tf_op jit(solution)/shard_map/ppermute | solution.py:34
  65.9 8.4 %collective-permute-start.26 = (f16[2,528,128]{2,1,0:T(8,128)(2,1)S(1)}, f16[2,528,128]{2,1,0:T(8,128)(2,1)S(1)}, u32[]{:S(2)}, u32[]{:S(2)}) collective-permute-start(f16[2,528,128]{2,1,0:T(8,128)(2,1)S(1)} %get-tuple-element.95), channel_id=1, source_target_pairs={{0,192},{8,200},{16,208},{24,216},{32,224},{40,232},{48,240},{56,2... | collective-permute-start | bytes 811016 | tf_op jit(solution)/shard_map/ppermute | solution.py:34
  66.3 16.5 %collective-permute-start.25 = (f16[2,528,128]{2,1,0:T(8,128)(2,1)S(1)}, f16[2,528,128]{2,1,0:T(8,128)(2,1)S(1)}, u32[]{:S(2)}, u32[]{:S(2)}) collective-permute-start(f16[2,528,128]{2,1,0:T(8,128)(2,1)S(1)} %get-tuple-element.96), channel_id=1, source_target_pairs={{0,128},{8,136},{16,144},{24,152},{32,160},{40,168},{48,176},{56,1... | collective-permute-start | bytes 811016 | tf_op jit(solution)/shard_map/ppermute | solution.py:34
  67.7 17.1 %collective-permute-start.24 = (f16[2,528,128]{2,1,0:T(8,128)(2,1)S(1)}, f16[2,528,128]{2,1,0:T(8,128)(2,1)S(1)}, u32[]{:S(2)}, u32[]{:S(2)}) collective-permute-start(f16[2,528,128]{2,1,0:T(8,128)(2,1)S(1)} %get-tuple-element.97), channel_id=1, source_target_pairs={{0,64},{8,72},{16,80},{24,88},{32,96},{40,104},{48,112},{56,120},{... | collective-permute-start | bytes 811016 | tf_op jit(solution)/shard_map/ppermute | solution.py:34
  73.0 13.9 %collective-permute-start.19 = (f16[2,528,128]{2,1,0:T(8,128)(2,1)S(1)}, f16[2,528,128]{2,1,0:T(8,128)(2,1)S(1)}, u32[]{:S(2)}, u32[]{:S(2)}) collective-permute-start(f16[2,528,128]{2,1,0:T(8,128)(2,1)S(1)} %get-tuple-element.98), channel_id=1, source_target_pairs={{0,48},{8,56},{16,0},{24,8},{32,16},{40,24},{48,32},{56,40},{64,11... | collective-permute-start | bytes 811016 | tf_op jit(solution)/shard_map/ppermute | solution.py:34
  73.4 15.1 %collective-permute-start.18 = (f16[2,528,128]{2,1,0:T(8,128)(2,1)S(1)}, f16[2,528,128]{2,1,0:T(8,128)(2,1)S(1)}, u32[]{:S(2)}, u32[]{:S(2)}) collective-permute-start(f16[2,528,128]{2,1,0:T(8,128)(2,1)S(1)} %get-tuple-element.99), channel_id=1, source_target_pairs={{0,32},{8,40},{16,48},{24,56},{32,0},{40,8},{48,16},{56,24},{64,96... | collective-permute-start | bytes 811016 | tf_op jit(solution)/shard_map/ppermute | solution.py:34
  74.3 15.1 %collective-permute-start.17 = (f16[2,528,128]{2,1,0:T(8,128)(2,1)S(1)}, f16[2,528,128]{2,1,0:T(8,128)(2,1)S(1)}, u32[]{:S(2)}, u32[]{:S(2)}) collective-permute-start(f16[2,528,128]{2,1,0:T(8,128)(2,1)S(1)} %get-tuple-element.100), channel_id=1, source_target_pairs={{0,16},{8,24},{16,32},{24,40},{32,48},{40,56},{48,0},{56,8},{64,80... | collective-permute-start | bytes 811016 | tf_op jit(solution)/shard_map/ppermute | solution.py:34
  82.8 15.0 %collective-permute-start.30 = (f32[27,32,128]{2,1,0:T(8,128)S(1)}, f32[27,32,128]{2,1,0:T(8,128)S(1)}, u32[]{:S(2)}, u32[]{:S(2)}) collective-permute-start(f32[27,32,128]{2,1,0:T(8,128)S(1)} %get-tuple-element.76), channel_id=1, source_target_pairs={{0,8},{8,0},{16,24},{24,16},{32,40},{40,32},{48,56},{56,48},{64,72... | collective-permute-start | bytes 1327112 | tf_op jit(solution)/shard_map/ppermute | solution.py:34
  85.1 6.8 %collective-permute-start.29 = (f16[2,144,128]{2,1,0:T(8,128)(2,1)S(1)}, f16[2,144,128]{2,1,0:T(8,128)(2,1)S(1)}, u32[]{:S(2)}, u32[]{:S(2)}) collective-permute-start(f16[2,144,128]{2,1,0:T(8,128)(2,1)S(1)} %get-tuple-element.101), channel_id=1, source_target_pairs={{0,48},{8,56},{16,0},{24,8},{32,16},{40,24},{48,32},{56,40},{64,11... | collective-permute-start | bytes 221192 | tf_op jit(solution)/shard_map/ppermute | solution.py:34
  87.0 5.7 %collective-permute-start.28 = (f16[2,144,128]{2,1,0:T(8,128)(2,1)S(1)}, f16[2,144,128]{2,1,0:T(8,128)(2,1)S(1)}, u32[]{:S(2)}, u32[]{:S(2)}) collective-permute-start(f16[2,144,128]{2,1,0:T(8,128)(2,1)S(1)} %get-tuple-element.102), channel_id=1, source_target_pairs={{0,32},{8,40},{16,48},{24,56},{32,0},{40,8},{48,16},{56,24},{64,96... | collective-permute-start | bytes 221192 | tf_op jit(solution)/shard_map/ppermute | solution.py:34
  88.5 5.7 %collective-permute-start.27 = (f16[2,144,128]{2,1,0:T(8,128)(2,1)S(1)}, f16[2,144,128]{2,1,0:T(8,128)(2,1)S(1)}, u32[]{:S(2)}, u32[]{:S(2)}) collective-permute-start(f16[2,144,128]{2,1,0:T(8,128)(2,1)S(1)} %get-tuple-element.103), channel_id=1, source_target_pairs={{0,16},{8,24},{16,32},{24,40},{32,48},{40,56},{48,0},{56,8},{64,80... | collective-permute-start | bytes 221192 | tf_op jit(solution)/shard_map/ppermute | solution.py:34
  89.7 4.6 %collective-permute-start.22 = (f16[2,144,128]{2,1,0:T(8,128)(2,1)S(1)}, f16[2,144,128]{2,1,0:T(8,128)(2,1)S(1)}, u32[]{:S(2)}, u32[]{:S(2)}) collective-permute-start(f16[2,144,128]{2,1,0:T(8,128)(2,1)S(1)} %get-tuple-element.104), channel_id=1, source_target_pairs={{0,192},{8,200},{16,208},{24,216},{32,224},{40,232},{48,240},{56,2... | collective-permute-start | bytes 221192 | tf_op jit(solution)/shard_map/ppermute | solution.py:34
  91.9 4.7 %collective-permute-start.21 = (f16[2,144,128]{2,1,0:T(8,128)(2,1)S(1)}, f16[2,144,128]{2,1,0:T(8,128)(2,1)S(1)}, u32[]{:S(2)}, u32[]{:S(2)}) collective-permute-start(f16[2,144,128]{2,1,0:T(8,128)(2,1)S(1)} %get-tuple-element.105), channel_id=1, source_target_pairs={{0,128},{8,136},{16,144},{24,152},{32,160},{40,168},{48,176},{56,1... | collective-permute-start | bytes 221192 | tf_op jit(solution)/shard_map/ppermute | solution.py:34
  92.6 5.2 %collective-permute-start.20 = (f16[2,144,128]{2,1,0:T(8,128)(2,1)S(1)}, f16[2,144,128]{2,1,0:T(8,128)(2,1)S(1)}, u32[]{:S(2)}, u32[]{:S(2)}) collective-permute-start(f16[2,144,128]{2,1,0:T(8,128)(2,1)S(1)} %get-tuple-element.106), channel_id=1, source_target_pairs={{0,64},{8,72},{16,80},{24,88},{32,96},{40,104},{48,112},{56,120},{... | collective-permute-start | bytes 221192 | tf_op jit(solution)/shard_map/ppermute | solution.py:34
  99.3 3.6 %collective-permute-start.31 = (bf16[4,64,128]{2,1,0:T(8,128)(2,1)S(1)}, bf16[4,64,128]{2,1,0:T(8,128)(2,1)S(1)}, u32[]{:S(2)}, u32[]{:S(2)}) collective-permute-start(bf16[4,64,128]{2,1,0:T(8,128)(2,1)S(1)} %get-tuple-element.86), channel_id=1, source_target_pairs={{0,8},{8,0},{16,24},{24,16},{32,40},{40,32},{48,56},{56,48},{64,72... | collective-permute-start | bytes 196616 | tf_op jit(solution)/shard_map/ppermute | solution.py:34
Sparse Core Ops, SparseCore 0:
  9.8 38.1 all-gather.1
  59.6 37.2 reduce-scatter.1

commit v5 on v4

--- a/solution.py
+++ b/solution.py
@@ -175,8 +175,9 @@
         msg[step - 1, :, size:] = power
 
 
-def last_kernel(place, *refs):
-    ins, own_ref, other_ref = refs[:8], refs[8], refs[9]
+def last_kernel(scale, place, *refs):
+    ins, sum_ref, got_ref, own_ref, other_ref, weight_ref = refs[:8], *refs[8:]
+    weight_ref[...] = (sum_ref[...] + got_ref[...]) * scale
     part = PLANE // 2
     for half in range(2):
         own, messages = ins[4 * half], ins[4 * half + 1 : 4 * half + 4]
@@ -382,20 +383,19 @@
         compiler_params=params,
         name="wgrad",
     )(place, columns_a, columns_b, taps_a, taps_b)
-    grad_weight = (own + swap_cores(other)) / math.sqrt(batch * cells)
-    ends, grad_weight = lax.optimization_barrier((ends, grad_weight))
-    own, other = pl.pallas_call(
-        last_kernel,
+    sums = [own, swap_cores(other)]
+    own, other, grad_weight = pl.pallas_call(
+        functools.partial(last_kernel, 1.0 / math.sqrt(batch * cells)),
         grid_spec=pltpu.PrefetchScalarGridSpec(
             num_scalar_prefetch=1,
             grid=(1,),
-            in_specs=[whole(e.shape) for e in ends],
-            out_specs=[whole((mine, PLANE // 2, co))] * 2,
+            in_specs=[whole(e.shape) for e in ends + sums],
+            out_specs=[whole((mine, PLANE // 2, co))] * 2 + [pl.BlockSpec(own.shape, lambda *_: (0, 0, 0))],
         ),
-        out_shape=[jax.ShapeDtypeStruct((mine, PLANE // 2, co), BF16)] * 2,
+        out_shape=[jax.ShapeDtypeStruct((mine, PLANE // 2, co), BF16)] * 2 + [jax.ShapeDtypeStruct(own.shape, F32)],
         compiler_params=params,
         name="last",
-    )(place, *ends)
+    )(place, *ends, *sums)
     got, grad_input = lax.optimization_barrier((swap_cores(other), grad_input))
     output = jnp.transpose(in_order(own, got, 0), (0, 2, 1))
     return output, grad_input, grad_weight

time: 111 us -> 110 us (level)
  transfers between devices with their start and end apart: 34 -> 34, of which waited for: 11 -> 11; matrix products, arithmetic and copies ran while one was open for 6% -> 5% of each run, Pallas kernels for 27% -> 27%
where the time goes in v5:
time: 110 us
  starting transfers between devices  34.6 us (31%)
  Pallas kernels  31.8 us (29%)
  waiting for transfers between devices  23 us (21%)
  between operations  14.4 us (13%)
  other arithmetic  3.47 us (3%)
  local copies, waits for them, and re-layouts  3.03 us (3%)
    ppermute x32, starting transfers between devices, move_xy(): return lax.ppermute(value, 'cin', pairs)  34.5 us
    ppermute x32, waiting for transfers between devices, move_xy(): return lax.ppermute(value, 'cin', pairs)  22.3 us
    pallas_call x2, Pallas kernels, dgrad(): pl.pallas_call(functools.partial(dgrad_kernel, half), grid_spec=pltpu.Pre...  11.8 us
    pallas_call x2, Pallas kernels, forward(): pl.pallas_call(functools.partial(fwd_kernel, half), grid_spec=pltpu.Prefe...  9 us
    pallas_call x1, Pallas kernels, body(): pl.pallas_call(wgrad_kernel, grid_spec=pltpu.PrefetchScalarGridSpec(num_s...  7.7 us
  transfers between devices with their start and end apart: 34, of which 11 were waited for; matrix products, arithmetic and copies ran while one was open for 5% of the time, Pallas kernels for 27%

profile of v5, /device:TPU:1, one launch (start us, length us, event | category | flops | bytes accessed | tf_op | source)
XLA Modules:
  0.0 110.3 jit_solution(13534815495904683652)
XLA Ops:
  7.2 0.7 all-gather.2.cloned.1.call-update
  8.0 0.9 dynamic-slice_bitcast_fusion.1
  8.9 3.3 %collective-permute-start = (bf16[4,64,128]{2,1,0:T(8,128)(2,1)S(1)}, bf16[4,64,128]{2,1,0:T(8,128)(2,1)S(1)}, u32[]{:S(2)}, u32[]{:S(2)}) collective-permute-start(bf16[4,64,128]{2,1,0:T(8,128)(2,1)S(1)} %get-tuple-element.94), channel_id=1, source_target_pairs={{0,8},{8,0},{16,24},{24,16},{32,40},{40,32},{48,56},{56,48},{64,72... | collective-permute-start | bytes 196616 | tf_op jit(solution)/shard_map/ppermute | solution.py:34
  12.2 0.9 collective-permute-done
  13.2 1.1 collective-permute-start.6
  14.6 0.7 collective-permute-start.4
  15.3 2.5 %collective-permute-start.3 = (bf16[2,128,128]{2,1,0:T(8,128)(2,1)S(1)}, bf16[2,128,128]{2,1,0:T(8,128)(2,1)S(1)}, u32[]{:S(2)}, u32[]{:S(2)}) collective-permute-start(bf16[2,128,128]{2,1,0:T(8,128)(2,1)S(1)} %get-tuple-element.40), channel_id=1, source_target_pairs={{0,48},{8,56},{16,0},{24,8},{32,16},{40,24},{48,32},{56,40},{64,11... | collective-permute-start | bytes 196616 | tf_op jit(solution)/shard_map/ppermute | solution.py:34
  17.8 0.5 collective-permute-start.2
  18.3 0.6 collective-permute-start.1
  18.9 1.4 %collective-permute-done.4 = bf16[2,128,128]{2,1,0:T(8,128)(2,1)S(1)} collective-permute-done((bf16[2,128,128]{2,1,0:T(8,128)(2,1)S(1)}, bf16[2,128,128]{2,1,0:T(8,128)(2,1)S(1)}, u32[]{:S(2)}, u32[]{:S(2)}) %collective-permute-start.4) | collective-permute-done | bytes 65568 | tf_op jit(solution)/shard_map/ppermute | solution.py:34
  20.3 2.1 %collective-permute-done.2 = bf16[2,128,128]{2,1,0:T(8,128)(2,1)S(1)} collective-permute-done((bf16[2,128,128]{2,1,0:T(8,128)(2,1)S(1)}, bf16[2,128,128]{2,1,0:T(8,128)(2,1)S(1)}, u32[]{:S(2)}, u32[]{:S(2)}) %collective-permute-start.2) | collective-permute-done | bytes 65568 | tf_op jit(solution)/shard_map/ppermute | solution.py:34
  22.4 0.7 collective-permute-done.1
  23.1 2.1 %collective-permute-start.9 = (bf16[4,2,128,128]{3,2,1,0:T(8,128)(2,1)S(1)}, bf16[4,2,128,128]{3,2,1,0:T(8,128)(2,1)S(1)}, u32[]{:S(2)}, u32[]{:S(2)}) collective-permute-start(bf16[4,2,128,128]{3,2,1,0:T(8,128)(2,1)S(1)} %get-tuple-element.48.refs_0_), channel_id=1, source_target_pairs={{0,192},{8,200},{16,208},{24,216},{32,224},{40,232},{48,240},{56,2... | collective-permute-start | bytes 786440 | tf_op jit(solution)/shard_map/ppermute | solution.py:34
  25.2 2.9 %collective-permute-start.10 = (bf16[27,32,128]{2,1,0:T(8,128)(2,1)}, bf16[27,32,128]{2,1,0:T(8,128)(2,1)S(1)}, u32[]{:S(2)}, u32[]{:S(2)}) collective-permute-start(bf16[27,32,128]{2,1,0:T(8,128)(2,1)} %param.4), channel_id=1, source_target_pairs={{0,8},{8,0},{16,24},{24,16},{32,40},{40,32},{48,56},{56,48},{64,72... | collective-permute-start | bytes 663560 | tf_op jit(solution)/shard_map/ppermute | solution.py:34
  28.1 1.4 %collective-permute-start.8 = (bf16[4,2,128,128]{3,2,1,0:T(8,128)(2,1)S(1)}, bf16[4,2,128,128]{3,2,1,0:T(8,128)(2,1)S(1)}, u32[]{:S(2)}, u32[]{:S(2)}) collective-permute-start(bf16[4,2,128,128]{3,2,1,0:T(8,128)(2,1)S(1)} %get-tuple-element.48.refs_0_), channel_id=1, source_target_pairs={{0,128},{8,136},{16,144},{24,152},{32,160},{40,168},{48,176},{56,1... | collective-permute-start | bytes 786440 | tf_op jit(solution)/shard_map/ppermute | solution.py:34
  29.8 0.9 collective-permute-start.13
  30.7 0.8 collective-permute-start.12
  31.9 0.4 maximum_select_fusion
  32.4 5.2 %collective-permute-done.8.refs_2_ = bf16[4,2,128,128]{3,2,1,0:T(8,128)(2,1)S(1)} collective-permute-done((bf16[4,2,128,128]{3,2,1,0:T(8,128)(2,1)S(1)}, bf16[4,2,128,128]{3,2,1,0:T(8,128)(2,1)S(1)}, u32[]{:S(2)}, u32[]{:S(2)}) %collective-permute-start.8) | collective-permute-done | bytes 262176 | tf_op jit(solution)/shard_map/ppermute | solution.py:34
  37.6 5.9 %collective-permute-done.7.refs_1_ = bf16[4,2,128,128]{3,2,1,0:T(8,128)(2,1)S(1)} collective-permute-done((bf16[4,2,128,128]{3,2,1,0:T(8,128)(2,1)S(1)}, bf16[4,2,128,128]{3,2,1,0:T(8,128)(2,1)S(1)}, u32[]{:S(2)}, u32[]{:S(2)}) %collective-permute-start.7) | collective-permute-done | bytes 262176 | tf_op jit(solution)/shard_map/ppermute | solution.py:34
  43.5 5.9 %dgrad.2 = (bf16[2,2048,384]{2,1,0:T(8,128)(2,1)}, f32[8,32,2048]{2,1,0:T(8,128)}, f32[2,32,2048]{2,1,0:T(8,128)}) custom-call(s32[3]{0:T(128)S(1)} %pad_add_fusion.place, bf16[4,2,128,128]{3,2,1,0:T(8,128)(2,1)S(1)} %get-tuple-element.48.refs_0_, bf16[4,2,128,128]{3,2,1,0:T(8,128)(2,1)S(1)} %collective-permute-done.7.refs_1_, ...), custom_call_target="tpu_custom_call" | custom-call | tf_op jit(solution)/shard_map/dgrad/pallas_call | solution.py:282
  49.3 0.5 collective-permute-start.11
  49.8 5.9 %dgrad.3 = (bf16[2,2048,384]{2,1,0:T(8,128)(2,1)}, f32[8,32,2048]{2,1,0:T(8,128)}, f32[2,32,2048]{2,1,0:T(8,128)}) custom-call(s32[3]{0:T(128)S(1)} %pad_add_fusion.place, bf16[4,2,128,128]{3,2,1,0:T(8,128)(2,1)S(1)} %get-tuple-element.50.refs_0_, bf16[4,2,128,128]{3,2,1,0:T(8,128)(2,1)S(1)} %collective-permute-done.12.refs_1_, ...), custom_call_target="tpu_custom_call", output_to_operand_aliasing={{1}: (6, {})} | custom-call | tf_op jit(solution)/shard_map/dgrad/pallas_call | solution.py:282
  55.8 1.1 constant_dynamic-slice_fusion
  56.8 1.0 collective-permute-done.15.term_b
  57.9 1.5 %place.1 = f32[8,32,2048]{2,1,0:T(8,128)} custom-call(s32[3]{0:T(128)S(1)} %pad_add_fusion.place, f32[8,32,2048]{2,1,0:T(8,128)} %get-tuple-element.71._, f32[2,32,2048]{2,1,0:T(8,128)S(1)} %collective-permute-done.11.term_a, f32[2,32,2048]{2,1,0:T(8,128)S(1)} %collective-permute-done.15.term_b), custom_call_target="tpu_custom_call", output_to_operand_aliasing={{}: (1, {})} | custom-call | tf_op jit(solution)/shard_map/place/pallas_call | solution.py:312
  60.4 0.7 collective-permute-done.23.other_ref
  61.1 4.5 %forward.3 = (bf16[2,576,2048]{2,1,0:T(8,128)(2,1)S(1)}, f32[3,2,528,128]{3,2,1,0:T(8,128)S(1)}, f32[2,528,128]{2,1,0:T(8,128)S(1)}) custom-call(s32[3]{0:T(128)S(1)} %pad_add_fusion.place, bf16[8,32,2048]{2,1,0:T(8,128)(2,1)S(1)} %copy-done, bf16[2,32,2048]{2,1,0:T(8,128)(2,1)S(1)} %collective-permute-done.23.other_ref, bf16[384,576]{1,0:T(8,128)(2,1)S(1)} %bitcast.53), custom_call_target="tpu_custom_call" | custom-call | tf_op jit(solution)/shard_map/forward/pallas_call | solution.py:333
  66.3 1.4 %collective-permute-start.25 = (f16[2,528,128]{2,1,0:T(8,128)(2,1)S(1)}, f16[2,528,128]{2,1,0:T(8,128)(2,1)S(1)}, u32[]{:S(2)}, u32[]{:S(2)}) collective-permute-start(f16[2,528,128]{2,1,0:T(8,128)(2,1)S(1)} %get-tuple-element.80), channel_id=1, source_target_pairs={{0,128},{8,136},{16,144},{24,152},{32,160},{40,168},{48,176},{56,1... | collective-permute-start | bytes 811016 | tf_op jit(solution)/shard_map/ppermute | solution.py:34
  67.7 0.5 collective-permute-start.24
  68.2 4.5 %forward.2 = (bf16[2,576,2048]{2,1,0:T(8,128)(2,1)S(1)}, f32[3,2,528,128]{3,2,1,0:T(8,128)S(1)}, f32[2,528,128]{2,1,0:T(8,128)S(1)}) custom-call(s32[3]{0:T(128)S(1)} %pad_add_fusion.place, bf16[8,32,2048]{2,1,0:T(8,128)(2,1)S(1)} %copy-done, bf16[2,32,2048]{2,1,0:T(8,128)(2,1)S(1)} %collective-permute-done.16.other_ref, bf16[384,576]{1,0:T(8,128)(2,1)S(1)} %bitcast.54), custom_call_target="tpu_custom_call" | custom-call | tf_op jit(solution)/shard_map/forward/pallas_call | solution.py:333
  73.4 0.9 collective-permute-start.18
  74.2 0.8 collective-permute-start.17
  75.0 7.7 %wgrad.1 = (f32[27,32,128]{2,1,0:T(8,128)S(1)}, f32[27,32,128]{2,1,0:T(8,128)S(1)}) custom-call(s32[3]{0:T(128)S(1)} %pad_add_fusion.place, bf16[2,576,2048]{2,1,0:T(8,128)(2,1)S(1)} %get-tuple-element.63.cols_a, bf16[2,576,2048]{2,1,0:T(8,128)(2,1)S(1)} %get-tuple-element.64.cols_b, bf16[2,2048,384]{2,1,0:T(8,128)(2,1)} %get-tuple-element.65.taps_a, ...), custom_call_target="tpu_custom_call" | custom-call | tf_op jit(solution)/shard_map/wgrad/pallas_call | solution.py:372
  82.8 2.0 %collective-permute-start.30 = (f32[27,32,128]{2,1,0:T(8,128)S(1)}, f32[27,32,128]{2,1,0:T(8,128)S(1)}, u32[]{:S(2)}, u32[]{:S(2)}) collective-permute-start(f32[27,32,128]{2,1,0:T(8,128)S(1)} %get-tuple-element.68), channel_id=1, source_target_pairs={{0,8},{8,0},{16,24},{24,16},{32,40},{40,32},{48,56},{56,48},{64,72... | collective-permute-start | bytes 1327112 | tf_op jit(solution)/shard_map/ppermute | solution.py:34
  85.1 1.8 %collective-permute-start.29 = (f16[2,144,128]{2,1,0:T(8,128)(2,1)S(1)}, f16[2,144,128]{2,1,0:T(8,128)(2,1)S(1)}, u32[]{:S(2)}, u32[]{:S(2)}) collective-permute-start(f16[2,144,128]{2,1,0:T(8,128)(2,1)S(1)} %get-tuple-element.85), channel_id=1, source_target_pairs={{0,48},{8,56},{16,0},{24,8},{32,16},{40,24},{48,32},{56,40},{64,11... | collective-permute-start | bytes 221192 | tf_op jit(solution)/shard_map/ppermute | solution.py:34
  86.9 1.5 %collective-permute-start.28 = (f16[2,144,128]{2,1,0:T(8,128)(2,1)S(1)}, f16[2,144,128]{2,1,0:T(8,128)(2,1)S(1)}, u32[]{:S(2)}, u32[]{:S(2)}) collective-permute-start(f16[2,144,128]{2,1,0:T(8,128)(2,1)S(1)} %get-tuple-element.86), channel_id=1, source_target_pairs={{0,32},{8,40},{16,48},{24,56},{32,0},{40,8},{48,16},{56,24},{64,96... | collective-permute-start | bytes 221192 | tf_op jit(solution)/shard_map/ppermute | solution.py:34
  88.5 0.8 collective-permute-start.27
  89.6 2.2 %collective-permute-start.22 = (f16[2,144,128]{2,1,0:T(8,128)(2,1)S(1)}, f16[2,144,128]{2,1,0:T(8,128)(2,1)S(1)}, u32[]{:S(2)}, u32[]{:S(2)}) collective-permute-start(f16[2,144,128]{2,1,0:T(8,128)(2,1)S(1)} %get-tuple-element.88), channel_id=1, source_target_pairs={{0,192},{8,200},{16,208},{24,216},{32,224},{40,232},{48,240},{56,2... | collective-permute-start | bytes 221192 | tf_op jit(solution)/shard_map/ppermute | solution.py:34
  91.9 0.7 collective-permute-start.21
  92.6 0.8 collective-permute-start.20
  93.4 0.8 collective-permute-done.27
  94.2 2.4 %collective-permute-done.21 = f16[2,144,128]{2,1,0:T(8,128)(2,1)S(1)} collective-permute-done((f16[2,144,128]{2,1,0:T(8,128)(2,1)S(1)}, f16[2,144,128]{2,1,0:T(8,128)(2,1)S(1)}, u32[]{:S(2)}, u32[]{:S(2)}) %collective-permute-start.21) | collective-permute-done | bytes 73760 | tf_op jit(solution)/shard_map/ppermute | solution.py:34
  96.6 1.1 %collective-permute-done.20 = f16[2,144,128]{2,1,0:T(8,128)(2,1)S(1)} collective-permute-done((f16[2,144,128]{2,1,0:T(8,128)(2,1)S(1)}, f16[2,144,128]{2,1,0:T(8,128)(2,1)S(1)}, u32[]{:S(2)}, u32[]{:S(2)}) %collective-permute-start.20) | collective-permute-done | bytes 73760 | tf_op jit(solution)/shard_map/ppermute | solution.py:34
  97.8 1.5 %last.1 = (bf16[4,64,128]{2,1,0:T(8,128)(2,1)S(1)}, bf16[4,64,128]{2,1,0:T(8,128)(2,1)S(1)}, f32[27,32,128]{2,1,0:T(8,128)}) custom-call(s32[3]{0:T(128)S(1)} %pad_add_fusion.place, f32[2,144,128]{2,1,0:T(8,128)S(1)} %get-tuple-element.56.refs_0_, f32[2,144,128]{2,1,0:T(8,128)S(1)} %convert_element_type.94.refs_1_, ...), custom_call_target="tpu_custom_call" | custom-call | tf_op jit(solution)/shard_map/last/pallas_call | solution.py:387
  99.3 1.9 %collective-permute-start.31 = (bf16[4,64,128]{2,1,0:T(8,128)(2,1)S(1)}, bf16[4,64,128]{2,1,0:T(8,128)(2,1)S(1)}, u32[]{:S(2)}, u32[]{:S(2)}) collective-permute-start(bf16[4,64,128]{2,1,0:T(8,128)(2,1)S(1)} %get-tuple-element.70), channel_id=1, source_target_pairs={{0,8},{8,0},{16,24},{24,16},{32,40},{40,32},{48,56},{56,48},{64,72... | collective-permute-start | bytes 196616 | tf_op jit(solution)/shard_map/ppermute | solution.py:34
  101.1 1.6 %convert_element_type.111 = bf16[1,32,2048]{2,1,0:T(8,128)(2,1)} convert(f32[1,32,2048]{2,1,0:T(8,128)} %reduce-scatter.2.cloned.1.call-done) | non-fusion elementwise | flops 65536 | bytes 393216 | tf_op jit(solution)/shard_map/convert_element_type | solution.py:326
  102.8 0.7 fusion
  (68 shorter events, 4.4 us)
Async XLA Ops:
  7.2 24.3 %copy-start.1 = (bf16[27,32,128]{2,1,0:T(8,128)(2,1)S(1)}, bf16[27,32,128]{2,1,0:T(8,128)(2,1)}, u32[]{:S(2)}) copy-start(bf16[27,32,128]{2,1,0:T(8,128)(2,1)} %param.4) | copy-start | bytes 663556
  7.2 48.6 %all-gather.2.cloned.1.call-start = ((), (), s32[]{:S(2)}) async-start(), calls=%async_computation.1 | async-start | bytes 1179648 | tf_op jit(solution)/shard_map/all_gather | solution.py:257
  7.9 93.2 %reduce-scatter.2.cloned.1.call-start = ((), (), s32[]{:S(2)}) async-start(), calls=%async_computation.2 | async-start | bytes 2359296 | tf_op jit(solution)/shard_map/reduce_scatter | solution.py:326
  8.9 4.2 %collective-permute-start = (bf16[4,64,128]{2,1,0:T(8,128)(2,1)S(1)}, bf16[4,64,128]{2,1,0:T(8,128)(2,1)S(1)}, u32[]{:S(2)}, u32[]{:S(2)}) collective-permute-start(bf16[4,64,128]{2,1,0:T(8,128)(2,1)S(1)} %get-tuple-element.94), channel_id=1, source_target_pairs={{0,8},{8,0},{16,24},{24,16},{32,40},{40,32},{48,56},{56,48},{64,72... | collective-permute-start | bytes 196616 | tf_op jit(solution)/shard_map/ppermute | solution.py:34
  13.2 5.1 %collective-permute-start.6 = (bf16[2,128,128]{2,1,0:T(8,128)(2,1)S(1)}, bf16[2,128,128]{2,1,0:T(8,128)(2,1)S(1)}, u32[]{:S(2)}, u32[]{:S(2)}) collective-permute-start(bf16[2,128,128]{2,1,0:T(8,128)(2,1)S(1)} %get-tuple-element.44), channel_id=1, source_target_pairs={{0,192},{8,200},{16,208},{24,216},{32,224},{40,232},{48,240},{56,2... | collective-permute-start | bytes 196616 | tf_op jit(solution)/shard_map/ppermute | solution.py:34
  14.2 4.7 %collective-permute-start.5 = (bf16[2,128,128]{2,1,0:T(8,128)(2,1)S(1)}, bf16[2,128,128]{2,1,0:T(8,128)(2,1)S(1)}, u32[]{:S(2)}, u32[]{:S(2)}) collective-permute-start(bf16[2,128,128]{2,1,0:T(8,128)(2,1)S(1)} %get-tuple-element.44), channel_id=1, source_target_pairs={{0,128},{8,136},{16,144},{24,152},{32,160},{40,168},{48,176},{56,1... | collective-permute-start | bytes 196616 | tf_op jit(solution)/shard_map/ppermute | solution.py:34
  14.6 5.8 %collective-permute-start.4 = (bf16[2,128,128]{2,1,0:T(8,128)(2,1)S(1)}, bf16[2,128,128]{2,1,0:T(8,128)(2,1)S(1)}, u32[]{:S(2)}, u32[]{:S(2)}) collective-permute-start(bf16[2,128,128]{2,1,0:T(8,128)(2,1)S(1)} %get-tuple-element.44), channel_id=1, source_target_pairs={{0,64},{8,72},{16,80},{24,88},{32,96},{40,104},{48,112},{56,120},{... | collective-permute-start | bytes 196616 | tf_op jit(solution)/shard_map/ppermute | solution.py:34
  15.3 5.1 %collective-permute-start.3 = (bf16[2,128,128]{2,1,0:T(8,128)(2,1)S(1)}, bf16[2,128,128]{2,1,0:T(8,128)(2,1)S(1)}, u32[]{:S(2)}, u32[]{:S(2)}) collective-permute-start(bf16[2,128,128]{2,1,0:T(8,128)(2,1)S(1)} %get-tuple-element.40), channel_id=1, source_target_pairs={{0,48},{8,56},{16,0},{24,8},{32,16},{40,24},{48,32},{56,40},{64,11... | collective-permute-start | bytes 196616 | tf_op jit(solution)/shard_map/ppermute | solution.py:34
  17.8 4.7 %collective-permute-start.2 = (bf16[2,128,128]{2,1,0:T(8,128)(2,1)S(1)}, bf16[2,128,128]{2,1,0:T(8,128)(2,1)S(1)}, u32[]{:S(2)}, u32[]{:S(2)}) collective-permute-start(bf16[2,128,128]{2,1,0:T(8,128)(2,1)S(1)} %get-tuple-element.40), channel_id=1, source_target_pairs={{0,32},{8,40},{16,48},{24,56},{32,0},{40,8},{48,16},{56,24},{64,96... | collective-permute-start | bytes 196616 | tf_op jit(solution)/shard_map/ppermute | solution.py:34
  18.3 4.8 %collective-permute-start.1 = (bf16[2,128,128]{2,1,0:T(8,128)(2,1)S(1)}, bf16[2,128,128]{2,1,0:T(8,128)(2,1)S(1)}, u32[]{:S(2)}, u32[]{:S(2)}) collective-permute-start(bf16[2,128,128]{2,1,0:T(8,128)(2,1)S(1)} %get-tuple-element.40), channel_id=1, source_target_pairs={{0,16},{8,24},{16,32},{24,40},{32,48},{40,56},{48,0},{56,8},{64,80... | collective-permute-start | bytes 196616 | tf_op jit(solution)/shard_map/ppermute | solution.py:34
  23.1 7.5 %collective-permute-start.9 = (bf16[4,2,128,128]{3,2,1,0:T(8,128)(2,1)S(1)}, bf16[4,2,128,128]{3,2,1,0:T(8,128)(2,1)S(1)}, u32[]{:S(2)}, u32[]{:S(2)}) collective-permute-start(bf16[4,2,128,128]{3,2,1,0:T(8,128)(2,1)S(1)} %get-tuple-element.48.refs_0_), channel_id=1, source_target_pairs={{0,192},{8,200},{16,208},{24,216},{32,224},{40,232},{48,240},{56,2... | collective-permute-start | bytes 786440 | tf_op jit(solution)/shard_map/ppermute | solution.py:34
  25.2 4.6 %collective-permute-start.10 = (bf16[27,32,128]{2,1,0:T(8,128)(2,1)}, bf16[27,32,128]{2,1,0:T(8,128)(2,1)S(1)}, u32[]{:S(2)}, u32[]{:S(2)}) collective-permute-start(bf16[27,32,128]{2,1,0:T(8,128)(2,1)} %param.4), channel_id=1, source_target_pairs={{0,8},{8,0},{16,24},{24,16},{32,40},{40,32},{48,56},{56,48},{64,72... | collective-permute-start | bytes 663560 | tf_op jit(solution)/shard_map/ppermute | solution.py:34
  28.1 9.5 %collective-permute-start.8 = (bf16[4,2,128,128]{3,2,1,0:T(8,128)(2,1)S(1)}, bf16[4,2,128,128]{3,2,1,0:T(8,128)(2,1)S(1)}, u32[]{:S(2)}, u32[]{:S(2)}) collective-permute-start(bf16[4,2,128,128]{3,2,1,0:T(8,128)(2,1)S(1)} %get-tuple-element.48.refs_0_), channel_id=1, source_target_pairs={{0,128},{8,136},{16,144},{24,152},{32,160},{40,168},{48,176},{56,1... | collective-permute-start | bytes 786440 | tf_op jit(solution)/shard_map/ppermute | solution.py:34
  29.5 14.0 %collective-permute-start.7 = (bf16[4,2,128,128]{3,2,1,0:T(8,128)(2,1)S(1)}, bf16[4,2,128,128]{3,2,1,0:T(8,128)(2,1)S(1)}, u32[]{:S(2)}, u32[]{:S(2)}) collective-permute-start(bf16[4,2,128,128]{3,2,1,0:T(8,128)(2,1)S(1)} %get-tuple-element.48.refs_0_), channel_id=1, source_target_pairs={{0,64},{8,72},{16,80},{24,88},{32,96},{40,104},{48,112},{56,120},{... | collective-permute-start | bytes 786440 | tf_op jit(solution)/shard_map/ppermute | solution.py:34
  29.5 20.3 %collective-permute-start.14 = (bf16[4,2,128,128]{3,2,1,0:T(8,128)(2,1)S(1)}, bf16[4,2,128,128]{3,2,1,0:T(8,128)(2,1)S(1)}, u32[]{:S(2)}, u32[]{:S(2)}) collective-permute-start(bf16[4,2,128,128]{3,2,1,0:T(8,128)(2,1)S(1)} %get-tuple-element.50.refs_0_), channel_id=1, source_target_pairs={{0,48},{8,56},{16,0},{24,8},{32,16},{40,24},{48,32},{56,40},{64,11... | collective-permute-start | bytes 786440 | tf_op jit(solution)/shard_map/ppermute | solution.py:34
  29.8 20.0 %collective-permute-start.13 = (bf16[4,2,128,128]{3,2,1,0:T(8,128)(2,1)S(1)}, bf16[4,2,128,128]{3,2,1,0:T(8,128)(2,1)S(1)}, u32[]{:S(2)}, u32[]{:S(2)}) collective-permute-start(bf16[4,2,128,128]{3,2,1,0:T(8,128)(2,1)S(1)} %get-tuple-element.50.refs_0_), channel_id=1, source_target_pairs={{0,32},{8,40},{16,48},{24,56},{32,0},{40,8},{48,16},{56,24},{64,96... | collective-permute-start | bytes 786440 | tf_op jit(solution)/shard_map/ppermute | solution.py:34
  30.7 19.2 %collective-permute-start.12 = (bf16[4,2,128,128]{3,2,1,0:T(8,128)(2,1)S(1)}, bf16[4,2,128,128]{3,2,1,0:T(8,128)(2,1)S(1)}, u32[]{:S(2)}, u32[]{:S(2)}) collective-permute-start(bf16[4,2,128,128]{3,2,1,0:T(8,128)(2,1)S(1)} %get-tuple-element.50.refs_0_), channel_id=1, source_target_pairs={{0,16},{8,24},{16,32},{24,40},{32,48},{40,56},{48,0},{56,8},{64,80... | collective-permute-start | bytes 786440 | tf_op jit(solution)/shard_map/ppermute | solution.py:34
  49.3 7.5 %collective-permute-start.11 = (f32[2,32,2048]{2,1,0:T(8,128)}, f32[2,32,2048]{2,1,0:T(8,128)S(1)}, u32[]{:S(2)}, u32[]{:S(2)}) collective-permute-start(f32[2,32,2048]{2,1,0:T(8,128)} %get-tuple-element.49), channel_id=1, source_target_pairs={{0,8},{8,0},{16,24},{24,16},{32,40},{40,32},{48,56},{56,48},{64,72... | collective-permute-start | bytes 1572872 | tf_op jit(solution)/shard_map/ppermute | solution.py:34
  55.8 2.1 %collective-permute-start.15 = (f32[2,32,2048]{2,1,0:T(8,128)}, f32[2,32,2048]{2,1,0:T(8,128)S(1)}, u32[]{:S(2)}, u32[]{:S(2)}) collective-permute-start(f32[2,32,2048]{2,1,0:T(8,128)} %get-tuple-element.52), channel_id=1, source_target_pairs={{0,8},{8,0},{16,24},{24,16},{32,40},{40,32},{48,56},{56,48},{64,72... | collective-permute-start | bytes 1572872 | tf_op jit(solution)/shard_map/ppermute | solution.py:34
  59.4 1.7 %copy-start = (bf16[8,32,2048]{2,1,0:T(8,128)(2,1)S(1)}, bf16[8,32,2048]{2,1,0:T(8,128)(2,1)}, u32[]{:S(2)}) copy-start(bf16[8,32,2048]{2,1,0:T(8,128)(2,1)} %all-gather.2.cloned.1.call-done.own_ref) | copy-start | bytes 3145732
  59.5 1.6 %collective-permute-start.23 = (bf16[2,32,2048]{2,1,0:T(8,128)(2,1)S(1)}, bf16[2,32,2048]{2,1,0:T(8,128)(2,1)S(1)}, u32[]{:S(2)}, u32[]{:S(2)}) collective-permute-start(bf16[2,32,2048]{2,1,0:T(8,128)(2,1)S(1)} %get-tuple-element.58), channel_id=1, source_target_pairs={{0,8},{8,0},{16,24},{24,16},{32,40},{40,32},{48,56},{56,48},{64,72... | collective-permute-start | bytes 786440 | tf_op jit(solution)/shard_map/ppermute | solution.py:34
  60.0 8.2 %collective-permute-start.16 = (bf16[2,32,2048]{2,1,0:T(8,128)(2,1)S(1)}, bf16[2,32,2048]{2,1,0:T(8,128)(2,1)S(1)}, u32[]{:S(2)}, u32[]{:S(2)}) collective-permute-start(bf16[2,32,2048]{2,1,0:T(8,128)(2,1)S(1)} %get-tuple-element.53), channel_id=1, source_target_pairs={{0,8},{8,0},{16,24},{24,16},{32,40},{40,32},{48,56},{56,48},{64,72... | collective-permute-start | bytes 786440 | tf_op jit(solution)/shard_map/ppermute | solution.py:34
  65.9 8.4 %collective-permute-start.26 = (f16[2,528,128]{2,1,0:T(8,128)(2,1)S(1)}, f16[2,528,128]{2,1,0:T(8,128)(2,1)S(1)}, u32[]{:S(2)}, u32[]{:S(2)}) collective-permute-start(f16[2,528,128]{2,1,0:T(8,128)(2,1)S(1)} %get-tuple-element.79), channel_id=1, source_target_pairs={{0,192},{8,200},{16,208},{24,216},{32,224},{40,232},{48,240},{56,2... | collective-permute-start | bytes 811016 | tf_op jit(solution)/shard_map/ppermute | solution.py:34
  66.3 16.5 %collective-permute-start.25 = (f16[2,528,128]{2,1,0:T(8,128)(2,1)S(1)}, f16[2,528,128]{2,1,0:T(8,128)(2,1)S(1)}, u32[]{:S(2)}, u32[]{:S(2)}) collective-permute-start(f16[2,528,128]{2,1,0:T(8,128)(2,1)S(1)} %get-tuple-element.80), channel_id=1, source_target_pairs={{0,128},{8,136},{16,144},{24,152},{32,160},{40,168},{48,176},{56,1... | collective-permute-start | bytes 811016 | tf_op jit(solution)/shard_map/ppermute | solution.py:34
  67.7 17.1 %collective-permute-start.24 = (f16[2,528,128]{2,1,0:T(8,128)(2,1)S(1)}, f16[2,528,128]{2,1,0:T(8,128)(2,1)S(1)}, u32[]{:S(2)}, u32[]{:S(2)}) collective-permute-start(f16[2,528,128]{2,1,0:T(8,128)(2,1)S(1)} %get-tuple-element.81), channel_id=1, source_target_pairs={{0,64},{8,72},{16,80},{24,88},{32,96},{40,104},{48,112},{56,120},{... | collective-permute-start | bytes 811016 | tf_op jit(solution)/shard_map/ppermute | solution.py:34
  73.0 13.9 %collective-permute-start.19 = (f16[2,528,128]{2,1,0:T(8,128)(2,1)S(1)}, f16[2,528,128]{2,1,0:T(8,128)(2,1)S(1)}, u32[]{:S(2)}, u32[]{:S(2)}) collective-permute-start(f16[2,528,128]{2,1,0:T(8,128)(2,1)S(1)} %get-tuple-element.82), channel_id=1, source_target_pairs={{0,48},{8,56},{16,0},{24,8},{32,16},{40,24},{48,32},{56,40},{64,11... | collective-permute-start | bytes 811016 | tf_op jit(solution)/shard_map/ppermute | solution.py:34
  73.4 15.1 %collective-permute-start.18 = (f16[2,528,128]{2,1,0:T(8,128)(2,1)S(1)}, f16[2,528,128]{2,1,0:T(8,128)(2,1)S(1)}, u32[]{:S(2)}, u32[]{:S(2)}) collective-permute-start(f16[2,528,128]{2,1,0:T(8,128)(2,1)S(1)} %get-tuple-element.83), channel_id=1, source_target_pairs={{0,32},{8,40},{16,48},{24,56},{32,0},{40,8},{48,16},{56,24},{64,96... | collective-permute-start | bytes 811016 | tf_op jit(solution)/shard_map/ppermute | solution.py:34
  74.2 15.1 %collective-permute-start.17 = (f16[2,528,128]{2,1,0:T(8,128)(2,1)S(1)}, f16[2,528,128]{2,1,0:T(8,128)(2,1)S(1)}, u32[]{:S(2)}, u32[]{:S(2)}) collective-permute-start(f16[2,528,128]{2,1,0:T(8,128)(2,1)S(1)} %get-tuple-element.84), channel_id=1, source_target_pairs={{0,16},{8,24},{16,32},{24,40},{32,48},{40,56},{48,0},{56,8},{64,80... | collective-permute-start | bytes 811016 | tf_op jit(solution)/shard_map/ppermute | solution.py:34
  82.8 15.0 %collective-permute-start.30 = (f32[27,32,128]{2,1,0:T(8,128)S(1)}, f32[27,32,128]{2,1,0:T(8,128)S(1)}, u32[]{:S(2)}, u32[]{:S(2)}) collective-permute-start(f32[27,32,128]{2,1,0:T(8,128)S(1)} %get-tuple-element.68), channel_id=1, source_target_pairs={{0,8},{8,0},{16,24},{24,16},{32,40},{40,32},{48,56},{56,48},{64,72... | collective-permute-start | bytes 1327112 | tf_op jit(solution)/shard_map/ppermute | solution.py:34
  85.1 6.8 %collective-permute-start.29 = (f16[2,144,128]{2,1,0:T(8,128)(2,1)S(1)}, f16[2,144,128]{2,1,0:T(8,128)(2,1)S(1)}, u32[]{:S(2)}, u32[]{:S(2)}) collective-permute-start(f16[2,144,128]{2,1,0:T(8,128)(2,1)S(1)} %get-tuple-element.85), channel_id=1, source_target_pairs={{0,48},{8,56},{16,0},{24,8},{32,16},{40,24},{48,32},{56,40},{64,11... | collective-permute-start | bytes 221192 | tf_op jit(solution)/shard_map/ppermute | solution.py:34
  86.9 5.7 %collective-permute-start.28 = (f16[2,144,128]{2,1,0:T(8,128)(2,1)S(1)}, f16[2,144,128]{2,1,0:T(8,128)(2,1)S(1)}, u32[]{:S(2)}, u32[]{:S(2)}) collective-permute-start(f16[2,144,128]{2,1,0:T(8,128)(2,1)S(1)} %get-tuple-element.86), channel_id=1, source_target_pairs={{0,32},{8,40},{16,48},{24,56},{32,0},{40,8},{48,16},{56,24},{64,96... | collective-permute-start | bytes 221192 | tf_op jit(solution)/shard_map/ppermute | solution.py:34
  88.5 5.7 %collective-permute-start.27 = (f16[2,144,128]{2,1,0:T(8,128)(2,1)S(1)}, f16[2,144,128]{2,1,0:T(8,128)(2,1)S(1)}, u32[]{:S(2)}, u32[]{:S(2)}) collective-permute-start(f16[2,144,128]{2,1,0:T(8,128)(2,1)S(1)} %get-tuple-element.87), channel_id=1, source_target_pairs={{0,16},{8,24},{16,32},{24,40},{32,48},{40,56},{48,0},{56,8},{64,80... | collective-permute-start | bytes 221192 | tf_op jit(solution)/shard_map/ppermute | solution.py:34
  89.6 4.6 %collective-permute-start.22 = (f16[2,144,128]{2,1,0:T(8,128)(2,1)S(1)}, f16[2,144,128]{2,1,0:T(8,128)(2,1)S(1)}, u32[]{:S(2)}, u32[]{:S(2)}) collective-permute-start(f16[2,144,128]{2,1,0:T(8,128)(2,1)S(1)} %get-tuple-element.88), channel_id=1, source_target_pairs={{0,192},{8,200},{16,208},{24,216},{32,224},{40,232},{48,240},{56,2... | collective-permute-start | bytes 221192 | tf_op jit(solution)/shard_map/ppermute | solution.py:34
  91.9 4.7 %collective-permute-start.21 = (f16[2,144,128]{2,1,0:T(8,128)(2,1)S(1)}, f16[2,144,128]{2,1,0:T(8,128)(2,1)S(1)}, u32[]{:S(2)}, u32[]{:S(2)}) collective-permute-start(f16[2,144,128]{2,1,0:T(8,128)(2,1)S(1)} %get-tuple-element.89), channel_id=1, source_target_pairs={{0,128},{8,136},{16,144},{24,152},{32,160},{40,168},{48,176},{56,1... | collective-permute-start | bytes 221192 | tf_op jit(solution)/shard_map/ppermute | solution.py:34
  92.6 5.2 %collective-permute-start.20 = (f16[2,144,128]{2,1,0:T(8,128)(2,1)S(1)}, f16[2,144,128]{2,1,0:T(8,128)(2,1)S(1)}, u32[]{:S(2)}, u32[]{:S(2)}) collective-permute-start(f16[2,144,128]{2,1,0:T(8,128)(2,1)S(1)} %get-tuple-element.90), channel_id=1, source_target_pairs={{0,64},{8,72},{16,80},{24,88},{32,96},{40,104},{48,112},{56,120},{... | collective-permute-start | bytes 221192 | tf_op jit(solution)/shard_map/ppermute | solution.py:34
  99.3 3.5 %collective-permute-start.31 = (bf16[4,64,128]{2,1,0:T(8,128)(2,1)S(1)}, bf16[4,64,128]{2,1,0:T(8,128)(2,1)S(1)}, u32[]{:S(2)}, u32[]{:S(2)}) collective-permute-start(bf16[4,64,128]{2,1,0:T(8,128)(2,1)S(1)} %get-tuple-element.70), channel_id=1, source_target_pairs={{0,8},{8,0},{16,24},{24,16},{32,40},{40,32},{48,56},{56,48},{64,72... | collective-permute-start | bytes 196616 | tf_op jit(solution)/shard_map/ppermute | solution.py:34
Sparse Core Ops, SparseCore 0:
  9.8 38.1 all-gather.1
  59.6 37.2 reduce-scatter.1
